TPU v7x, 32 devices: a whole 2x2x4 slice. The times are simulated.
32 devices in a mesh: groups: 2 (over y), seq: 8 (over z, core), head: 2 (over x).
Axes of the slice: x: 2, y: 2, z: 4, core: 2. Of those that a mesh axis runs over, the one named last changes fastest.
Arguments:
- query_rows: bfloat16 [4096, 1024], P(('groups', 'seq'), 'head'), parts along dimension 0, may hold values from -8 to 8
- key_rows: bfloat16 [4096, 1024], P(('groups', 'seq'), 'head'), parts along dimension 0, may hold values from -8 to 8
- value_rows: bfloat16 [4096, 1024], P(('groups', 'seq'), 'head'), parts along dimension 0, may hold values from -6 to 6
- grad_output: bfloat16 [4096, 1024], P(('groups', 'seq'), 'head'), parts along dimension 0, may hold values from -6 to 6
- dilation_offsets: int32 [1, 8], P(None, 'head'), may hold values from 0 to 0, as said below
Outputs:
- attended: bfloat16 [4096, 1024], P(('groups', 'seq'), 'head'), parts along dimension 0
- query_grad: bfloat16 [4096, 1024], P(('groups', 'seq'), 'head'), parts along dimension 0
- key_grad: bfloat16 [4096, 1024], P(('groups', 'seq'), 'head'), parts along dimension 0
- value_grad: bfloat16 [4096, 1024], P(('groups', 'seq'), 'head'), parts along dimension 0
There are 2 independent parts, one for each index of `groups`. A program takes and returns all parts, laid end to end along the dimension named above; an argument that names none is the same for every part. Nothing has to cross between parts.
Inputs may be any that keep to these rules, and one draw needn't show every extreme that they name: `dilation_offsets`: row l (counting from 0) holds for each head a number from 0 to 2^l - 1.
All inputs are finite; a program needn't handle non-finite values.
Results may differ from a plain program's by a relative error of at most 0.01.
Values may be sent and summed in bfloat16 or wider, within the bound.
No kernel may reach another device: no remote copies, remote signals or barrier semaphores. Data moves between devices by JAX's collectives and lax.ppermute only.
A program may use at most 128 MiB of HBM per device.

v0:
```python
import jax
import jax.numpy as jnp
from jax import lax
from jax.sharding import PartitionSpec as P

HD = 128
SEG = 2048


def shortened(array):

    def short(part):
        return part.astype(jnp.bfloat16) if part.dtype == jnp.float32 else part

    return jax.tree.map(short, array)


def from_partner(array, axis, stride):
    return lax.ppermute(array, axis, [(i, i ^ 1 << stride) for i in range(lax.axis_size(axis))])


def pick_rows(values, row_mask):
    stride = row_mask.shape[0]
    shaped = values.reshape((values.shape[0] // stride, stride) + values.shape[1:])
    mask_wide = row_mask.reshape(row_mask.shape + (1,) * (values.ndim - 2))
    return jnp.sum(jnp.where(mask_wide, shaped, jnp.zeros((), values.dtype)), axis=1)


def place_rows(values, row_mask):
    stride = row_mask.shape[0]
    mask_wide = row_mask.reshape(row_mask.shape + (1,) * (values.ndim - 2))
    spread = jnp.where(mask_wide, values[:, None], jnp.zeros((), values.dtype))
    return spread.reshape((values.shape[0] * stride,) + values.shape[1:])


def upper_of(seq_index, bit_number):
    return seq_index // 2**bit_number % 2 == 1


def widen_apart(buffers, bit_totals, seq_index):
    widened = []
    for buffer, bit_total in zip(buffers, bit_totals):
        for bit_number in range(bit_total):
            partner = jax.tree.map(
                lambda part, own: part.astype(own.dtype),
                from_partner(shortened(buffer), "seq", bit_number),
                buffer,
            )
            upper_side = upper_of(seq_index, bit_number)
            buffer = jnp.where(
                upper_side,
                jnp.concatenate([partner, buffer], 0),
                jnp.concatenate([buffer, partner], 0),
            )
        widened.append(buffer)
    return widened


def narrow_apart(buffers, bit_totals, seq_index):
    narrowed = []
    for buffer, bit_total in zip(buffers, bit_totals):
        for bit_number in reversed(range(bit_total)):
            half_rows = buffer.shape[0] // 2
            lower_half = buffer[:half_rows]
            upper_half = buffer[half_rows:]
            upper_side = upper_of(seq_index, bit_number)
            outgoing = jnp.where(upper_side, lower_half, upper_half)
            kept_half = jnp.where(upper_side, upper_half, lower_half)
            buffer = kept_half + from_partner(outgoing, "seq", bit_number)
        narrowed.append(buffer)
    return narrowed


def split_keys(gathered, head_count):
    width = head_count * HD
    key_all = gathered[:, :width].reshape(-1, head_count, HD)
    value_all = gathered[:, width : 2 * width].reshape(-1, head_count, HD)
    return (key_all, value_all)


def forward_level(query_part, gathered, head_count):
    score_scale = HD ** (-0.5)
    key_all, value_all = split_keys(gathered, head_count)
    scores = (
        jnp.einsum("nhd,khd->hnk", query_part, key_all, preferred_element_type=jnp.float32)
        * score_scale
    )
    row_peak = jnp.max(scores, axis=2, keepdims=True)
    row_sums = jnp.sum(jnp.exp(scores - row_peak), axis=2, keepdims=True)
    level_lse = row_peak + jnp.log(row_sums)
    level_probs = jnp.exp(scores - level_lse).astype(jnp.bfloat16)
    partial_value = jnp.einsum(
        "hnk,khd->nhd", level_probs, value_all, preferred_element_type=jnp.float32
    )
    return (partial_value, jnp.transpose(level_lse[:, :, 0]))


def backward_level(query_part, grad_part, total_part, delta_part, gathered, head_count):
    score_scale = HD ** (-0.5)
    key_all, value_all = split_keys(gathered, head_count)
    scores = (
        jnp.einsum("nhd,khd->hnk", query_part, key_all, preferred_element_type=jnp.float32)
        * score_scale
    )
    glob = jnp.exp(scores - jnp.transpose(total_part)[:, :, None])
    glob_low = glob.astype(jnp.bfloat16)
    value_part = jnp.einsum("hnk,nhd->khd", glob_low, grad_part, preferred_element_type=jnp.float32)
    dprob = jnp.einsum("nhd,khd->hnk", grad_part, value_all, preferred_element_type=jnp.float32)
    dscore = (glob * (dprob - jnp.transpose(delta_part)[:, :, None])).astype(jnp.bfloat16)
    query_part_grad = (
        jnp.einsum("hnk,khd->nhd", dscore, key_all, preferred_element_type=jnp.float32)
        * score_scale
    )
    key_part = (
        jnp.einsum("hnk,nhd->khd", dscore, query_part, preferred_element_type=jnp.float32)
        * score_scale
    )
    key_count = key_part.shape[0]
    grad_term = jnp.concatenate(
        [key_part.reshape(key_count, -1), value_part.reshape(key_count, -1)], axis=1
    )
    return (query_part_grad, grad_term)


def shards(query_rows, key_rows, value_rows, grad_output, dilation_offsets):
    row_count = query_rows.shape[0]
    head_count = query_rows.shape[1] // HD
    level_count = dilation_offsets.shape[0]
    seq_index = lax.axis_index("seq")
    seq_width = lax.axis_size("seq")
    query_three = query_rows.reshape(row_count, head_count, HD)
    key_three = key_rows.reshape(row_count, head_count, HD)
    value_three = value_rows.reshape(row_count, head_count, HD)
    grad_three = grad_output.reshape(row_count, head_count, HD)
    level_masks = []
    full_masks = []
    query_parts = []
    kept_pieces = []
    segment_bits = []
    for level_no in range(level_count):
        stride = 2**level_no
        row_mask = (
            lax.broadcasted_iota(jnp.int32, (stride, head_count), 0)
            == dilation_offsets[level_no][None, :]
        )
        full_mask = (
            lax.broadcasted_iota(jnp.int32, (row_count, head_count), 0) % stride
            == dilation_offsets[level_no][None, :]
        )
        level_masks.append(row_mask)
        full_masks.append(full_mask)
        query_parts.append(pick_rows(query_three, row_mask))
        key_three_part = pick_rows(key_three, row_mask)
        value_three_part = pick_rows(value_three, row_mask)
        piece = jnp.concatenate(
            [
                key_three_part.reshape(row_count // stride, -1),
                value_three_part.reshape(row_count // stride, -1),
            ],
            axis=1,
        )
        kept_pieces.append(piece)
        segment_bits.append(
            min((SEG * stride // row_count).bit_length() - 1, seq_width.bit_length() - 1)
        )
    paired = list(range(level_count - 1))
    paired_bits = [segment_bits[member] for member in paired]
    widened = widen_apart([kept_pieces[member] for member in paired], paired_bits, seq_index)
    gathered = list(kept_pieces)
    for member, buffer in zip(paired, widened):
        gathered[member] = buffer
    gathered[level_count - 1] = lax.all_gather(
        kept_pieces[level_count - 1], "seq", axis=0, tiled=True
    )
    out_parts = []
    lse_full = []
    for level_no in range(level_count):
        partial_value, level_lse = forward_level(
            query_parts[level_no], gathered[level_no], head_count
        )
        out_parts.append(place_rows(partial_value, level_masks[level_no]))
        lse_full.append(place_rows(level_lse, level_masks[level_no]))
    row_peak = lse_full[0]
    for level_no in range(1, level_count):
        row_peak = jnp.maximum(
            row_peak, jnp.where(full_masks[level_no], lse_full[level_no], lse_full[0])
        )
    exp_total = jnp.zeros((row_count, head_count), jnp.float32)
    for level_no in range(level_count):
        exp_total = exp_total + jnp.where(
            full_masks[level_no], jnp.exp(lse_full[level_no] - row_peak), jnp.float32(0.0)
        )
    total_lse = row_peak + jnp.log(exp_total)
    combined = jnp.zeros((row_count, head_count, HD), jnp.float32)
    for level_no in range(level_count):
        weight = jnp.exp(lse_full[level_no] - total_lse)
        combined = combined + jnp.where(
            full_masks[level_no][:, :, None],
            weight[:, :, None] * out_parts[level_no],
            jnp.float32(0.0),
        )
    attended = combined.astype(jnp.bfloat16)
    delta = jnp.sum(attended.astype(jnp.float32) * grad_three.astype(jnp.float32), axis=2)
    query_acc = jnp.zeros((row_count, head_count, HD), jnp.float32)
    grad_terms = []
    for level_no in range(level_count):
        row_mask = level_masks[level_no]
        grad_part = pick_rows(grad_three, row_mask)
        total_part = pick_rows(total_lse, row_mask)
        delta_part = pick_rows(delta, row_mask)
        query_part_grad, grad_term = backward_level(
            query_parts[level_no], grad_part, total_part, delta_part, gathered[level_no], head_count
        )
        query_acc = query_acc + place_rows(query_part_grad, row_mask)
        grad_terms.append(grad_term)
    narrowed = narrow_apart([grad_terms[member] for member in paired], paired_bits, seq_index)
    owned = list(grad_terms)
    for member, buffer in zip(paired, narrowed):
        owned[member] = buffer
    top_term = grad_terms[level_count - 1]
    owned[level_count - 1] = lax.psum_scatter(top_term, "seq", scatter_dimension=0, tiled=True)
    key_acc = jnp.zeros((row_count, head_count, HD), jnp.float32)
    value_acc = jnp.zeros((row_count, head_count, HD), jnp.float32)
    for level_no in range(level_count):
        own_rows = owned[level_no]
        key_own = own_rows[:, : head_count * HD].reshape(-1, head_count, HD)
        value_own = own_rows[:, head_count * HD :].reshape(-1, head_count, HD)
        key_acc = key_acc + place_rows(key_own, level_masks[level_no])
        value_acc = value_acc + place_rows(value_own, level_masks[level_no])
    flat = (row_count, head_count * HD)
    return (
        attended.reshape(flat),
        query_acc.astype(jnp.bfloat16).reshape(flat),
        key_acc.astype(jnp.bfloat16).reshape(flat),
        value_acc.astype(jnp.bfloat16).reshape(flat),
    )


def solution(mesh):
    in_specs = (
        P(("groups", "seq"), "head"),
        P(("groups", "seq"), "head"),
        P(("groups", "seq"), "head"),
        P(("groups", "seq"), "head"),
        P(None, "head"),
    )
    out_specs = (
        P(("groups", "seq"), "head"),
        P(("groups", "seq"), "head"),
        P(("groups", "seq"), "head"),
        P(("groups", "seq"), "head"),
    )
    return jax.shard_map(shards, mesh=mesh, in_specs=in_specs, out_specs=out_specs, check_vma=False)
```

profile of v0, /device:TPU:0, one launch (start us, length us, event | category | flops | bytes accessed | tf_op | source)
XLA Modules:
  0.0 179.3 jit_solution(6711979293234945704)
XLA Ops:
  7.2 0.7 compare_bitcast_fusion.1
  7.9 1.1 copy.21
  9.0 1.1 copy.22
  10.1 0.1 broadcast_select_fusion.1
  10.3 0.8 pad_maximum_fusion.1
  11.2 1.1 copy.25
  12.3 1.1 copy.20
  13.4 48.4 %all-gather.2.cloned.1.call-done = bf16[2048,1024]{0,1:T(8,128)(2,1)} async-done(((bf16[256,1024]{0,1:T(8,128)(2,1)}), bf16[2048,1024]{0,1:T(8,128)(2,1)}) %all-gather.2.cloned.1.call-update) | async-done | bytes 4194320 | tf_op jit(solution)/shard_map/all_gather | solution.py:172
  61.8 2.6 %fusion.27 = (bf16[2048,512]{0,1:T(8,128)(2,1)S(1)}, bf16[2048,512]{0,1:T(8,128)(2,1)S(1)}) fusion(bf16[2048,1024]{0,1:T(8,128)(2,1)} %all-gather.2.cloned.1.call-done), kind=kLoop, calls=%fused_computation.53 | loop fusion | bytes 8388608 | tf_op jit(solution)/shard_map/slice | solution.py:76
  64.4 1.5 multiply_reduce_fusion
  65.9 1.6 exponential_reduce_fusion
  67.7 1.9 %multiply_reduce_fusion.1 = (f32[256,4]{0,1:T(4,128)S(1)}, bf16[256,4,128]{0,2,1:T(8,128)(2,1)S(1)}) fusion(pred[4]{0:T(512)(128)(4,1)S(1)} %get-tuple-element.18, bf16[256,512]{0,1:T(8,128)(2,1)S(1)} %copy.25, bf16[2048,4,128]{0,2,1:T(8,128)(2,1)S(1)} %bitcast.53, f32[4,256,2048]{2,1,0:T(8,128)S(1)} %get-tuple-element.23, ...), kind=kOutput, calls=%fused_computation.27 | convolution fusion | flops 544209920 | bytes 11022344 | tf_op jit(solution)/shard_map/hnk,khd->nhd/dot_general | solution.py:92
  69.7 2.0 %fusion.1 = f32[4,128,2048]{2,1,0:T(8,128)S(1)} fusion(f32[4,256,2048]{2,1,0:T(8,128)S(1)} %get-tuple-element.23, f32[4,256]{1,0:T(4,128)S(1)} %get-tuple-element.12, bf16[256,4,128]{0,2,1:T(8,128)(2,1)S(1)} %bitcast.57, pred[4]{0:T(512)(128)(4,1)S(1)} %get-tuple-element.19), kind=kOutput, calls=%fused_computation.7 | convolution fusion | flops 543293440 | bytes 12849156 | tf_op jit(solution)/shard_map/hnk,nhd->khd/dot_general | solution.py:107
  71.8 2.9 %multiply_convert_fusion = bf16[4,256,2048]{2,1,0:T(8,128)(2,1)S(1)} fusion(f32[4,256,2048]{2,1,0:T(8,128)S(1)} %get-tuple-element.23, bf16[2048,4,128]{0,2,1:T(8,128)(2,1)S(1)} %bitcast.54, f32[4,256]{1,0:T(4,128)S(1)} %select_bitcast_fusion, f32[4,256]{1,0:T(4,128)S(1)} %get-tuple-element.12, bf16[256,4,128]{0,2,1:T(8,128)(2,1)S(1)} %bitcast.58, ...), kind=kOutput, calls=%fused_computation.1 | convolution fusion | flops 547487744 | bytes 14950404 | tf_op jit(solution)/shard_map/nhd,khd->hnk/dot_general | solution.py:108
  74.7 1.9 %copy-done = bf16[4,256,2048]{2,1,0:T(8,128)(2,1)} copy-done((bf16[4,256,2048]{2,1,0:T(8,128)(2,1)}, bf16[4,256,2048]{2,1,0:T(8,128)(2,1)S(1)}, u32[]{:S(2)}) %copy-start) | copy-done | bytes 4194328
  76.7 0.9 convolution_multiply_fusion
  77.6 3.8 %pad_maximum_fusion = f32[2048,1024]{0,1:T(8,128)} fusion(f32[2048,512]{0,1:T(8,128)S(1)} %bitcast.52, f32[2048,512]{0,1:T(8,128)S(1)} %bitcast.49), kind=kLoop, calls=%fused_computation | loop fusion | flops 2097152 | bytes 16777216 | tf_op jit(solution)/shard_map/concatenate | solution.py:119
  81.6 0.8 copy.28
  82.4 3.7 %fusion.9 = bf16[4,128,256]{2,1,0:T(8,128)(2,1)S(1)} fusion(bf16[2048,4,128]{0,2,1:T(8,128)(2,1)S(1)} %bitcast.51, bf16[4,256,2048]{2,1,0:T(8,128)(2,1)} %copy-done, pred[4]{0:T(512)(128)(4,1)S(1)} %get-tuple-element.19), kind=kOutput, calls=%fused_computation.16 | convolution fusion | flops 537264128 | bytes 6553604 | tf_op jit(solution)/shard_map/hnk,khd->nhd/dot_general | solution.py:111
  86.2 0.8 copy.29
  87.0 82.4 %reduce-scatter.2.cloned.1.call-done = f32[256,1024]{0,1:T(8,128)} async-done(((f32[2048,1024]{0,1:T(8,128)}), f32[256,1024]{0,1:T(8,128)}) %reduce-scatter.2.cloned.1.call-update) | async-done | bytes 1048592 | tf_op jit(solution)/shard_map/reduce_scatter | solution.py:221
  169.4 1.3 fusion.13
  170.8 0.8 copy.30
  171.6 0.8 copy.31
  (10 shorter events, 0.6 us)
Async XLA Ops:
  7.2 54.6 %all-gather.2.cloned.1.call-start = ((), (), s32[]{:S(2)}) async-start(), calls=%async_computation.1 | async-start | bytes 4718592 | tf_op jit(solution)/shard_map/all_gather | solution.py:172
  11.1 158.3 %reduce-scatter.2.cloned.1.call-start = ((), (), s32[]{:S(2)}) async-start(), calls=%async_computation.2 | async-start | bytes 9437184 | tf_op jit(solution)/shard_map/reduce_scatter | solution.py:221
  74.7 1.9 %copy-start = (bf16[4,256,2048]{2,1,0:T(8,128)(2,1)}, bf16[4,256,2048]{2,1,0:T(8,128)(2,1)S(1)}, u32[]{:S(2)}) copy-start(bf16[4,256,2048]{2,1,0:T(8,128)(2,1)S(1)} %multiply_convert_fusion) | copy-start | bytes 12582916
Sparse Core Ops, SparseCore 0:
  11.3 50.4 all-gather.1
  81.6 87.8 reduce-scatter.1
where the time goes:
time: 180 us; the launch traced here: 179 us
  waiting for transfers between devices  131 us (73%)
  between operations  14.2 us (8%)
  matrix products  13 us (7%)
  local copies, waits for them, and re-layouts  12.4 us (7%)
  other arithmetic  8.79 us (5%)
    reduce_scatter x1, waiting for transfers between devices, shards(): lax.psum_scatter(top_term, 'seq', scatter_dimension=0, tiled=True)  82.4 us
    all_gather x1, waiting for transfers between devices, shards(): lax.all_gather(kept_pieces[level_count - 1], 'seq', axis=0, tiled=True)  48.4 us
    unnamed x10, local copies, waits for them, and re-layouts  9.65 us
    concatenate x1, other arithmetic, backward_level(): jnp.concatenate([key_part.reshape(key_count, -1), value_part.reshape(key_...  3.8 us
    dot_general x1, matrix products, backward_level(): jnp.einsum('hnk,khd->nhd', dscore, key_all, preferred_element_type=jnp.fl...  3.72 us
  transfers between devices with their start and end apart: 2, of which 2 were waited for; matrix products, arithmetic and copies ran while one was open for 4% of the time, Pallas kernels for 0%

commit v1 on v0

--- a/solution.py
+++ b/solution.py
@@ -1,6 +1,10 @@
+import functools
+
 import jax
 import jax.numpy as jnp
 from jax import lax
+from jax.experimental import pallas as pl
+from jax.experimental.pallas import tpu as pltpu
 from jax.sharding import PartitionSpec as P
 
 HD = 128
@@ -122,7 +126,7 @@
     return (query_part_grad, grad_term)
 
 
-def shards(query_rows, key_rows, value_rows, grad_output, dilation_offsets):
+def shards_levels(query_rows, key_rows, value_rows, grad_output, dilation_offsets):
     row_count = query_rows.shape[0]
     head_count = query_rows.shape[1] // HD
     level_count = dilation_offsets.shape[0]
@@ -236,6 +240,208 @@
     )
 
 
+VMEM_BYTES = 56 * 2**20
+NT = (((1,), (1,)), ((), ()))
+TN = (((0,), (0,)), ((), ()))
+
+
+def vmem_specs(count):
+    return [pl.BlockSpec(memory_space=pltpu.VMEM)] * count
+
+
+def head_columns(chip, offset):
+    return pl.ds(pl.multiple_of((chip ^ offset) * HD, HD), HD)
+
+
+def pack_kernel(chips, chip_ref, *refs):
+    first, second = refs[:2]
+    chip = chip_ref[0]
+    for offset in range(chips):
+        columns = head_columns(chip, offset)
+        refs[2 + offset][0] = first[:, columns]
+        refs[2 + offset][1] = second[:, columns]
+
+
+def pack(chip, first, second, chips):
+    rows = first.shape[0]
+    block = jax.ShapeDtypeStruct((2, rows, HD), first.dtype)
+    return pl.pallas_call(
+        functools.partial(pack_kernel, chips),
+        out_shape=[block] * chips,
+        in_specs=[pl.BlockSpec(memory_space=pltpu.SMEM)] + vmem_specs(2),
+        out_specs=vmem_specs(chips),
+        compiler_params=pltpu.CompilerParams(vmem_limit_bytes=VMEM_BYTES),
+        cost_estimate=pl.CostEstimate(flops=0, bytes_accessed=4 * first.size * 2, transcendentals=0),
+        name="pack",
+    )(chip, first, second)
+
+
+def unpack_kernel(chips, chip_ref, *refs):
+    chip = chip_ref[0]
+    first, second = refs[chips : chips + 2]
+    for offset in range(chips):
+        columns = head_columns(chip, offset)
+        first[:, columns] = refs[offset][0]
+        second[:, columns] = refs[offset][1]
+
+
+def unpack(chip, blocks):
+    chips = len(blocks)
+    rows = blocks[0].shape[1]
+    whole = jax.ShapeDtypeStruct((rows, chips * HD), blocks[0].dtype)
+    return pl.pallas_call(
+        functools.partial(unpack_kernel, chips),
+        out_shape=[whole] * 2,
+        in_specs=[pl.BlockSpec(memory_space=pltpu.SMEM)] + vmem_specs(chips),
+        out_specs=vmem_specs(2),
+        compiler_params=pltpu.CompilerParams(vmem_limit_bytes=VMEM_BYTES),
+        name="unpack",
+    )(chip, *blocks)
+
+
+def attention_kernel(chips, *refs):
+    pairs = refs[: 2 * chips]
+    query_grads = refs[2 * chips : 3 * chips]
+    outs = refs[3 * chips : 4 * chips]
+    own_ref, other_ref = refs[4 * chips : 4 * chips + 2]
+    key_ref, value_ref, dkey_ref, dvalue_ref = refs[4 * chips + 2 :]
+    rows = pairs[0].shape[1]
+    for index, pair in enumerate(pairs):
+        key_ref[index * rows : (index + 1) * rows] = pair[0]
+        value_ref[index * rows : (index + 1) * rows] = pair[1]
+    score_scale = HD ** (-0.5)
+    exp_scale = score_scale * 1.4426950408889634
+    key_all = key_ref[...]
+    value_all = value_ref[...]
+    for index in range(chips):
+        query = query_grads[index][0]
+        grad = query_grads[index][1]
+        scores = lax.dot_general(query, key_all, NT, preferred_element_type=jnp.float32)
+        row_peak = jnp.max(scores, axis=1, keepdims=True)
+        probs = jnp.exp2(scores * exp_scale - row_peak * exp_scale)
+        probs = probs * (1.0 / jnp.sum(probs, axis=1, keepdims=True))
+        probs_low = probs.astype(jnp.bfloat16)
+        attended = jnp.dot(probs_low, value_all, preferred_element_type=jnp.float32)
+        attended = attended.astype(jnp.bfloat16)
+        delta = jnp.sum(
+            attended.astype(jnp.float32) * grad.astype(jnp.float32), axis=1, keepdims=True
+        )
+        dprobs = lax.dot_general(grad, value_all, NT, preferred_element_type=jnp.float32)
+        dscore = (probs * (dprobs - delta)).astype(jnp.bfloat16)
+        query_grad = jnp.dot(dscore, key_all, preferred_element_type=jnp.float32) * score_scale
+        outs[index][0] = attended
+        outs[index][1] = query_grad.astype(jnp.bfloat16)
+        dkey = lax.dot_general(dscore, query, TN, preferred_element_type=jnp.float32)
+        dvalue = lax.dot_general(probs_low, grad, TN, preferred_element_type=jnp.float32)
+        if index == 0:
+            dkey_ref[...] = dkey
+            dvalue_ref[...] = dvalue
+        else:
+            dkey_ref[...] += dkey
+            dvalue_ref[...] += dvalue
+    half = chips * rows
+    own_ref[0] = dkey_ref[:half] * score_scale
+    own_ref[1] = dvalue_ref[:half]
+    other_ref[0] = (dkey_ref[half:] * score_scale).astype(other_ref.dtype)
+    other_ref[1] = dvalue_ref[half:].astype(other_ref.dtype)
+
+
+def attention(pairs, query_grads):
+    chips = len(query_grads)
+    rows = pairs[0].shape[1]
+    keys = 2 * chips * rows
+    block = jax.ShapeDtypeStruct((2, rows, HD), jnp.bfloat16)
+    products = chips * rows * keys * HD
+    return pl.pallas_call(
+        functools.partial(attention_kernel, chips),
+        out_shape=[block] * chips
+        + [
+            jax.ShapeDtypeStruct((2, chips * rows, HD), jnp.float32),
+            jax.ShapeDtypeStruct((2, chips * rows, HD), jnp.bfloat16),
+        ],
+        in_specs=vmem_specs(3 * chips),
+        out_specs=vmem_specs(chips + 2),
+        scratch_shapes=[
+            pltpu.VMEM((keys, HD), jnp.bfloat16),
+            pltpu.VMEM((keys, HD), jnp.bfloat16),
+            pltpu.VMEM((keys, HD), jnp.float32),
+            pltpu.VMEM((keys, HD), jnp.float32),
+        ],
+        compiler_params=pltpu.CompilerParams(vmem_limit_bytes=VMEM_BYTES),
+        cost_estimate=pl.CostEstimate(
+            flops=12 * products, bytes_accessed=6 * keys * HD * 2, transcendentals=chips * rows * keys
+        ),
+        name="attention",
+    )(*pairs, *query_grads)
+
+
+def add_kernel(chips, own_ref, other_ref, *outs):
+    rows = outs[0].shape[1]
+    for index in range(chips):
+        part = slice(index * rows, (index + 1) * rows)
+        outs[index][...] = (own_ref[:, part] + other_ref[:, part].astype(jnp.float32)).astype(
+            jnp.bfloat16
+        )
+
+
+def add_partials(own, other, chips):
+    rows = own.shape[1] // chips
+    block = jax.ShapeDtypeStruct((2, rows, HD), jnp.bfloat16)
+    return pl.pallas_call(
+        functools.partial(add_kernel, chips),
+        out_shape=[block] * chips,
+        in_specs=vmem_specs(2),
+        out_specs=vmem_specs(chips),
+        compiler_params=pltpu.CompilerParams(vmem_limit_bytes=VMEM_BYTES),
+        name="add_partials",
+    )(own, other)
+
+
+def to_chip(array, offset):
+    return lax.ppermute(
+        array, "seq", [(i, i ^ (2 * offset)) for i in range(lax.axis_size("seq"))]
+    )
+
+
+def to_core(array):
+    return lax.ppermute(array, "seq", [(i, i ^ 1) for i in range(lax.axis_size("seq"))])
+
+
+def exchange_order(chips):
+    return [offset for offset in sorted(range(1, chips), key=lambda o: (-o.bit_length(), o))]
+
+
+def exchange(blocks):
+    moved = list(blocks)
+    for offset in exchange_order(len(blocks)):
+        moved[offset] = to_chip(blocks[offset], offset)
+    return moved
+
+
+def shards_one_level(query_rows, key_rows, value_rows, grad_output):
+    chips = lax.axis_size("seq") // 2
+    chip = (lax.axis_index("seq") // 2).reshape(1)
+    pair_blocks = exchange(pack(chip, key_rows, value_rows, chips))
+    query_blocks = exchange(pack(chip, query_rows, grad_output, chips))
+    pair_blocks = pair_blocks + [to_core(block) for block in pair_blocks]
+    *out_blocks, own, other = attention(pair_blocks, query_blocks)
+    grad_blocks = add_partials(own, to_core(other), chips)
+    attended, query_grad = unpack(chip, exchange(out_blocks))
+    key_grad, value_grad = unpack(chip, exchange(grad_blocks))
+    return (attended, query_grad, key_grad, value_grad)
+
+
+def shards(query_rows, key_rows, value_rows, grad_output, dilation_offsets):
+    seq_width = lax.axis_size("seq")
+    if (
+        dilation_offsets.shape[0] == 1
+        and query_rows.shape[0] * seq_width == SEG
+        and query_rows.shape[1] // HD * 2 == seq_width
+    ):
+        return shards_one_level(query_rows, key_rows, value_rows, grad_output)
+    return shards_levels(query_rows, key_rows, value_rows, grad_output, dilation_offsets)
+
+
 def solution(mesh):
     in_specs = (
         P(("groups", "seq"), "head"),

time: 180 us -> 71.5 us (0.40)
  the two profiles are of different devices: /device:TPU:0 before, /device:TPU:12 now
where the time goes in v1:
time: 71.5 us; the launch traced here: 70.8 us
  waiting for transfers between devices  31.3 us (44%)
  Pallas kernels  21.3 us (30%)
  starting transfers between devices  14.5 us (20%)
  local copies, waits for them, and re-layouts  2.86 us (4%)
  between operations  0.78 us (1%)
    ppermute x12, waiting for transfers between devices, to_chip(): lax.ppermute(array, 'seq', [(i, i ^ 2 * offset) for i in range(lax.axis_s...  31.3 us
    ppermute x12, starting transfers between devices, to_chip(): lax.ppermute(array, 'seq', [(i, i ^ 2 * offset) for i in range(lax.axis_s...  14.5 us
    pallas_call x1, Pallas kernels, attention(): pl.pallas_call(functools.partial(attention_kernel, chips), out_shape=[blo...  11.3 us
    pallas_call x2, Pallas kernels, unpack(): pl.pallas_call(functools.partial(unpack_kernel, chips), out_shape=[whole]...  3.95 us
    pallas_call x2, Pallas kernels, pack(): pl.pallas_call(functools.partial(pack_kernel, chips), out_shape=[block] *...  3.86 us
    unnamed x36, local copies, waits for them, and re-layouts  2.86 us
    pallas_call x1, Pallas kernels, add_partials(): pl.pallas_call(functools.partial(add_kernel, chips), out_shape=[block] *...  2.19 us
  transfers between devices with their start and end apart: 17, of which 8 were waited for; matrix products, arithmetic and copies ran while one was open for 0% of the time, Pallas kernels for 9%

profile of v1, /device:TPU:12, one launch (start us, length us, event | category | flops | bytes accessed | tf_op | source)
XLA Modules:
  0.0 70.8 jit_solution(5017346935743880536)
XLA Ops:
  0.6 2.0 %pack.3 = (bf16[2,256,128]{2,1,0:T(8,128)(2,1)}, bf16[2,256,128]{2,1,0:T(8,128)(2,1)}, bf16[2,256,128]{2,1,0:T(8,128)(2,1)}, bf16[2,256,128]{2,1,0:T(8,128)(2,1)}) custom-call(s32[1]{0:T(128)} %bitcast.chip_ref, bf16[256,512]{1,0:T(8,128)(2,1)} %refs_0_.3, bf16[256,512]{1,0:T(8,128)(2,1)} %refs_1_.3), custom_call_target="tpu_custom_call" | custom-call | bytes 1048576 | tf_op jit(solution)/shard_map/pack/pallas_call | solution.py:268
  3.1 2.6 %collective-permute-start.8 = (bf16[2,256,128]{2,1,0:T(8,128)(2,1)}, bf16[2,256,128]{2,1,0:T(8,128)(2,1)S(1)}, u32[]{:S(2)}, u32[]{:S(2)}) collective-permute-start(bf16[2,256,128]{2,1,0:T(8,128)(2,1)} %get-tuple-element.32), channel_id=1, source_target_pairs={{0,8},{2,10},{4,12},{6,14},{8,0},{10,2},{12,4},{14,6},{1,9},{3,11}... | collective-permute-start | bytes 393224 | tf_op jit(solution)/shard_map/ppermute | solution.py:401
  5.6 1.9 %pack.2 = (bf16[2,256,128]{2,1,0:T(8,128)(2,1)}, bf16[2,256,128]{2,1,0:T(8,128)(2,1)}, bf16[2,256,128]{2,1,0:T(8,128)(2,1)}, bf16[2,256,128]{2,1,0:T(8,128)(2,1)}) custom-call(s32[1]{0:T(128)} %bitcast.chip_ref, bf16[256,512]{1,0:T(8,128)(2,1)} %refs_0_.2, bf16[256,512]{1,0:T(8,128)(2,1)} %refs_1_.2), custom_call_target="tpu_custom_call" | custom-call | bytes 1048576 | tf_op jit(solution)/shard_map/pack/pallas_call | solution.py:268
  7.5 1.6 %collective-permute-start = (bf16[2,256,128]{2,1,0:T(8,128)(2,1)}, bf16[2,256,128]{2,1,0:T(8,128)(2,1)S(1)}, u32[]{:S(2)}, u32[]{:S(2)}) collective-permute-start(bf16[2,256,128]{2,1,0:T(8,128)(2,1)} %get-tuple-element.27), channel_id=1, source_target_pairs={{0,4},{2,6},{4,0},{6,2},{8,12},{10,14},{12,8},{14,10},{1,5},{3,7},... | collective-permute-start | bytes 393224 | tf_op jit(solution)/shard_map/ppermute | solution.py:401
  9.5 1.6 %collective-permute-start.2 = (bf16[2,256,128]{2,1,0:T(8,128)(2,1)}, bf16[2,256,128]{2,1,0:T(8,128)(2,1)S(1)}, u32[]{:S(2)}, u32[]{:S(2)}) collective-permute-start(bf16[2,256,128]{2,1,0:T(8,128)(2,1)} %get-tuple-element.29), channel_id=1, source_target_pairs={{0,12},{2,14},{4,8},{6,10},{8,4},{10,6},{12,0},{14,2},{1,13},{3,15... | collective-permute-start | bytes 393224 | tf_op jit(solution)/shard_map/ppermute | solution.py:401
  11.0 0.9 %collective-permute-start.9 = (bf16[2,256,128]{2,1,0:T(8,128)(2,1)S(1)}, bf16[2,256,128]{2,1,0:T(8,128)(2,1)S(1)}, u32[]{:S(2)}, u32[]{:S(2)}) collective-permute-start(bf16[2,256,128]{2,1,0:T(8,128)(2,1)S(1)} %copy-done.12), channel_id=1, source_target_pairs={{0,12},{2,14},{4,8},{6,10},{8,4},{10,6},{12,0},{14,2},{1,13},{3,15... | collective-permute-start | bytes 393224 | tf_op jit(solution)/shard_map/ppermute | solution.py:401
  12.0 1.1 %collective-permute-done.8.refs_10_ = bf16[2,256,128]{2,1,0:T(8,128)(2,1)S(1)} collective-permute-done((bf16[2,256,128]{2,1,0:T(8,128)(2,1)}, bf16[2,256,128]{2,1,0:T(8,128)(2,1)S(1)}, u32[]{:S(2)}, u32[]{:S(2)}) %collective-permute-start.8) | collective-permute-done | bytes 131104 | tf_op jit(solution)/shard_map/ppermute | solution.py:401
  13.0 1.7 %collective-permute-done.refs_1_ = bf16[2,256,128]{2,1,0:T(8,128)(2,1)S(1)} collective-permute-done((bf16[2,256,128]{2,1,0:T(8,128)(2,1)}, bf16[2,256,128]{2,1,0:T(8,128)(2,1)S(1)}, u32[]{:S(2)}, u32[]{:S(2)}) %collective-permute-start) | collective-permute-done | bytes 131104 | tf_op jit(solution)/shard_map/ppermute | solution.py:401
  14.7 9.1 %collective-permute-done.1.refs_2_ = bf16[2,256,128]{2,1,0:T(8,128)(2,1)S(1)} collective-permute-done((bf16[2,256,128]{2,1,0:T(8,128)(2,1)}, bf16[2,256,128]{2,1,0:T(8,128)(2,1)S(1)}, u32[]{:S(2)}, u32[]{:S(2)}) %collective-permute-start.1) | collective-permute-done | bytes 131104 | tf_op jit(solution)/shard_map/ppermute | solution.py:401
  23.8 3.2 %collective-permute-done.2.refs_3_ = bf16[2,256,128]{2,1,0:T(8,128)(2,1)S(1)} collective-permute-done((bf16[2,256,128]{2,1,0:T(8,128)(2,1)}, bf16[2,256,128]{2,1,0:T(8,128)(2,1)S(1)}, u32[]{:S(2)}, u32[]{:S(2)}) %collective-permute-start.2) | collective-permute-done | bytes 131104 | tf_op jit(solution)/shard_map/ppermute | solution.py:401
  27.0 1.9 %collective-permute-done.9.refs_11_ = bf16[2,256,128]{2,1,0:T(8,128)(2,1)S(1)} collective-permute-done((bf16[2,256,128]{2,1,0:T(8,128)(2,1)S(1)}, bf16[2,256,128]{2,1,0:T(8,128)(2,1)S(1)}, u32[]{:S(2)}, u32[]{:S(2)}) %collective-permute-start.9) | collective-permute-done | bytes 131104 | tf_op jit(solution)/shard_map/ppermute | solution.py:401
  29.8 11.3 %attention.1 = (bf16[2,256,128]{2,1,0:T(8,128)(2,1)}, bf16[2,256,128]{2,1,0:T(8,128)(2,1)}, bf16[2,256,128]{2,1,0:T(8,128)(2,1)}, bf16[2,256,128]{2,1,0:T(8,128)...) custom-call(bf16[2,256,128]{2,1,0:T(8,128)(2,1)} %get-tuple-element.26.refs_0_, ...), custom_call_target="tpu_custom_call" | custom-call | flops 3221225472 | bytes 3145728 | tf_op jit(solution)/shard_map/attention/pallas_call | solution.py:355
  41.2 3.0 %collective-permute-start.11 = (bf16[2,256,128]{2,1,0:T(8,128)(2,1)}, bf16[2,256,128]{2,1,0:T(8,128)(2,1)S(1)}, u32[]{:S(2)}, u32[]{:S(2)}) collective-permute-start(bf16[2,256,128]{2,1,0:T(8,128)(2,1)} %get-tuple-element.36), channel_id=1, source_target_pairs={{0,8},{2,10},{4,12},{6,14},{8,0},{10,2},{12,4},{14,6},{1,9},{3,11}... | collective-permute-start | bytes 393224 | tf_op jit(solution)/shard_map/ppermute | solution.py:401
  44.7 0.8 %copy-done = bf16[2,1024,128]{2,1,0:T(8,128)(2,1)} copy-done((bf16[2,1024,128]{2,1,0:T(8,128)(2,1)}, bf16[2,1024,128]{2,1,0:T(8,128)(2,1)S(1)}, u32[]{:S(2)}) %copy-start) | copy-done | bytes 524312
  45.5 2.2 %add_partials.1 = (bf16[2,256,128]{2,1,0:T(8,128)(2,1)}, bf16[2,256,128]{2,1,0:T(8,128)(2,1)}, bf16[2,256,128]{2,1,0:T(8,128)(2,1)}, bf16[2,256,128]{2,1,0:T(8,128)(2,1)}) custom-call(f32[2,1024,128]{2,1,0:T(8,128)} %get-tuple-element.40.own_ref, bf16[2,1024,128]{2,1,0:T(8,128)(2,1)} %copy-done), custom_call_target="tpu_custom_call" | custom-call | tf_op jit(solution)/shard_map/add_partials/pallas_call | solution.py:390
  47.7 1.0 %collective-permute-start.14 = (bf16[2,256,128]{2,1,0:T(8,128)(2,1)}, bf16[2,256,128]{2,1,0:T(8,128)(2,1)S(1)}, u32[]{:S(2)}, u32[]{:S(2)}) collective-permute-start(bf16[2,256,128]{2,1,0:T(8,128)(2,1)} %get-tuple-element.43), channel_id=1, source_target_pairs={{0,4},{2,6},{4,0},{6,2},{8,12},{10,14},{12,8},{14,10},{1,5},{3,7},... | collective-permute-start | bytes 393224 | tf_op jit(solution)/shard_map/ppermute | solution.py:401
  48.7 2.0 %collective-permute-start.15 = (bf16[2,256,128]{2,1,0:T(8,128)(2,1)}, bf16[2,256,128]{2,1,0:T(8,128)(2,1)S(1)}, u32[]{:S(2)}, u32[]{:S(2)}) collective-permute-start(bf16[2,256,128]{2,1,0:T(8,128)(2,1)} %get-tuple-element.44), channel_id=1, source_target_pairs={{0,8},{2,10},{4,12},{6,14},{8,0},{10,2},{12,4},{14,6},{1,9},{3,11}... | collective-permute-start | bytes 393224 | tf_op jit(solution)/shard_map/ppermute | solution.py:401
  51.2 2.9 %collective-permute-done.11.refs_2_ = bf16[2,256,128]{2,1,0:T(8,128)(2,1)S(1)} collective-permute-done((bf16[2,256,128]{2,1,0:T(8,128)(2,1)}, bf16[2,256,128]{2,1,0:T(8,128)(2,1)S(1)}, u32[]{:S(2)}, u32[]{:S(2)}) %collective-permute-start.11) | collective-permute-done | bytes 131104 | tf_op jit(solution)/shard_map/ppermute | solution.py:401
  54.1 9.2 %collective-permute-done.12.refs_3_ = bf16[2,256,128]{2,1,0:T(8,128)(2,1)S(1)} collective-permute-done((bf16[2,256,128]{2,1,0:T(8,128)(2,1)}, bf16[2,256,128]{2,1,0:T(8,128)(2,1)S(1)}, u32[]{:S(2)}, u32[]{:S(2)}) %collective-permute-start.12) | collective-permute-done | bytes 131104 | tf_op jit(solution)/shard_map/ppermute | solution.py:401
  63.3 0.6 copy-done.5
  64.0 2.0 %unpack.2 = (bf16[256,512]{1,0:T(8,128)(2,1)}, bf16[256,512]{1,0:T(8,128)(2,1)}) custom-call(s32[1]{0:T(128)} %bitcast.chip_ref, bf16[2,256,128]{2,1,0:T(8,128)(2,1)} %get-tuple-element.34.refs_0_, bf16[2,256,128]{2,1,0:T(8,128)(2,1)} %copy-done.1, bf16[2,256,128]{2,1,0:T(8,128)(2,1)} %copy-done.3, bf16[2,256,128]{2,1,0:T(8,128)(2,1)} %copy-done.5), custom_call_target="tpu_custom_call" | custom-call | tf_op jit(solution)/shard_map/unpack/pallas_call | solution.py:292
  66.0 2.2 %collective-permute-done.16.refs_3_ = bf16[2,256,128]{2,1,0:T(8,128)(2,1)S(1)} collective-permute-done((bf16[2,256,128]{2,1,0:T(8,128)(2,1)}, bf16[2,256,128]{2,1,0:T(8,128)(2,1)S(1)}, u32[]{:S(2)}, u32[]{:S(2)}) %collective-permute-start.16) | collective-permute-done | bytes 131104 | tf_op jit(solution)/shard_map/ppermute | solution.py:401
  68.2 0.7 copy-done.6
  68.8 2.0 %unpack.3 = (bf16[256,512]{1,0:T(8,128)(2,1)}, bf16[256,512]{1,0:T(8,128)(2,1)}) custom-call(s32[1]{0:T(128)} %bitcast.chip_ref, bf16[2,256,128]{2,1,0:T(8,128)(2,1)} %get-tuple-element.42.refs_0_, bf16[2,256,128]{2,1,0:T(8,128)(2,1)} %copy-done.2, bf16[2,256,128]{2,1,0:T(8,128)(2,1)} %copy-done.4, bf16[2,256,128]{2,1,0:T(8,128)(2,1)} %copy-done.6), custom_call_target="tpu_custom_call" | custom-call | tf_op jit(solution)/shard_map/unpack/pallas_call | solution.py:292
  (52 shorter events, 2.6 us)
Async XLA Ops:
  2.6 8.4 %collective-permute-start.7 = (bf16[2,256,128]{2,1,0:T(8,128)(2,1)}, bf16[2,256,128]{2,1,0:T(8,128)(2,1)S(1)}, u32[]{:S(2)}, u32[]{:S(2)}) collective-permute-start(bf16[2,256,128]{2,1,0:T(8,128)(2,1)} %get-tuple-element.31), channel_id=1, source_target_pairs={{0,4},{2,6},{4,0},{6,2},{8,12},{10,14},{12,8},{14,10},{1,5},{3,7},... | collective-permute-start | bytes 393224 | tf_op jit(solution)/shard_map/ppermute | solution.py:401
  3.0 8.0 %copy-start.12 = (bf16[2,256,128]{2,1,0:T(8,128)(2,1)S(1)}, bf16[2,256,128]{2,1,0:T(8,128)(2,1)}, u32[]{:S(2)}) copy-start(bf16[2,256,128]{2,1,0:T(8,128)(2,1)} %get-tuple-element.33) | copy-start | bytes 393220
  3.1 10.0 %collective-permute-start.8 = (bf16[2,256,128]{2,1,0:T(8,128)(2,1)}, bf16[2,256,128]{2,1,0:T(8,128)(2,1)S(1)}, u32[]{:S(2)}, u32[]{:S(2)}) collective-permute-start(bf16[2,256,128]{2,1,0:T(8,128)(2,1)} %get-tuple-element.32), channel_id=1, source_target_pairs={{0,8},{2,10},{4,12},{6,14},{8,0},{10,2},{12,4},{14,6},{1,9},{3,11}... | collective-permute-start | bytes 393224 | tf_op jit(solution)/shard_map/ppermute | solution.py:401
  7.5 7.1 %collective-permute-start = (bf16[2,256,128]{2,1,0:T(8,128)(2,1)}, bf16[2,256,128]{2,1,0:T(8,128)(2,1)S(1)}, u32[]{:S(2)}, u32[]{:S(2)}) collective-permute-start(bf16[2,256,128]{2,1,0:T(8,128)(2,1)} %get-tuple-element.27), channel_id=1, source_target_pairs={{0,4},{2,6},{4,0},{6,2},{8,12},{10,14},{12,8},{14,10},{1,5},{3,7},... | collective-permute-start | bytes 393224 | tf_op jit(solution)/shard_map/ppermute | solution.py:401
  9.1 14.6 %collective-permute-start.1 = (bf16[2,256,128]{2,1,0:T(8,128)(2,1)}, bf16[2,256,128]{2,1,0:T(8,128)(2,1)S(1)}, u32[]{:S(2)}, u32[]{:S(2)}) collective-permute-start(bf16[2,256,128]{2,1,0:T(8,128)(2,1)} %get-tuple-element.28), channel_id=1, source_target_pairs={{0,8},{2,10},{4,12},{6,14},{8,0},{10,2},{12,4},{14,6},{1,9},{3,11}... | collective-permute-start | bytes 393224 | tf_op jit(solution)/shard_map/ppermute | solution.py:401
  9.5 17.5 %collective-permute-start.2 = (bf16[2,256,128]{2,1,0:T(8,128)(2,1)}, bf16[2,256,128]{2,1,0:T(8,128)(2,1)S(1)}, u32[]{:S(2)}, u32[]{:S(2)}) collective-permute-start(bf16[2,256,128]{2,1,0:T(8,128)(2,1)} %get-tuple-element.29), channel_id=1, source_target_pairs={{0,12},{2,14},{4,8},{6,10},{8,4},{10,6},{12,0},{14,2},{1,13},{3,15... | collective-permute-start | bytes 393224 | tf_op jit(solution)/shard_map/ppermute | solution.py:401
  11.0 18.0 %copy-start.7 = (bf16[2,256,128]{2,1,0:T(8,128)(2,1)}, bf16[2,256,128]{2,1,0:T(8,128)(2,1)S(1)}, u32[]{:S(2)}) copy-start(bf16[2,256,128]{2,1,0:T(8,128)(2,1)S(1)} %collective-permute-done.7.refs_9_) | copy-start | bytes 393220
  11.0 17.9 %collective-permute-start.9 = (bf16[2,256,128]{2,1,0:T(8,128)(2,1)S(1)}, bf16[2,256,128]{2,1,0:T(8,128)(2,1)S(1)}, u32[]{:S(2)}, u32[]{:S(2)}) collective-permute-start(bf16[2,256,128]{2,1,0:T(8,128)(2,1)S(1)} %copy-done.12), channel_id=1, source_target_pairs={{0,12},{2,14},{4,8},{6,10},{8,4},{10,6},{12,0},{14,2},{1,13},{3,15... | collective-permute-start | bytes 393224 | tf_op jit(solution)/shard_map/ppermute | solution.py:401
  13.0 16.0 %copy-start.8 = (bf16[2,256,128]{2,1,0:T(8,128)(2,1)}, bf16[2,256,128]{2,1,0:T(8,128)(2,1)S(1)}, u32[]{:S(2)}) copy-start(bf16[2,256,128]{2,1,0:T(8,128)(2,1)S(1)} %collective-permute-done.8.refs_10_) | copy-start | bytes 393220
  13.0 15.9 %collective-permute-start.3 = (bf16[2,256,128]{2,1,0:T(8,128)(2,1)}, bf16[2,256,128]{2,1,0:T(8,128)(2,1)S(1)}, u32[]{:S(2)}, u32[]{:S(2)}) collective-permute-start(bf16[2,256,128]{2,1,0:T(8,128)(2,1)} %get-tuple-element.26.refs_0_), channel_id=1, source_target_pairs={{0,2},{2,0},{4,6},{6,4},{8,10},{10,8},{12,14},{14,12},{1,3},{3,1},... | collective-permute-start | bytes 393224 | tf_op jit(solution)/shard_map/ppermute | solution.py:407
  14.7 14.3 %copy-start.9 = (bf16[2,256,128]{2,1,0:T(8,128)(2,1)}, bf16[2,256,128]{2,1,0:T(8,128)(2,1)S(1)}, u32[]{:S(2)}) copy-start(bf16[2,256,128]{2,1,0:T(8,128)(2,1)S(1)} %collective-permute-done.refs_1_) | copy-start | bytes 393220
  14.7 14.3 %collective-permute-start.4 = (bf16[2,256,128]{2,1,0:T(8,128)(2,1)S(1)}, bf16[2,256,128]{2,1,0:T(8,128)(2,1)S(1)}, u32[]{:S(2)}, u32[]{:S(2)}) collective-permute-start(bf16[2,256,128]{2,1,0:T(8,128)(2,1)S(1)} %collective-permute-done.refs_1_), channel_id=1, source_target_pairs={{0,2},{2,0},{4,6},{6,4},{8,10},{10,8},{12,14},{14,12},{1,3},{3,1},... | collective-permute-start | bytes 393224 | tf_op jit(solution)/shard_map/ppermute | solution.py:407
  23.8 5.3 %copy-start.10 = (bf16[2,256,128]{2,1,0:T(8,128)(2,1)}, bf16[2,256,128]{2,1,0:T(8,128)(2,1)S(1)}, u32[]{:S(2)}) copy-start(bf16[2,256,128]{2,1,0:T(8,128)(2,1)S(1)} %collective-permute-done.1.refs_2_) | copy-start | bytes 393220
  23.8 5.2 %collective-permute-start.5 = (bf16[2,256,128]{2,1,0:T(8,128)(2,1)S(1)}, bf16[2,256,128]{2,1,0:T(8,128)(2,1)S(1)}, u32[]{:S(2)}, u32[]{:S(2)}) collective-permute-start(bf16[2,256,128]{2,1,0:T(8,128)(2,1)S(1)} %collective-permute-done.1.refs_2_), channel_id=1, source_target_pairs={{0,2},{2,0},{4,6},{6,4},{8,10},{10,8},{12,14},{14,12},{1,3},{3,1},... | collective-permute-start | bytes 393224 | tf_op jit(solution)/shard_map/ppermute | solution.py:407
  27.0 2.0 %collective-permute-start.6 = (bf16[2,256,128]{2,1,0:T(8,128)(2,1)S(1)}, bf16[2,256,128]{2,1,0:T(8,128)(2,1)S(1)}, u32[]{:S(2)}, u32[]{:S(2)}) collective-permute-start(bf16[2,256,128]{2,1,0:T(8,128)(2,1)S(1)} %collective-permute-done.2.refs_3_), channel_id=1, source_target_pairs={{0,2},{2,0},{4,6},{6,4},{8,10},{10,8},{12,14},{14,12},{1,3},{3,1},... | collective-permute-start | bytes 393224 | tf_op jit(solution)/shard_map/ppermute | solution.py:407
  41.1 3.6 %collective-permute-start.13 = (bf16[2,1024,128]{2,1,0:T(8,128)(2,1)}, bf16[2,1024,128]{2,1,0:T(8,128)(2,1)S(1)}, u32[]{:S(2)}, u32[]{:S(2)}) collective-permute-start(bf16[2,1024,128]{2,1,0:T(8,128)(2,1)} %get-tuple-element.41), channel_id=1, source_target_pairs={{0,2},{2,0},{4,6},{6,4},{8,10},{10,8},{12,14},{14,12},{1,3},{3,1},... | collective-permute-start | bytes 1572872 | tf_op jit(solution)/shard_map/ppermute | solution.py:407
  41.1 9.6 %collective-permute-start.10 = (bf16[2,256,128]{2,1,0:T(8,128)(2,1)}, bf16[2,256,128]{2,1,0:T(8,128)(2,1)S(1)}, u32[]{:S(2)}, u32[]{:S(2)}) collective-permute-start(bf16[2,256,128]{2,1,0:T(8,128)(2,1)} %get-tuple-element.35), channel_id=1, source_target_pairs={{0,4},{2,6},{4,0},{6,2},{8,12},{10,14},{12,8},{14,10},{1,5},{3,7},... | collective-permute-start | bytes 393224 | tf_op jit(solution)/shard_map/ppermute | solution.py:401
  41.2 12.9 %collective-permute-start.11 = (bf16[2,256,128]{2,1,0:T(8,128)(2,1)}, bf16[2,256,128]{2,1,0:T(8,128)(2,1)S(1)}, u32[]{:S(2)}, u32[]{:S(2)}) collective-permute-start(bf16[2,256,128]{2,1,0:T(8,128)(2,1)} %get-tuple-element.36), channel_id=1, source_target_pairs={{0,8},{2,10},{4,12},{6,14},{8,0},{10,2},{12,4},{14,6},{1,9},{3,11}... | collective-permute-start | bytes 393224 | tf_op jit(solution)/shard_map/ppermute | solution.py:401
  44.2 19.1 %collective-permute-start.12 = (bf16[2,256,128]{2,1,0:T(8,128)(2,1)}, bf16[2,256,128]{2,1,0:T(8,128)(2,1)S(1)}, u32[]{:S(2)}, u32[]{:S(2)}) collective-permute-start(bf16[2,256,128]{2,1,0:T(8,128)(2,1)} %get-tuple-element.37), channel_id=1, source_target_pairs={{0,12},{2,14},{4,8},{6,10},{8,4},{10,6},{12,0},{14,2},{1,13},{3,15... | collective-permute-start | bytes 393224 | tf_op jit(solution)/shard_map/ppermute | solution.py:401
  47.7 18.3 %collective-permute-start.14 = (bf16[2,256,128]{2,1,0:T(8,128)(2,1)}, bf16[2,256,128]{2,1,0:T(8,128)(2,1)S(1)}, u32[]{:S(2)}, u32[]{:S(2)}) collective-permute-start(bf16[2,256,128]{2,1,0:T(8,128)(2,1)} %get-tuple-element.43), channel_id=1, source_target_pairs={{0,4},{2,6},{4,0},{6,2},{8,12},{10,14},{12,8},{14,10},{1,5},{3,7},... | collective-permute-start | bytes 393224 | tf_op jit(solution)/shard_map/ppermute | solution.py:401
  48.7 17.3 %collective-permute-start.15 = (bf16[2,256,128]{2,1,0:T(8,128)(2,1)}, bf16[2,256,128]{2,1,0:T(8,128)(2,1)S(1)}, u32[]{:S(2)}, u32[]{:S(2)}) collective-permute-start(bf16[2,256,128]{2,1,0:T(8,128)(2,1)} %get-tuple-element.44), channel_id=1, source_target_pairs={{0,8},{2,10},{4,12},{6,14},{8,0},{10,2},{12,4},{14,6},{1,9},{3,11}... | collective-permute-start | bytes 393224 | tf_op jit(solution)/shard_map/ppermute | solution.py:401
  50.7 12.6 %copy-start.1 = (bf16[2,256,128]{2,1,0:T(8,128)(2,1)}, bf16[2,256,128]{2,1,0:T(8,128)(2,1)S(1)}, u32[]{:S(2)}) copy-start(bf16[2,256,128]{2,1,0:T(8,128)(2,1)S(1)} %collective-permute-done.10.refs_1_) | copy-start | bytes 393220
  50.7 17.5 %collective-permute-start.16 = (bf16[2,256,128]{2,1,0:T(8,128)(2,1)}, bf16[2,256,128]{2,1,0:T(8,128)(2,1)S(1)}, u32[]{:S(2)}, u32[]{:S(2)}) collective-permute-start(bf16[2,256,128]{2,1,0:T(8,128)(2,1)} %get-tuple-element.45), channel_id=1, source_target_pairs={{0,12},{2,14},{4,8},{6,10},{8,4},{10,6},{12,0},{14,2},{1,13},{3,15... | collective-permute-start | bytes 393224 | tf_op jit(solution)/shard_map/ppermute | solution.py:401
  54.1 9.2 %copy-start.3 = (bf16[2,256,128]{2,1,0:T(8,128)(2,1)}, bf16[2,256,128]{2,1,0:T(8,128)(2,1)S(1)}, u32[]{:S(2)}) copy-start(bf16[2,256,128]{2,1,0:T(8,128)(2,1)S(1)} %collective-permute-done.11.refs_2_) | copy-start | bytes 393220
  (11 other events, 12.3 us)

commit v2 on v0

--- a/solution.py
+++ b/solution.py
@@ -1,6 +1,10 @@
+import functools
+
 import jax
 import jax.numpy as jnp
 from jax import lax
+from jax.experimental import pallas as pl
+from jax.experimental.pallas import tpu as pltpu
 from jax.sharding import PartitionSpec as P
 
 HD = 128
@@ -122,7 +126,7 @@
     return (query_part_grad, grad_term)
 
 
-def shards(query_rows, key_rows, value_rows, grad_output, dilation_offsets):
+def shards_levels(query_rows, key_rows, value_rows, grad_output, dilation_offsets):
     row_count = query_rows.shape[0]
     head_count = query_rows.shape[1] // HD
     level_count = dilation_offsets.shape[0]
@@ -236,6 +240,272 @@
     )
 
 
+NT = (((1,), (1,)), ((), ()))
+TN = (((0,), (0,)), ((), ()))
+MIB = 2**20
+FORWARD_ROWS = 128
+BACKWARD_ROWS = 256
+
+
+def vmem_specs(count):
+    return [pl.BlockSpec(memory_space=pltpu.VMEM)] * count
+
+
+def any_specs(count):
+    return [pl.BlockSpec(memory_space=pl.ANY)] * count
+
+
+def head_columns(chip, offset):
+    return pl.ds(pl.multiple_of((chip ^ offset) * HD, HD), HD)
+
+
+def pack(chip, arrays, offset):
+    start = (chip[0] ^ offset) * HD
+    return jnp.stack([lax.dynamic_slice_in_dim(array, start, HD, axis=1) for array in arrays])
+
+
+def unpack_kernel(layout, chip_ref, *refs):
+    count = max(max(arrays) for _, arrays in layout) + 1
+    blocks, outs, sems = refs[: len(layout)], refs[len(layout) : -1], refs[-1]
+    chip = chip_ref[0]
+    copies = []
+    for at, (offset, arrays) in enumerate(layout):
+        for place, index in enumerate(arrays):
+            copies.append(
+                pltpu.make_async_copy(
+                    blocks[at].at[place],
+                    outs[index].at[:, head_columns(chip, offset)],
+                    sems.at[at, place],
+                )
+            )
+    for copy in copies:
+        copy.start()
+    for copy in copies:
+        copy.wait()
+
+
+def unpack(chip, blocks, layout, width):
+    count = max(max(arrays) for _, arrays in layout) + 1
+    rows = blocks[0].shape[1]
+    return pl.pallas_call(
+        functools.partial(unpack_kernel, layout),
+        out_shape=[jax.ShapeDtypeStruct((rows, width), blocks[0].dtype)] * count,
+        in_specs=[pl.BlockSpec(memory_space=pltpu.SMEM)] + any_specs(len(blocks)),
+        out_specs=any_specs(count),
+        scratch_shapes=[pltpu.SemaphoreType.DMA((len(layout), count))],
+        compiler_params=pltpu.CompilerParams(vmem_limit_bytes=MIB),
+        name="unpack",
+    )(chip, *blocks)
+
+
+def forward_kernel(chips, *refs):
+    blocks = refs[: 2 * chips]
+    outs = refs[2 * chips : 3 * chips]
+    probs_ref, scale_ref, key_ref, value_ref = refs[3 * chips :]
+    rows = blocks[0].shape[1]
+    for index, block in enumerate(blocks):
+        key_ref[index * rows : (index + 1) * rows] = block[0]
+        value_ref[index * rows : (index + 1) * rows, :HD] = block[1]
+    value_ref[:, HD:] = jnp.ones((value_ref.shape[0], HD), value_ref.dtype)
+    exp_scale = HD ** (-0.5) * 1.4426950408889634
+    key_all = key_ref[...]
+    value_all = value_ref[...]
+    step = min(FORWARD_ROWS, rows)
+    for index in range(chips):
+        for start in range(0, rows, step):
+            query = blocks[index][2, start : start + step]
+            scores = lax.dot_general(query, key_all, NT, preferred_element_type=jnp.float32)
+            row_peak = jnp.max(scores, axis=1, keepdims=True)
+            probs = jnp.exp2(scores * exp_scale - row_peak * exp_scale).astype(jnp.bfloat16)
+            here = slice(index * rows + start, index * rows + start + step)
+            probs_ref[here] = probs
+            sums = jnp.dot(probs, value_all, preferred_element_type=jnp.float32)
+            row_scale = 1.0 / sums[:, HD:]
+            scale_ref[here] = row_scale
+            outs[index][0, start : start + step] = (sums[:, :HD] * row_scale).astype(jnp.bfloat16)
+
+
+def forward(blocks, chips):
+    rows = blocks[0].shape[1]
+    queries = chips * rows
+    keys = 2 * queries
+    products = queries * keys * HD
+    return pl.pallas_call(
+        functools.partial(forward_kernel, chips),
+        out_shape=[jax.ShapeDtypeStruct((1, rows, HD), jnp.bfloat16)] * chips
+        + [
+            jax.ShapeDtypeStruct((queries, keys), jnp.bfloat16),
+            jax.ShapeDtypeStruct((queries, HD), jnp.float32),
+        ],
+        in_specs=vmem_specs(2 * chips),
+        out_specs=vmem_specs(chips + 2),
+        scratch_shapes=[
+            pltpu.VMEM((keys, HD), jnp.bfloat16),
+            pltpu.VMEM((keys, 2 * HD), jnp.bfloat16),
+        ],
+        compiler_params=pltpu.CompilerParams(vmem_limit_bytes=20 * MIB),
+        cost_estimate=pl.CostEstimate(
+            flops=4 * products, bytes_accessed=8 * MIB, transcendentals=queries * keys
+        ),
+        name="forward",
+    )(*blocks)
+
+
+def backward_kernel(chips, first, *refs):
+    blocks = refs[:chips]
+    key_blocks = refs[chips : 2 * chips]
+    attended = refs[2 * chips : 3 * chips]
+    probs_ref, scale_ref = refs[3 * chips : 3 * chips + 2]
+    if first:
+        query_ref, pair_ref, key_ref, value_ref, dkey_ref, dvalue_ref = refs[3 * chips + 2 :]
+    else:
+        query_ref = refs[3 * chips + 2]
+        outs = refs[3 * chips + 3 : 4 * chips + 3]
+        pair_ref, key_ref, value_ref, dkey_ref, dvalue_ref = refs[4 * chips + 3 :]
+    rows = blocks[0].shape[1]
+    score_scale = HD ** (-0.5)
+    for index, block in enumerate(key_blocks):
+        key_ref[index * rows : (index + 1) * rows] = block[0]
+        value_ref[index * rows : (index + 1) * rows] = block[1]
+    key_all = key_ref[...]
+    value_all = value_ref[...]
+    columns = slice(chips * rows, 2 * chips * rows) if first else slice(0, chips * rows)
+    step = min(BACKWARD_ROWS, rows)
+    fresh = True
+    for index in range(chips):
+        for start in range(0, rows, step):
+            part = slice(start, start + step)
+            here = slice(index * rows + start, index * rows + start + step)
+            query = blocks[index][2, part]
+            grad = blocks[index][3, part].astype(jnp.float32) * scale_ref[here]
+            grad = grad.astype(jnp.bfloat16)
+            probs = probs_ref[here, columns]
+            delta = jnp.sum(
+                attended[index][0, part].astype(jnp.float32) * grad.astype(jnp.float32),
+                axis=1,
+                keepdims=True,
+            )
+            dprobs = lax.dot_general(grad, value_all, NT, preferred_element_type=jnp.float32)
+            dscore = (probs.astype(jnp.float32) * (dprobs - delta)).astype(jnp.bfloat16)
+            query_grad = jnp.dot(dscore, key_all, preferred_element_type=jnp.float32)
+            if first:
+                query_ref[here] = query_grad
+            else:
+                query_grad = (query_grad + query_ref[here]) * score_scale
+                outs[index][0, part] = query_grad.astype(jnp.bfloat16)
+            dkey = lax.dot_general(dscore, query, TN, preferred_element_type=jnp.float32)
+            dvalue = lax.dot_general(probs, grad, TN, preferred_element_type=jnp.float32)
+            if fresh:
+                dkey_ref[...] = dkey
+                dvalue_ref[...] = dvalue
+                fresh = False
+            else:
+                dkey_ref[...] += dkey
+                dvalue_ref[...] += dvalue
+    pair_ref[0] = (dkey_ref[...] * score_scale).astype(pair_ref.dtype)
+    pair_ref[1] = dvalue_ref[...].astype(pair_ref.dtype)
+
+
+def backward(first, blocks, key_blocks, attended, probs, scale, query_terms=()):
+    chips = len(blocks)
+    rows = blocks[0].shape[1]
+    queries = probs.shape[0]
+    query_outs = [jax.ShapeDtypeStruct((queries, HD), jnp.float32)]
+    if not first:
+        query_outs = [jax.ShapeDtypeStruct((1, rows, HD), jnp.bfloat16)] * chips
+    return pl.pallas_call(
+        functools.partial(backward_kernel, chips, first),
+        out_shape=query_outs
+        + [jax.ShapeDtypeStruct((2, queries, HD), jnp.bfloat16 if first else jnp.float32)],
+        in_specs=vmem_specs(3 * chips + 2 + len(query_terms)),
+        out_specs=vmem_specs(len(query_outs) + 1),
+        scratch_shapes=[
+            pltpu.VMEM((queries, HD), jnp.bfloat16),
+            pltpu.VMEM((queries, HD), jnp.bfloat16),
+            pltpu.VMEM((queries, HD), jnp.float32),
+            pltpu.VMEM((queries, HD), jnp.float32),
+        ],
+        compiler_params=pltpu.CompilerParams(vmem_limit_bytes=20 * MIB),
+        cost_estimate=pl.CostEstimate(
+            flops=8 * queries * queries * HD, bytes_accessed=4 * MIB, transcendentals=0
+        ),
+        name="backward",
+    )(*blocks, *key_blocks, *attended, probs, scale, *query_terms)
+
+
+def add_kernel(chips, own_ref, other_ref, *refs):
+    outs = refs[-chips:]
+    rows = outs[0].shape[1]
+    for index, out in enumerate(outs):
+        part = slice(index * rows, (index + 1) * rows)
+        total = own_ref[:, part] + other_ref[:, part].astype(jnp.float32)
+        out[0:2] = total.astype(jnp.bfloat16)
+        out[2] = refs[index][0]
+        if out.shape[0] == 4:
+            out[3] = refs[chips + index][0]
+
+
+def add_partials(own, other, query_blocks, attended_near):
+    chips = len(query_blocks)
+    rows = own.shape[1] // chips
+    return pl.pallas_call(
+        functools.partial(add_kernel, chips),
+        out_shape=[
+            jax.ShapeDtypeStruct((4 if index < len(attended_near) else 3, rows, HD), jnp.bfloat16)
+            for index in range(chips)
+        ],
+        in_specs=vmem_specs(2 + chips + len(attended_near)),
+        out_specs=vmem_specs(chips),
+        compiler_params=pltpu.CompilerParams(vmem_limit_bytes=8 * MIB),
+        cost_estimate=pl.CostEstimate(
+            flops=own.size, bytes_accessed=8 * own.size, transcendentals=0
+        ),
+        name="add_partials",
+    )(own, other, *query_blocks, *attended_near)
+
+
+def to_chip(array, offset):
+    return lax.ppermute(
+        array, "seq", [(i, i ^ (2 * offset)) for i in range(lax.axis_size("seq"))]
+    )
+
+
+def to_core(array):
+    return lax.ppermute(array, "seq", [(i, i ^ 1) for i in range(lax.axis_size("seq"))])
+
+
+def shards_one_level(query_rows, key_rows, value_rows, grad_output):
+    chips = lax.axis_size("seq") // 2
+    chip = (lax.axis_index("seq") // 2).reshape(1)
+    far = sorted(range(2, chips), key=lambda offset: (-offset.bit_length(), offset))
+    arrays = [key_rows, value_rows, query_rows, grad_output]
+    blocks = [None] * chips
+    for offset in far + [1]:
+        blocks[offset] = to_chip(pack(chip, arrays, offset), offset)
+    blocks[0] = pack(chip, arrays, 0)
+    others = [to_core(block) for block in blocks]
+    *attended, probs, scale = forward(blocks + others, chips)
+    query_terms, other = backward(True, blocks, others, attended, probs, scale)
+    other = to_core(other)
+    *query_blocks, own = backward(False, blocks, blocks, attended, probs, scale, [query_terms])
+    outs = add_partials(own, other, query_blocks, attended)
+    moved = [outs[0]] + [to_chip(outs[offset], offset) for offset in range(1, chips)]
+    out_blocks = moved
+    out_layout = [(offset, (2, 3, 1, 0)[: outs[offset].shape[0]]) for offset in range(chips)]
+    return tuple(unpack(chip, out_blocks, out_layout, query_rows.shape[1]))
+
+
+def shards(query_rows, key_rows, value_rows, grad_output, dilation_offsets):
+    seq_width = lax.axis_size("seq")
+    if (
+        dilation_offsets.shape[0] == 1
+        and query_rows.shape[0] * seq_width == SEG
+        and query_rows.shape[1] // HD * 2 == seq_width
+    ):
+        return shards_one_level(query_rows, key_rows, value_rows, grad_output)
+    return shards_levels(query_rows, key_rows, value_rows, grad_output, dilation_offsets)
+
+
 def solution(mesh):
     in_specs = (
         P(("groups", "seq"), "head"),

time: 180 us -> 66.9 us (0.37)
  the two profiles are of different devices: /device:TPU:0 before, /device:TPU:12 now
where the time goes in v2:
time: 66.9 us; the launch traced here: 65.8 us
  waiting for transfers between devices  45.3 us (68%)
  Pallas kernels  9.35 us (14%)
  starting transfers between devices  8 us (12%)
  local copies, waits for them, and re-layouts  2.25 us (3%)
  between operations  0.76 us (1%)
    ppermute x6, waiting for transfers between devices, to_chip(): lax.ppermute(array, 'seq', [(i, i ^ 2 * offset) for i in range(lax.axis_s...  43.8 us
    ppermute x6, starting transfers between devices, to_chip(): lax.ppermute(array, 'seq', [(i, i ^ 2 * offset) for i in range(lax.axis_s...  7.7 us
    pallas_call x2, Pallas kernels, backward(): pl.pallas_call(functools.partial(backward_kernel, chips, first), out_shap...  4.76 us
    pallas_call x1, Pallas kernels, forward(): pl.pallas_call(functools.partial(forward_kernel, chips), out_shape=[jax.S...  3.39 us
    another operation x2, local copies, waits for them, and re-layouts, pack(): jnp.stack([lax.dynamic_slice_in_dim(array, start, HD, axis=1) for array i...  2.25 us
    ppermute x5, waiting for transfers between devices, to_core(): lax.ppermute(array, 'seq', [(i, i ^ 1) for i in range(lax.axis_size('seq'...  1.52 us
  transfers between devices with their start and end apart: 11, of which 7 were waited for; matrix products, arithmetic and copies ran while one was open for 0% of the time, Pallas kernels for 4%

profile of v2, /device:TPU:12, one launch (start us, length us, event | category | flops | bytes accessed | tf_op | source)
XLA Modules:
  0.0 65.8 jit_solution(11532157420791543530)
XLA Ops:
  0.7 1.1 %dynamic-slice_bitcast_fusion = (bf16[1,256,128]{2,1,0:T(8,128)(2,1)S(1)}, bf16[1,256,128]{2,1,0:T(8,128)(2,1)S(1)}, bf16[1,256,128]{2,1,0:T(8,128)(2,1)S(1)}, b...) fusion(bf16[256,512]{1,0:T(8,128)(2,1)} %param.8, ...), kind=kLoop, calls=%fused_computation.4 | loop fusion | bytes 1048592 | tf_op jit(solution)/shard_map/stack | solution.py:264
  1.8 1.1 %dynamic-slice_bitcast_fusion.2 = (bf16[1,256,128]{2,1,0:T(8,128)(2,1)S(1)}, bf16[1,256,128]{2,1,0:T(8,128)(2,1)S(1)}, bf16[1,256,128]{2,1,0:T(8,128)(2,1)S(1)},...) fusion(bf16[256,512]{1,0:T(8,128)(2,1)} %param.7, ...), kind=kLoop, calls=%fused_computation.6 | loop fusion | bytes 1048592 | tf_op jit(solution)/shard_map/stack | solution.py:264
  3.0 2.7 %collective-permute-start.1 = (bf16[4,256,128]{2,1,0:T(8,128)(2,1)S(1)}, bf16[4,256,128]{2,1,0:T(8,128)(2,1)S(1)}, u32[]{:S(2)}, u32[]{:S(2)}) collective-permute-start(bf16[4,256,128]{2,1,0:T(8,128)(2,1)S(1)} %pad_maximum_fusion.2), channel_id=1, source_target_pairs={{0,8},{2,10},{4,12},{6,14},{8,0},{10,2},{12,4},{14,6},{1,9},{3,11}... | collective-permute-start | bytes 786440 | tf_op jit(solution)/shard_map/ppermute | solution.py:468
  5.7 0.5 collective-permute-start
  6.2 0.5 collective-permute-start.2
  6.8 0.1 collective-permute-start.3
  6.9 10.8 %collective-permute-done.1.refs_2_.refs_6_ = bf16[4,256,128]{2,1,0:T(8,128)(2,1)S(1)} collective-permute-done((bf16[4,256,128]{2,1,0:T(8,128)(2,1)S(1)}, bf16[4,256,128]{2,1,0:T(8,128)(2,1)S(1)}, u32[]{:S(2)}, u32[]{:S(2)}) %collective-permute-start.1) | collective-permute-done | bytes 262176 | tf_op jit(solution)/shard_map/ppermute | solution.py:468
  17.7 1.2 %collective-permute-done.refs_1_.refs_5_ = bf16[4,256,128]{2,1,0:T(8,128)(2,1)S(1)} collective-permute-done((bf16[4,256,128]{2,1,0:T(8,128)(2,1)S(1)}, bf16[4,256,128]{2,1,0:T(8,128)(2,1)S(1)}, u32[]{:S(2)}, u32[]{:S(2)}) %collective-permute-start) | collective-permute-done | bytes 262176 | tf_op jit(solution)/shard_map/ppermute | solution.py:468
  18.9 0.0 collective-permute-start.4
  18.9 9.0 %collective-permute-done.2.refs_3_.refs_7_ = bf16[4,256,128]{2,1,0:T(8,128)(2,1)S(1)} collective-permute-done((bf16[4,256,128]{2,1,0:T(8,128)(2,1)S(1)}, bf16[4,256,128]{2,1,0:T(8,128)(2,1)S(1)}, u32[]{:S(2)}, u32[]{:S(2)}) %collective-permute-start.2) | collective-permute-done | bytes 262176 | tf_op jit(solution)/shard_map/ppermute | solution.py:468
  27.9 0.0 collective-permute-start.6
  28.0 0.0 collective-permute-done.5.refs_6_
  28.0 1.5 %collective-permute-done.6.refs_7_ = bf16[4,256,128]{2,1,0:T(8,128)(2,1)S(1)} collective-permute-done((bf16[4,256,128]{2,1,0:T(8,128)(2,1)S(1)}, bf16[4,256,128]{2,1,0:T(8,128)(2,1)S(1)}, u32[]{:S(2)}, u32[]{:S(2)}) %collective-permute-start.6) | collective-permute-done | bytes 262176 | tf_op jit(solution)/shard_map/ppermute | solution.py:474
  29.5 3.4 %forward.1 = (bf16[1,256,128]{2,1,0:T(8,128)(2,1)S(1)}, bf16[1,256,128]{2,1,0:T(8,128)(2,1)S(1)}, bf16[1,256,128]{2,1,0:T(8,128)(2,1)S(1)}, bf16[1,256,128]{2,1,...) custom-call(bf16[4,256,128]{2,1,0:T(8,128)(2,1)S(1)} %pad_maximum_fusion.refs_0_.refs_4_, ...), custom_call_target="tpu_custom_call" | custom-call | flops 1073741824 | bytes 8388608 | tf_op jit(solution)/shard_map/forward/pallas_call | solution.py:333
  32.9 2.4 %backward.2 = (f32[1024,128]{1,0:T(8,128)S(1)}, bf16[2,1024,128]{2,1,0:T(8,128)(2,1)S(1)}) custom-call(bf16[4,256,128]{2,1,0:T(8,128)(2,1)S(1)} %pad_maximum_fusion.refs_0_.refs_4_, bf16[4,256,128]{2,1,0:T(8,128)(2,1)S(1)} %collective-permute-done.refs_1_.refs_5_, bf16[4,256,128]{2,1,0:T(8,128)(2,1)S(1)} %collective-permute-done.1.refs_2_.refs_6_, ...), custom_call_target="tpu_custom_call" | custom-call | flops 1073741824 | bytes 4194304 | tf_op jit(solution)/shard_map/backward/pallas_call | solution.py:416
  35.3 0.2 collective-permute-start.7
  35.5 2.4 %backward.3 = (bf16[1,256,128]{2,1,0:T(8,128)(2,1)S(1)}, bf16[1,256,128]{2,1,0:T(8,128)(2,1)S(1)}, bf16[1,256,128]{2,1,0:T(8,128)(2,1)S(1)}, bf16[1,256,128]{2,1,0:T(8,128)(2,1)S(1)}, f32[2,1024,128]{2,1,0:T(8,128)S(1)}) custom-call(bf16[4,256,128]{2,1,0:T(8,128)(2,1)S(1)} %pad_maximum_fusion.refs_0_.refs_4_, ...), custom_call_target="tpu_custom_call" | custom-call | flops 1073741824 | bytes 4194304 | tf_op jit(solution)/shard_map/backward/pallas_call | solution.py:416
  37.8 0.1 add_partials.1
  38.0 0.1 collective-permute-start.8
  38.0 3.9 %collective-permute-start.9 = (bf16[4,256,128]{2,1,0:T(8,128)(2,1)S(1)}, bf16[4,256,128]{2,1,0:T(8,128)(2,1)S(1)}, u32[]{:S(2)}, u32[]{:S(2)}) collective-permute-start(bf16[4,256,128]{2,1,0:T(8,128)(2,1)S(1)} %get-tuple-element.36), channel_id=1, source_target_pairs={{0,8},{2,10},{4,12},{6,14},{8,0},{10,2},{12,4},{14,6},{1,9},{3,11}... | collective-permute-start | bytes 786440 | tf_op jit(solution)/shard_map/ppermute | solution.py:468
  42.0 8.0 %collective-permute-done.8.refs_1_ = bf16[4,256,128]{2,1,0:T(8,128)(2,1)S(1)} collective-permute-done((bf16[4,256,128]{2,1,0:T(8,128)(2,1)S(1)}, bf16[4,256,128]{2,1,0:T(8,128)(2,1)S(1)}, u32[]{:S(2)}, u32[]{:S(2)}) %collective-permute-start.8) | collective-permute-done | bytes 262176 | tf_op jit(solution)/shard_map/ppermute | solution.py:468
  50.0 10.0 %collective-permute-done.9.refs_2_ = bf16[4,256,128]{2,1,0:T(8,128)(2,1)S(1)} collective-permute-done((bf16[4,256,128]{2,1,0:T(8,128)(2,1)S(1)}, bf16[4,256,128]{2,1,0:T(8,128)(2,1)S(1)}, u32[]{:S(2)}, u32[]{:S(2)}) %collective-permute-start.9) | collective-permute-done | bytes 262176 | tf_op jit(solution)/shard_map/ppermute | solution.py:468
  60.0 4.8 %collective-permute-done.10.refs_3_ = bf16[4,256,128]{2,1,0:T(8,128)(2,1)S(1)} collective-permute-done((bf16[4,256,128]{2,1,0:T(8,128)(2,1)S(1)}, bf16[4,256,128]{2,1,0:T(8,128)(2,1)S(1)}, u32[]{:S(2)}, u32[]{:S(2)}) %collective-permute-start.10) | collective-permute-done | bytes 262176 | tf_op jit(solution)/shard_map/ppermute | solution.py:468
  64.7 1.1 %unpack.1 = (bf16[256,512]{1,0:T(8,128)(2,1)}, bf16[256,512]{1,0:T(8,128)(2,1)}, bf16[256,512]{1,0:T(8,128)(2,1)}, bf16[256,512]{1,0:T(8,128)(2,1)}) custom-call(s32[1]{0:T(128)} %bitcast.chip_ref, bf16[4,256,128]{2,1,0:T(8,128)(2,1)S(1)} %get-tuple-element.34.refs_0_, bf16[4,256,128]{2,1,0:T(8,128)(2,1)S(1)} %collective-permute-done.8.refs_1_, ...), custom_call_target="tpu_custom_call" | custom-call | tf_op jit(solution)/shard_map/unpack/pallas_call | solution.py:290
  (9 shorter events, 0.2 us)
Async XLA Ops:
  3.0 14.7 %collective-permute-start.1 = (bf16[4,256,128]{2,1,0:T(8,128)(2,1)S(1)}, bf16[4,256,128]{2,1,0:T(8,128)(2,1)S(1)}, u32[]{:S(2)}, u32[]{:S(2)}) collective-permute-start(bf16[4,256,128]{2,1,0:T(8,128)(2,1)S(1)} %pad_maximum_fusion.2), channel_id=1, source_target_pairs={{0,8},{2,10},{4,12},{6,14},{8,0},{10,2},{12,4},{14,6},{1,9},{3,11}... | collective-permute-start | bytes 786440 | tf_op jit(solution)/shard_map/ppermute | solution.py:468
  5.7 13.2 %collective-permute-start = (bf16[4,256,128]{2,1,0:T(8,128)(2,1)S(1)}, bf16[4,256,128]{2,1,0:T(8,128)(2,1)S(1)}, u32[]{:S(2)}, u32[]{:S(2)}) collective-permute-start(bf16[4,256,128]{2,1,0:T(8,128)(2,1)S(1)} %pad_maximum_fusion.1), channel_id=1, source_target_pairs={{0,4},{2,6},{4,0},{6,2},{8,12},{10,14},{12,8},{14,10},{1,5},{3,7},... | collective-permute-start | bytes 786440 | tf_op jit(solution)/shard_map/ppermute | solution.py:468
  6.2 21.7 %collective-permute-start.2 = (bf16[4,256,128]{2,1,0:T(8,128)(2,1)S(1)}, bf16[4,256,128]{2,1,0:T(8,128)(2,1)S(1)}, u32[]{:S(2)}, u32[]{:S(2)}) collective-permute-start(bf16[4,256,128]{2,1,0:T(8,128)(2,1)S(1)} %pad_maximum_fusion.3), channel_id=1, source_target_pairs={{0,12},{2,14},{4,8},{6,10},{8,4},{10,6},{12,0},{14,2},{1,13},{3,15... | collective-permute-start | bytes 786440 | tf_op jit(solution)/shard_map/ppermute | solution.py:468
  6.8 21.2 %collective-permute-start.3 = (bf16[4,256,128]{2,1,0:T(8,128)(2,1)S(1)}, bf16[4,256,128]{2,1,0:T(8,128)(2,1)S(1)}, u32[]{:S(2)}, u32[]{:S(2)}) collective-permute-start(bf16[4,256,128]{2,1,0:T(8,128)(2,1)S(1)} %pad_maximum_fusion.refs_0_.refs_4_), channel_id=1, source_target_pairs={{0,2},{2,0},{4,6},{6,4},{8,10},{10,8},{12,14},{14,12},{1,3},{3,1},... | collective-permute-start | bytes 786440 | tf_op jit(solution)/shard_map/ppermute | solution.py:474
  17.7 10.3 %collective-permute-start.5 = (bf16[4,256,128]{2,1,0:T(8,128)(2,1)S(1)}, bf16[4,256,128]{2,1,0:T(8,128)(2,1)S(1)}, u32[]{:S(2)}, u32[]{:S(2)}) collective-permute-start(bf16[4,256,128]{2,1,0:T(8,128)(2,1)S(1)} %collective-permute-done.1.refs_2_.refs_6_), channel_id=1, source_target_pairs={{0,2},{2,0},{4,6},{6,4},{8,10},{10,8},{12,14},{14,12},{1,3},{3,1},... | collective-permute-start | bytes 786440 | tf_op jit(solution)/shard_map/ppermute | solution.py:474
  18.9 9.1 %collective-permute-start.4 = (bf16[4,256,128]{2,1,0:T(8,128)(2,1)S(1)}, bf16[4,256,128]{2,1,0:T(8,128)(2,1)S(1)}, u32[]{:S(2)}, u32[]{:S(2)}) collective-permute-start(bf16[4,256,128]{2,1,0:T(8,128)(2,1)S(1)} %collective-permute-done.refs_1_.refs_5_), channel_id=1, source_target_pairs={{0,2},{2,0},{4,6},{6,4},{8,10},{10,8},{12,14},{14,12},{1,3},{3,1},... | collective-permute-start | bytes 786440 | tf_op jit(solution)/shard_map/ppermute | solution.py:474
  27.9 1.5 %collective-permute-start.6 = (bf16[4,256,128]{2,1,0:T(8,128)(2,1)S(1)}, bf16[4,256,128]{2,1,0:T(8,128)(2,1)S(1)}, u32[]{:S(2)}, u32[]{:S(2)}) collective-permute-start(bf16[4,256,128]{2,1,0:T(8,128)(2,1)S(1)} %collective-permute-done.2.refs_3_.refs_7_), channel_id=1, source_target_pairs={{0,2},{2,0},{4,6},{6,4},{8,10},{10,8},{12,14},{14,12},{1,3},{3,1},... | collective-permute-start | bytes 786440 | tf_op jit(solution)/shard_map/ppermute | solution.py:474
  35.3 2.6 %collective-permute-start.7 = (bf16[2,1024,128]{2,1,0:T(8,128)(2,1)S(1)}, bf16[2,1024,128]{2,1,0:T(8,128)(2,1)S(1)}, u32[]{:S(2)}, u32[]{:S(2)}) collective-permute-start(bf16[2,1024,128]{2,1,0:T(8,128)(2,1)S(1)} %get-tuple-element.29), channel_id=1, source_target_pairs={{0,2},{2,0},{4,6},{6,4},{8,10},{10,8},{12,14},{14,12},{1,3},{3,1},... | collective-permute-start | bytes 1572872 | tf_op jit(solution)/shard_map/ppermute | solution.py:474
  38.0 12.0 %collective-permute-start.8 = (bf16[4,256,128]{2,1,0:T(8,128)(2,1)S(1)}, bf16[4,256,128]{2,1,0:T(8,128)(2,1)S(1)}, u32[]{:S(2)}, u32[]{:S(2)}) collective-permute-start(bf16[4,256,128]{2,1,0:T(8,128)(2,1)S(1)} %get-tuple-element.35), channel_id=1, source_target_pairs={{0,4},{2,6},{4,0},{6,2},{8,12},{10,14},{12,8},{14,10},{1,5},{3,7},... | collective-permute-start | bytes 786440 | tf_op jit(solution)/shard_map/ppermute | solution.py:468
  38.0 21.9 %collective-permute-start.9 = (bf16[4,256,128]{2,1,0:T(8,128)(2,1)S(1)}, bf16[4,256,128]{2,1,0:T(8,128)(2,1)S(1)}, u32[]{:S(2)}, u32[]{:S(2)}) collective-permute-start(bf16[4,256,128]{2,1,0:T(8,128)(2,1)S(1)} %get-tuple-element.36), channel_id=1, source_target_pairs={{0,8},{2,10},{4,12},{6,14},{8,0},{10,2},{12,4},{14,6},{1,9},{3,11}... | collective-permute-start | bytes 786440 | tf_op jit(solution)/shard_map/ppermute | solution.py:468
  42.0 22.7 %collective-permute-start.10 = (bf16[4,256,128]{2,1,0:T(8,128)(2,1)S(1)}, bf16[4,256,128]{2,1,0:T(8,128)(2,1)S(1)}, u32[]{:S(2)}, u32[]{:S(2)}) collective-permute-start(bf16[4,256,128]{2,1,0:T(8,128)(2,1)S(1)} %get-tuple-element.37), channel_id=1, source_target_pairs={{0,12},{2,14},{4,8},{6,10},{8,4},{10,6},{12,0},{14,2},{1,13},{3,15... | collective-permute-start | bytes 786440 | tf_op jit(solution)/shard_map/ppermute | solution.py:468

commit v3 on v0

--- a/solution.py
+++ b/solution.py
@@ -1,6 +1,10 @@
+import functools
+
 import jax
 import jax.numpy as jnp
 from jax import lax
+from jax.experimental import pallas as pl
+from jax.experimental.pallas import tpu as pltpu
 from jax.sharding import PartitionSpec as P
 
 HD = 128
@@ -122,7 +126,7 @@
     return (query_part_grad, grad_term)
 
 
-def shards(query_rows, key_rows, value_rows, grad_output, dilation_offsets):
+def shards_levels(query_rows, key_rows, value_rows, grad_output, dilation_offsets):
     row_count = query_rows.shape[0]
     head_count = query_rows.shape[1] // HD
     level_count = dilation_offsets.shape[0]
@@ -236,6 +240,326 @@
     )
 
 
+NT = (((1,), (1,)), ((), ()))
+TN = (((0,), (0,)), ((), ()))
+MIB = 2**20
+FORWARD_ROWS = 128
+BACKWARD_ROWS = 256
+SCORE_SCALE = HD ** (-0.5)
+EXP_SCALE = SCORE_SCALE * 1.4426950408889634
+
+
+def vmem_specs(count):
+    return [pl.BlockSpec(memory_space=pltpu.VMEM)] * count
+
+
+def any_specs(count):
+    return [pl.BlockSpec(memory_space=pl.ANY)] * count
+
+
+def head_columns(chip, offset):
+    return pl.ds(pl.multiple_of((chip ^ offset) * HD, HD), HD)
+
+
+def pack(chip, arrays, offset):
+    start = (chip[0] ^ offset) * HD
+    return jnp.stack([lax.dynamic_slice_in_dim(array, start, HD, axis=1) for array in arrays])
+
+
+def unpack_kernel(layout, chip_ref, *refs):
+    count = max(max(arrays) for _, arrays in layout) + 1
+    blocks, outs, sems = refs[: len(layout)], refs[len(layout) : -1], refs[-1]
+    chip = chip_ref[0]
+    copies = []
+    for at, (offset, arrays) in enumerate(layout):
+        for place, index in enumerate(arrays):
+            copies.append(
+                pltpu.make_async_copy(
+                    blocks[at].at[place],
+                    outs[index].at[:, head_columns(chip, offset)],
+                    sems.at[at, place],
+                )
+            )
+    for copy in copies:
+        copy.start()
+    for copy in copies:
+        copy.wait()
+
+
+def unpack(chip, blocks, layout, width):
+    count = max(max(arrays) for _, arrays in layout) + 1
+    rows = blocks[0].shape[1]
+    return pl.pallas_call(
+        functools.partial(unpack_kernel, layout),
+        out_shape=[jax.ShapeDtypeStruct((rows, width), blocks[0].dtype)] * count,
+        in_specs=[pl.BlockSpec(memory_space=pltpu.SMEM)] + any_specs(len(blocks)),
+        out_specs=any_specs(count),
+        scratch_shapes=[pltpu.SemaphoreType.DMA((len(layout), count))],
+        compiler_params=pltpu.CompilerParams(vmem_limit_bytes=MIB),
+        name="unpack",
+    )(chip, *blocks)
+
+
+def load_keys(blocks, key_ref, value_ref):
+    rows = blocks[0].shape[1]
+    for index, block in enumerate(blocks):
+        key_ref[index * rows : (index + 1) * rows] = block[0]
+        value_ref[index * rows : (index + 1) * rows, :HD] = block[1]
+    if value_ref.shape[1] > HD:
+        value_ref[:, HD:] = jnp.ones((value_ref.shape[0], HD), value_ref.dtype)
+
+
+def forward_rows(query, key_all, value_ones):
+    scores = lax.dot_general(query, key_all, NT, preferred_element_type=jnp.float32)
+    row_peak = jnp.max(scores, axis=1, keepdims=True)
+    probs = jnp.exp2(scores * EXP_SCALE - row_peak * EXP_SCALE).astype(jnp.bfloat16)
+    sums = jnp.dot(probs, value_ones, preferred_element_type=jnp.float32)
+    row_scale = 1.0 / sums[:, HD:]
+    return probs, row_scale, (sums[:, :HD] * row_scale).astype(jnp.bfloat16)
+
+
+def query_pair(block, part):
+    first = block.shape[0] - 2
+    return block[first, part], block[first + 1, part]
+
+
+def scaled_grad(grad, row_scale, attended):
+    grad = (grad.astype(jnp.float32) * row_scale).astype(jnp.bfloat16)
+    products = attended.astype(jnp.float32) * grad.astype(jnp.float32)
+    return grad, jnp.sum(products, axis=1, keepdims=True)
+
+
+def backward_rows(query, grad, delta, probs, key_part, value_part):
+    dprobs = lax.dot_general(grad, value_part, NT, preferred_element_type=jnp.float32)
+    dscore = (probs.astype(jnp.float32) * (dprobs - delta)).astype(jnp.bfloat16)
+    return (
+        jnp.dot(dscore, key_part, preferred_element_type=jnp.float32),
+        lax.dot_general(dscore, query, TN, preferred_element_type=jnp.float32),
+        lax.dot_general(probs, grad, TN, preferred_element_type=jnp.float32),
+    )
+
+
+def forward_pass(query_blocks, outs, key_ref, value_ref, probs_ref, scale_ref):
+    rows = outs[0].shape[1]
+    step = min(FORWARD_ROWS, rows)
+    key_all = key_ref[...]
+    value_ones = value_ref[...]
+    for index, block in enumerate(query_blocks):
+        for start in range(0, rows, step):
+            part = slice(start, start + step)
+            here = slice(index * rows + start, index * rows + start + step)
+            probs, row_scale, attended = forward_rows(
+                query_pair(block, part)[0], key_all, value_ones
+            )
+            probs_ref[here] = probs
+            scale_ref[here] = row_scale
+            outs[index][0, part] = attended
+
+
+def row_parts(query_blocks, rows):
+    step = min(BACKWARD_ROWS, rows)
+    for index in range(len(query_blocks)):
+        for start in range(0, rows, step):
+            first = index * rows + start
+            yield index, slice(start, start + step), slice(first, first + step)
+
+
+def near_kernel(chips, near, *refs):
+    pair_blocks, refs = refs[: 2 * chips], refs[2 * chips :]
+    outs, query_outs, refs = refs[:near], refs[near : 2 * near], refs[2 * near :]
+    terms_ref, key_ref, value_ref, probs_ref, scale_ref = refs
+    query_blocks = pair_blocks[:near]
+    rows = outs[0].shape[1]
+    load_keys(pair_blocks, key_ref, value_ref)
+    forward_pass(query_blocks, outs, key_ref, value_ref, probs_ref, scale_ref)
+    for index, part, here in row_parts(query_blocks, rows):
+        query, grad = query_pair(query_blocks[index], part)
+        grad, delta = scaled_grad(
+            grad, scale_ref[here], outs[index][0, part]
+        )
+        dquery, dkey, dvalue = backward_rows(
+            query, grad, delta, probs_ref[here], key_ref[...], value_ref[:, :HD]
+        )
+        query_outs[index][0, part] = (dquery * SCORE_SCALE).astype(jnp.bfloat16)
+        if here.start == 0:
+            terms_ref[0] = dkey
+            terms_ref[1] = dvalue
+        else:
+            terms_ref[0] += dkey
+            terms_ref[1] += dvalue
+
+
+def far_kernel(chips, far, *refs):
+    pair_blocks, query_blocks, refs = refs[: 2 * chips], refs[2 * chips :][:far], refs[2 * chips + far :]
+    near_ref, outs, refs = refs[0], refs[1 : 1 + far], refs[1 + far :]
+    probs_out, scale_ref, query_terms, other_ref = refs[:4]
+    key_ref, value_ref, probs_ref, terms_ref = refs[4:]
+    rows = outs[0].shape[1]
+    half = chips * rows
+    load_keys(pair_blocks, key_ref, value_ref)
+    forward_pass(query_blocks, outs, key_ref, value_ref, probs_ref, scale_ref)
+    terms_ref[...] = near_ref[:, half:]
+    for index, part, here in row_parts(query_blocks, rows):
+        query, grad = query_pair(query_blocks[index], part)
+        grad, delta = scaled_grad(
+            grad, scale_ref[here], outs[index][0, part]
+        )
+        probs_out[here] = probs_ref[here, :half]
+        dquery, dkey, dvalue = backward_rows(
+            query, grad, delta, probs_ref[here, half:], key_ref[half:], value_ref[half:, :HD]
+        )
+        query_terms[here] = dquery
+        terms_ref[0] += dkey
+        terms_ref[1] += dvalue
+    other_ref[0] = (terms_ref[0] * SCORE_SCALE).astype(other_ref.dtype)
+    other_ref[1] = terms_ref[1].astype(other_ref.dtype)
+
+
+def own_kernel(chips, far, *refs):
+    pair_blocks, query_blocks, refs = refs[:chips], refs[chips:][:far], refs[chips + far :]
+    attended, refs = refs[:far], refs[far:]
+    near_ref, probs_ref, scale_ref, query_terms = refs[:4]
+    query_outs, refs = refs[4 : 4 + far], refs[4 + far :]
+    own_ref, key_ref, value_ref = refs
+    rows = attended[0].shape[1]
+    half = chips * rows
+    load_keys(pair_blocks, key_ref, value_ref)
+    own_ref[...] = near_ref[:, :half]
+    for index, part, here in row_parts(query_blocks, rows):
+        query, grad = query_pair(query_blocks[index], part)
+        grad, delta = scaled_grad(
+            grad, scale_ref[here], attended[index][0, part]
+        )
+        dquery, dkey, dvalue = backward_rows(
+            query, grad, delta, probs_ref[here], key_ref[...], value_ref[...]
+        )
+        dquery = (dquery + query_terms[here]) * SCORE_SCALE
+        query_outs[index][0, part] = dquery.astype(jnp.bfloat16)
+        own_ref[0] += dkey
+        own_ref[1] += dvalue
+    own_ref[0] *= SCORE_SCALE
+
+
+def call_vmem(kernel, name, operands, outs, scratch, products, limit):
+    return pl.pallas_call(
+        kernel,
+        out_shape=[jax.ShapeDtypeStruct(shape, dtype) for shape, dtype in outs],
+        in_specs=vmem_specs(len(operands)),
+        out_specs=vmem_specs(len(outs)),
+        scratch_shapes=[pltpu.VMEM(shape, dtype) for shape, dtype in scratch],
+        compiler_params=pltpu.CompilerParams(vmem_limit_bytes=limit),
+        cost_estimate=pl.CostEstimate(flops=2 * products, bytes_accessed=MIB, transcendentals=0),
+        name=name,
+    )(*operands)
+
+
+def add_kernel(chips, own_ref, other_ref, *refs):
+    query_blocks, attended, outs = refs[:chips], refs[chips : 2 * chips], refs[2 * chips :]
+    rows = outs[0].shape[1]
+    for index, out in enumerate(outs):
+        part = slice(index * rows, (index + 1) * rows)
+        total = own_ref[:, part] + other_ref[:, part].astype(jnp.float32)
+        out[0] = attended[index][0]
+        out[1] = query_blocks[index][0]
+        out[2:4] = total.astype(jnp.bfloat16)
+
+
+def to_chip(array, offset):
+    return lax.ppermute(
+        array, "seq", [(i, i ^ (2 * offset)) for i in range(lax.axis_size("seq"))]
+    )
+
+
+def to_core(array):
+    return lax.ppermute(array, "seq", [(i, i ^ 1) for i in range(lax.axis_size("seq"))])
+
+
+def after(array, other):
+    return lax.optimization_barrier((array, other))[0]
+
+
+def shards_one_level(query_rows, key_rows, value_rows, grad_output):
+    bf16, f32 = jnp.bfloat16, jnp.float32
+    chips = lax.axis_size("seq") // 2
+    near = 2
+    far = chips - near
+    rows = query_rows.shape[0]
+    half, keys = chips * rows, 2 * chips * rows
+    chip = (lax.axis_index("seq") // 2).reshape(1)
+    pairs = [key_rows, value_rows]
+    queries = [query_rows, grad_output]
+    wanted = [(offset, pairs) for offset in range(near, chips)]
+    wanted += [(1, pairs + queries), (0, pairs + queries)]
+    wanted += [(offset, queries) for offset in range(near, chips)]
+    packed = []
+    for offset, arrays in wanted:
+        packed.append(pack(chip, arrays, offset))
+        chip = after(chip, packed[-1])
+    moved = [to_chip(block, offset) if offset else block for block, (offset, _) in zip(packed, wanted)]
+    pair_blocks = [moved[far + 1], moved[far]] + moved[:far]
+    query_blocks = moved[far + 2 :]
+    all_blocks = pair_blocks + [to_core(block) for block in pair_blocks]
+    block = ((1, rows, HD), bf16)
+    product = near * rows * keys * HD
+    *outs, terms = call_vmem(
+        functools.partial(near_kernel, chips, near),
+        "near",
+        all_blocks,
+        [block] * (2 * near) + [((2, keys, HD), f32)],
+        [((keys, HD), bf16), ((keys, 2 * HD), bf16), ((near * rows, keys), bf16), ((near * rows, HD), f32)],
+        6 * product,
+        24 * MIB,
+    )
+    attended, query_grads = outs[:near], outs[near:]
+    product = far * rows * half * HD
+    *outs, probs, scale, query_terms, other = call_vmem(
+        functools.partial(far_kernel, chips, far),
+        "far",
+        all_blocks + query_blocks + [terms],
+        [block] * far
+        + [((far * rows, half), bf16), ((far * rows, HD), f32), ((far * rows, HD), f32), ((2, half, HD), bf16)],
+        [((keys, HD), bf16), ((keys, 2 * HD), bf16), ((far * rows, keys), bf16), ((2, half, HD), f32)],
+        8 * product,
+        24 * MIB,
+    )
+    other = to_core(other)
+    attended = attended + outs
+    *outs, own = call_vmem(
+        functools.partial(own_kernel, chips, far),
+        "own",
+        pair_blocks + query_blocks + outs + [terms, probs, scale, query_terms],
+        [block] * far + [((2, half, HD), f32)],
+        [((half, HD), bf16), ((half, HD), bf16)],
+        4 * product,
+        16 * MIB,
+    )
+    query_grads = query_grads + outs
+    outs = call_vmem(
+        functools.partial(add_kernel, chips),
+        "add_partials",
+        [own, other] + query_grads + attended,
+        [((4, rows, HD), bf16)] * chips,
+        [],
+        rows,
+        8 * MIB,
+    )
+    order = list(range(near, chips)) + [1]
+    returned = [outs[0]] + [to_chip(outs[offset], offset) for offset in order]
+    layout = [(offset, (0, 1, 2, 3)) for offset in [0] + order]
+    return tuple(unpack(chip, returned, layout, query_rows.shape[1]))
+
+
+def shards(query_rows, key_rows, value_rows, grad_output, dilation_offsets):
+    seq_width = lax.axis_size("seq")
+    if (
+        dilation_offsets.shape[0] == 1
+        and query_rows.shape[0] * seq_width == SEG
+        and query_rows.shape[1] // HD * 2 == seq_width
+    ):
+        return shards_one_level(query_rows, key_rows, value_rows, grad_output)
+    return shards_levels(query_rows, key_rows, value_rows, grad_output, dilation_offsets)
+
+
 def solution(mesh):
     in_specs = (
         P(("groups", "seq"), "head"),

time: 180 us -> 61.6 us (0.34)
  the two profiles are of different devices: /device:TPU:0 before, /device:TPU:12 now
where the time goes in v3:
time: 61.6 us; the launch traced here: 60.8 us
  waiting for transfers between devices  29.9 us (49%)
  starting transfers between devices  13.2 us (21%)
  Pallas kernels  9.68 us (16%)
  local copies, waits for them, and re-layouts  6.97 us (11%)
  between operations  0.83 us (1%)
    ppermute x8, waiting for transfers between devices, to_chip(): lax.ppermute(array, 'seq', [(i, i ^ 2 * offset) for i in range(lax.axis_s...  28.5 us
    ppermute x8, starting transfers between devices, to_chip(): lax.ppermute(array, 'seq', [(i, i ^ 2 * offset) for i in range(lax.axis_s...  12.4 us
    pallas_call x4, Pallas kernels, call_vmem(): pl.pallas_call(kernel, out_shape=[jax.ShapeDtypeStruct(shape, dtype) for...  8.59 us
    another operation x15, local copies, waits for them, and re-layouts, pack(): jnp.stack([lax.dynamic_slice_in_dim(array, start, HD, axis=1) for array i...  6.96 us
    ppermute x5, waiting for transfers between devices, to_core(): lax.ppermute(array, 'seq', [(i, i ^ 1) for i in range(lax.axis_size('seq'...  1.39 us
  transfers between devices with their start and end apart: 13, of which 6 were waited for; matrix products, arithmetic and copies ran while one was open for 10% of the time, Pallas kernels for 9%

profile of v3, /device:TPU:12, one launch (start us, length us, event | category | flops | bytes accessed | tf_op | source)
XLA Modules:
  0.0 60.8 jit_solution(15519110539546889093)
XLA Ops:
  0.7 0.9 %dynamic-slice_bitcast_fusion.14 = (bf16[1,256,128]{2,1,0:T(8,128)(2,1)S(1)}, bf16[1,256,128]{2,1,0:T(8,128)(2,1)S(1)}) fusion(bf16[256,512]{1,0:T(8,128)(2,1)} %param.7, s32[]{:T(128)S(6)} %select_n.34, bf16[256,512]{1,0:T(8,128)(2,1)} %param.6), kind=kLoop, calls=%fused_computation.20 | loop fusion | bytes 262148 | tf_op jit(solution)/shard_map/stack | solution.py:266
  1.6 2.7 %collective-permute-start.1 = (bf16[2,256,128]{2,1,0:T(8,128)(2,1)S(1)}, bf16[2,256,128]{2,1,0:T(8,128)(2,1)S(1)}, u32[]{:S(2)}, u32[]{:S(2)}) collective-permute-start(bf16[2,256,128]{2,1,0:T(8,128)(2,1)S(1)} %pad_maximum_fusion.2), channel_id=1, source_target_pairs={{0,8},{2,10},{4,12},{6,14},{8,0},{10,2},{12,4},{14,6},{1,9},{3,11}... | collective-permute-start | bytes 393224 | tf_op jit(solution)/shard_map/ppermute | solution.py:468
  4.3 0.8 %dynamic-slice_bitcast_fusion.12 = bf16[1,256,128]{2,1,0:T(8,128)(2,1)S(1)} fusion(bf16[256,512]{1,0:T(8,128)(2,1)} %param.7, s32[]{:T(128)S(6)} %select_n.35), kind=kLoop, calls=%fused_computation.18 | loop fusion | bytes 131076 | tf_op jit(solution)/shard_map/stack | solution.py:266
  5.1 0.8 %dynamic-slice_bitcast_fusion.13 = bf16[1,256,128]{2,1,0:T(8,128)(2,1)S(1)} fusion(bf16[256,512]{1,0:T(8,128)(2,1)} %param.6, s32[]{:T(128)S(6)} %select_n.35), kind=kLoop, calls=%fused_computation.19 | loop fusion | bytes 131076 | tf_op jit(solution)/shard_map/stack | solution.py:266
  6.1 0.8 %dynamic-slice_bitcast_fusion.10 = bf16[1,256,128]{2,1,0:T(8,128)(2,1)S(1)} fusion(bf16[256,512]{1,0:T(8,128)(2,1)} %param.7, s32[]{:T(128)S(6)} %select_n.36), kind=kLoop, calls=%fused_computation.16 | loop fusion | bytes 131076 | tf_op jit(solution)/shard_map/stack | solution.py:266
  6.9 0.8 %dynamic-slice_bitcast_fusion.11 = bf16[1,256,128]{2,1,0:T(8,128)(2,1)S(1)} fusion(bf16[256,512]{1,0:T(8,128)(2,1)} %param.6, s32[]{:T(128)S(6)} %select_n.36), kind=kLoop, calls=%fused_computation.17 | loop fusion | bytes 131076 | tf_op jit(solution)/shard_map/stack | solution.py:266
  7.8 0.9 %dynamic-slice_bitcast_fusion.9 = bf16[1,256,128]{2,1,0:T(8,128)(2,1)S(1)} fusion(bf16[256,512]{1,0:T(8,128)(2,1)} %param.5, s32[]{:T(128)S(6)} %select_n.36), kind=kLoop, calls=%fused_computation.15 | loop fusion | bytes 131076 | tf_op jit(solution)/shard_map/stack | solution.py:266
  8.7 1.8 %collective-permute-start = (bf16[4,256,128]{2,1,0:T(8,128)(2,1)S(1)}, bf16[4,256,128]{2,1,0:T(8,128)(2,1)S(1)}, u32[]{:S(2)}, u32[]{:S(2)}) collective-permute-start(bf16[4,256,128]{2,1,0:T(8,128)(2,1)S(1)} %pad_maximum_fusion), channel_id=1, source_target_pairs={{0,4},{2,6},{4,0},{6,2},{8,12},{10,14},{12,8},{14,10},{1,5},{3,7},... | collective-permute-start | bytes 786440 | tf_op jit(solution)/shard_map/ppermute | solution.py:468
  10.6 0.9 %dynamic-slice_bitcast_fusion.6 = bf16[1,256,128]{2,1,0:T(8,128)(2,1)S(1)} fusion(bf16[256,512]{1,0:T(8,128)(2,1)} %param.7, s32[]{:T(128)S(6)} %select_n.37), kind=kLoop, calls=%fused_computation.12 | loop fusion | bytes 131076 | tf_op jit(solution)/shard_map/stack | solution.py:266
  11.4 0.8 %dynamic-slice_bitcast_fusion.7 = bf16[1,256,128]{2,1,0:T(8,128)(2,1)S(1)} fusion(bf16[256,512]{1,0:T(8,128)(2,1)} %param.6, s32[]{:T(128)S(6)} %select_n.37), kind=kLoop, calls=%fused_computation.13 | loop fusion | bytes 131076 | tf_op jit(solution)/shard_map/stack | solution.py:266
  12.5 1.8 %collective-permute-start.3 = (bf16[2,256,128]{2,1,0:T(8,128)(2,1)S(1)}, bf16[2,256,128]{2,1,0:T(8,128)(2,1)S(1)}, u32[]{:S(2)}, u32[]{:S(2)}) collective-permute-start(bf16[2,256,128]{2,1,0:T(8,128)(2,1)S(1)} %pad_maximum_fusion.4), channel_id=1, source_target_pairs={{0,8},{2,10},{4,12},{6,14},{8,0},{10,2},{12,4},{14,6},{1,9},{3,11}... | collective-permute-start | bytes 393224 | tf_op jit(solution)/shard_map/ppermute | solution.py:468
  14.2 5.4 %collective-permute-done.refs_1_ = bf16[4,256,128]{2,1,0:T(8,128)(2,1)S(1)} collective-permute-done((bf16[4,256,128]{2,1,0:T(8,128)(2,1)S(1)}, bf16[4,256,128]{2,1,0:T(8,128)(2,1)S(1)}, u32[]{:S(2)}, u32[]{:S(2)}) %collective-permute-start) | collective-permute-done | bytes 262176 | tf_op jit(solution)/shard_map/ppermute | solution.py:468
  19.7 0.6 collective-permute-start.8
  20.4 1.0 %collective-permute-done.8.refs_7_ = bf16[2,256,128]{2,1,0:T(8,128)(2,1)S(1)} collective-permute-done((bf16[2,256,128]{2,1,0:T(8,128)(2,1)S(1)}, bf16[2,256,128]{2,1,0:T(8,128)(2,1)S(1)}, u32[]{:S(2)}, u32[]{:S(2)}) %collective-permute-start.8) | collective-permute-done | bytes 131104 | tf_op jit(solution)/shard_map/ppermute | solution.py:474
  21.7 4.0 %near.1 = (bf16[1,256,128]{2,1,0:T(8,128)(2,1)S(1)}, bf16[1,256,128]{2,1,0:T(8,128)(2,1)S(1)}, bf16[1,256,128]{2,1,0:T(8,128)(2,1)S(1)}, bf16[1,256,128]{2,1,0:T(8,128)(2,1)S(1)}, f32[2,2048,128]{2,1,0:T(8,128)S(1)}) custom-call(bf16[4,256,128]{2,1,0:T(8,128)(2,1)S(1)} %pad_maximum_fusion.1.refs_0_, bf16[4,256,128]{2,1,0:T(8,128)(2,1)S(1)} %collective-permute-done.refs_1_, ...), custom_call_target="tpu_custom_call" | custom-call | flops 1610612736 | bytes 1048576 | tf_op jit(solution)/shard_map/near/pallas_call | solution.py:444
  25.6 1.3 %collective-permute-done.4.refs_9_.refs_5_ = bf16[2,256,128]{2,1,0:T(8,128)(2,1)S(1)} collective-permute-done((bf16[2,256,128]{2,1,0:T(8,128)(2,1)S(1)}, bf16[2,256,128]{2,1,0:T(8,128)(2,1)S(1)}, u32[]{:S(2)}, u32[]{:S(2)}) %collective-permute-start.4) | collective-permute-done | bytes 131104 | tf_op jit(solution)/shard_map/ppermute | solution.py:468
  27.0 3.0 %far.1 = (bf16[1,256,128]{2,1,0:T(8,128)(2,1)S(1)}, bf16[1,256,128]{2,1,0:T(8,128)(2,1)S(1)}, bf16[512,1024]{1,0:T(8,128)(2,1)S(1)}, f32[512,128]{1,0:T(8,128)S(...) custom-call(bf16[4,256,128]{2,1,0:T(8,128)(2,1)S(1)} %pad_maximum_fusion.1.refs_0_, ...), custom_call_target="tpu_custom_call" | custom-call | flops 1073741824 | bytes 1048576 | tf_op jit(solution)/shard_map/far/pallas_call | solution.py:444
  30.1 1.5 %own.1 = (bf16[1,256,128]{2,1,0:T(8,128)(2,1)S(1)}, bf16[1,256,128]{2,1,0:T(8,128)(2,1)S(1)}, f32[2,1024,128]{2,1,0:T(8,128)S(1)}) custom-call(bf16[4,256,128]{2,1,0:T(8,128)(2,1)S(1)} %pad_maximum_fusion.1.refs_0_, bf16[4,256,128]{2,1,0:T(8,128)(2,1)S(1)} %collective-permute-done.refs_1_, bf16[2,256,128]{2,1,0:T(8,128)(2,1)S(1)} %collective-permute-done.1.refs_2_, ...), custom_call_target="tpu_custom_call" | custom-call | flops 536870912 | bytes 1048576 | tf_op jit(solution)/shard_map/own/pallas_call | solution.py:444
  31.6 0.4 collective-permute-done.9.other_ref
  32.1 4.1 %collective-permute-start.10 = (bf16[4,256,128]{2,1,0:T(8,128)(2,1)S(1)}, bf16[4,256,128]{2,1,0:T(8,128)(2,1)S(1)}, u32[]{:S(2)}, u32[]{:S(2)}) collective-permute-start(bf16[4,256,128]{2,1,0:T(8,128)(2,1)S(1)} %get-tuple-element.49), channel_id=1, source_target_pairs={{0,8},{2,10},{4,12},{6,14},{8,0},{10,2},{12,4},{14,6},{1,9},{3,11}... | collective-permute-start | bytes 786440 | tf_op jit(solution)/shard_map/ppermute | solution.py:468
  36.2 1.7 %collective-permute-start.11 = (bf16[4,256,128]{2,1,0:T(8,128)(2,1)S(1)}, bf16[4,256,128]{2,1,0:T(8,128)(2,1)S(1)}, u32[]{:S(2)}, u32[]{:S(2)}) collective-permute-start(bf16[4,256,128]{2,1,0:T(8,128)(2,1)S(1)} %get-tuple-element.50), channel_id=1, source_target_pairs={{0,12},{2,14},{4,8},{6,10},{8,4},{10,6},{12,0},{14,2},{1,13},{3,15... | collective-permute-start | bytes 786440 | tf_op jit(solution)/shard_map/ppermute | solution.py:468
  37.9 15.5 %collective-permute-done.10.refs_1_ = bf16[4,256,128]{2,1,0:T(8,128)(2,1)S(1)} collective-permute-done((bf16[4,256,128]{2,1,0:T(8,128)(2,1)S(1)}, bf16[4,256,128]{2,1,0:T(8,128)(2,1)S(1)}, u32[]{:S(2)}, u32[]{:S(2)}) %collective-permute-start.10) | collective-permute-done | bytes 262176 | tf_op jit(solution)/shard_map/ppermute | solution.py:468
  53.4 6.3 %collective-permute-done.11.refs_2_ = bf16[4,256,128]{2,1,0:T(8,128)(2,1)S(1)} collective-permute-done((bf16[4,256,128]{2,1,0:T(8,128)(2,1)S(1)}, bf16[4,256,128]{2,1,0:T(8,128)(2,1)S(1)}, u32[]{:S(2)}, u32[]{:S(2)}) %collective-permute-start.11) | collective-permute-done | bytes 262176 | tf_op jit(solution)/shard_map/ppermute | solution.py:468
  59.7 1.1 %unpack.1 = (bf16[256,512]{1,0:T(8,128)(2,1)}, bf16[256,512]{1,0:T(8,128)(2,1)}, bf16[256,512]{1,0:T(8,128)(2,1)}, bf16[256,512]{1,0:T(8,128)(2,1)}) custom-call(s32[1]{0:T(128)} %bitcast.chip_ref, bf16[4,256,128]{2,1,0:T(8,128)(2,1)S(1)} %get-tuple-element.48.refs_0_, bf16[4,256,128]{2,1,0:T(8,128)(2,1)S(1)} %collective-permute-done.10.refs_1_, ...), custom_call_target="tpu_custom_call" | custom-call | tf_op jit(solution)/shard_map/unpack/pallas_call | solution.py:292
  (32 shorter events, 1.0 us)
Async XLA Ops:
  0.6 7.2 %copy-start = (bf16[256,512]{1,0:T(8,128)(2,1)S(1)}, bf16[256,512]{1,0:T(8,128)(2,1)}, u32[]{:S(2)}) copy-start(bf16[256,512]{1,0:T(8,128)(2,1)} %param.8) | copy-start | bytes 786436
  0.6 9.9 %copy-start.1 = (bf16[256,512]{1,0:T(8,128)(2,1)S(1)}, bf16[256,512]{1,0:T(8,128)(2,1)}, u32[]{:S(2)}) copy-start(bf16[256,512]{1,0:T(8,128)(2,1)} %param.5) | copy-start | bytes 786436
  1.6 18.6 %collective-permute-start.1 = (bf16[2,256,128]{2,1,0:T(8,128)(2,1)S(1)}, bf16[2,256,128]{2,1,0:T(8,128)(2,1)S(1)}, u32[]{:S(2)}, u32[]{:S(2)}) collective-permute-start(bf16[2,256,128]{2,1,0:T(8,128)(2,1)S(1)} %pad_maximum_fusion.2), channel_id=1, source_target_pairs={{0,8},{2,10},{4,12},{6,14},{8,0},{10,2},{12,4},{14,6},{1,9},{3,11}... | collective-permute-start | bytes 393224 | tf_op jit(solution)/shard_map/ppermute | solution.py:468
  6.0 13.7 %collective-permute-start.2 = (bf16[2,256,128]{2,1,0:T(8,128)(2,1)S(1)}, bf16[2,256,128]{2,1,0:T(8,128)(2,1)S(1)}, u32[]{:S(2)}, u32[]{:S(2)}) collective-permute-start(bf16[2,256,128]{2,1,0:T(8,128)(2,1)S(1)} %pad_maximum_fusion.3), channel_id=1, source_target_pairs={{0,12},{2,14},{4,8},{6,10},{8,4},{10,6},{12,0},{14,2},{1,13},{3,15... | collective-permute-start | bytes 393224 | tf_op jit(solution)/shard_map/ppermute | solution.py:468
  8.7 10.9 %collective-permute-start = (bf16[4,256,128]{2,1,0:T(8,128)(2,1)S(1)}, bf16[4,256,128]{2,1,0:T(8,128)(2,1)S(1)}, u32[]{:S(2)}, u32[]{:S(2)}) collective-permute-start(bf16[4,256,128]{2,1,0:T(8,128)(2,1)S(1)} %pad_maximum_fusion), channel_id=1, source_target_pairs={{0,4},{2,6},{4,0},{6,2},{8,12},{10,14},{12,8},{14,10},{1,5},{3,7},... | collective-permute-start | bytes 786440 | tf_op jit(solution)/shard_map/ppermute | solution.py:468
  12.3 9.4 %collective-permute-start.5 = (bf16[4,256,128]{2,1,0:T(8,128)(2,1)S(1)}, bf16[4,256,128]{2,1,0:T(8,128)(2,1)S(1)}, u32[]{:S(2)}, u32[]{:S(2)}) collective-permute-start(bf16[4,256,128]{2,1,0:T(8,128)(2,1)S(1)} %pad_maximum_fusion.1.refs_0_), channel_id=1, source_target_pairs={{0,2},{2,0},{4,6},{6,4},{8,10},{10,8},{12,14},{14,12},{1,3},{3,1},... | collective-permute-start | bytes 786440 | tf_op jit(solution)/shard_map/ppermute | solution.py:474
  12.5 14.5 %collective-permute-start.3 = (bf16[2,256,128]{2,1,0:T(8,128)(2,1)S(1)}, bf16[2,256,128]{2,1,0:T(8,128)(2,1)S(1)}, u32[]{:S(2)}, u32[]{:S(2)}) collective-permute-start(bf16[2,256,128]{2,1,0:T(8,128)(2,1)S(1)} %pad_maximum_fusion.4), channel_id=1, source_target_pairs={{0,8},{2,10},{4,12},{6,14},{8,0},{10,2},{12,4},{14,6},{1,9},{3,11}... | collective-permute-start | bytes 393224 | tf_op jit(solution)/shard_map/ppermute | solution.py:468
  19.6 2.0 %collective-permute-start.6 = (bf16[4,256,128]{2,1,0:T(8,128)(2,1)S(1)}, bf16[4,256,128]{2,1,0:T(8,128)(2,1)S(1)}, u32[]{:S(2)}, u32[]{:S(2)}) collective-permute-start(bf16[4,256,128]{2,1,0:T(8,128)(2,1)S(1)} %collective-permute-done.refs_1_), channel_id=1, source_target_pairs={{0,2},{2,0},{4,6},{6,4},{8,10},{10,8},{12,14},{14,12},{1,3},{3,1},... | collective-permute-start | bytes 786440 | tf_op jit(solution)/shard_map/ppermute | solution.py:474
  19.7 1.7 %collective-permute-start.8 = (bf16[2,256,128]{2,1,0:T(8,128)(2,1)S(1)}, bf16[2,256,128]{2,1,0:T(8,128)(2,1)S(1)}, u32[]{:S(2)}, u32[]{:S(2)}) collective-permute-start(bf16[2,256,128]{2,1,0:T(8,128)(2,1)S(1)} %collective-permute-done.2.refs_3_), channel_id=1, source_target_pairs={{0,2},{2,0},{4,6},{6,4},{8,10},{10,8},{12,14},{14,12},{1,3},{3,1},... | collective-permute-start | bytes 393224 | tf_op jit(solution)/shard_map/ppermute | solution.py:474
  20.2 1.4 %collective-permute-start.7 = (bf16[2,256,128]{2,1,0:T(8,128)(2,1)S(1)}, bf16[2,256,128]{2,1,0:T(8,128)(2,1)S(1)}, u32[]{:S(2)}, u32[]{:S(2)}) collective-permute-start(bf16[2,256,128]{2,1,0:T(8,128)(2,1)S(1)} %collective-permute-done.1.refs_2_), channel_id=1, source_target_pairs={{0,2},{2,0},{4,6},{6,4},{8,10},{10,8},{12,14},{14,12},{1,3},{3,1},... | collective-permute-start | bytes 393224 | tf_op jit(solution)/shard_map/ppermute | solution.py:474
  21.4 5.6 %collective-permute-start.4 = (bf16[2,256,128]{2,1,0:T(8,128)(2,1)S(1)}, bf16[2,256,128]{2,1,0:T(8,128)(2,1)S(1)}, u32[]{:S(2)}, u32[]{:S(2)}) collective-permute-start(bf16[2,256,128]{2,1,0:T(8,128)(2,1)S(1)} %pad_maximum_fusion.5), channel_id=1, source_target_pairs={{0,12},{2,14},{4,8},{6,10},{8,4},{10,6},{12,0},{14,2},{1,13},{3,15... | collective-permute-start | bytes 393224 | tf_op jit(solution)/shard_map/ppermute | solution.py:468
  30.0 2.0 %collective-permute-start.9 = (bf16[2,1024,128]{2,1,0:T(8,128)(2,1)S(1)}, bf16[2,1024,128]{2,1,0:T(8,128)(2,1)S(1)}, u32[]{:S(2)}, u32[]{:S(2)}) collective-permute-start(bf16[2,1024,128]{2,1,0:T(8,128)(2,1)S(1)} %get-tuple-element.41), channel_id=1, source_target_pairs={{0,2},{2,0},{4,6},{6,4},{8,10},{10,8},{12,14},{14,12},{1,3},{3,1},... | collective-permute-start | bytes 1572872 | tf_op jit(solution)/shard_map/ppermute | solution.py:474
  32.1 21.3 %collective-permute-start.10 = (bf16[4,256,128]{2,1,0:T(8,128)(2,1)S(1)}, bf16[4,256,128]{2,1,0:T(8,128)(2,1)S(1)}, u32[]{:S(2)}, u32[]{:S(2)}) collective-permute-start(bf16[4,256,128]{2,1,0:T(8,128)(2,1)S(1)} %get-tuple-element.49), channel_id=1, source_target_pairs={{0,8},{2,10},{4,12},{6,14},{8,0},{10,2},{12,4},{14,6},{1,9},{3,11}... | collective-permute-start | bytes 786440 | tf_op jit(solution)/shard_map/ppermute | solution.py:468
  36.2 23.5 %collective-permute-start.11 = (bf16[4,256,128]{2,1,0:T(8,128)(2,1)S(1)}, bf16[4,256,128]{2,1,0:T(8,128)(2,1)S(1)}, u32[]{:S(2)}, u32[]{:S(2)}) collective-permute-start(bf16[4,256,128]{2,1,0:T(8,128)(2,1)S(1)} %get-tuple-element.50), channel_id=1, source_target_pairs={{0,12},{2,14},{4,8},{6,10},{8,4},{10,6},{12,0},{14,2},{1,13},{3,15... | collective-permute-start | bytes 786440 | tf_op jit(solution)/shard_map/ppermute | solution.py:468
  37.9 21.8 %collective-permute-start.12 = (bf16[4,256,128]{2,1,0:T(8,128)(2,1)S(1)}, bf16[4,256,128]{2,1,0:T(8,128)(2,1)S(1)}, u32[]{:S(2)}, u32[]{:S(2)}) collective-permute-start(bf16[4,256,128]{2,1,0:T(8,128)(2,1)S(1)} %get-tuple-element.51), channel_id=1, source_target_pairs={{0,4},{2,6},{4,0},{6,2},{8,12},{10,14},{12,8},{14,10},{1,5},{3,7},... | collective-permute-start | bytes 786440 | tf_op jit(solution)/shard_map/ppermute | solution.py:468

commit v4 on v3

--- a/solution.py
+++ b/solution.py
@@ -364,79 +364,64 @@
             yield index, slice(start, start + step), slice(first, first + step)
 
 
+def add_terms(terms_ref, given_ref, dkey, dvalue):
+    terms_ref[0] = dkey if given_ref is None else given_ref[0] + dkey
+    terms_ref[1] = dvalue if given_ref is None else given_ref[1] + dvalue
+
+
 def near_kernel(chips, near, *refs):
     pair_blocks, refs = refs[: 2 * chips], refs[2 * chips :]
     outs, query_outs, refs = refs[:near], refs[near : 2 * near], refs[2 * near :]
-    terms_ref, key_ref, value_ref, probs_ref, scale_ref = refs
+    own_ref, other_ref, key_ref, value_ref, probs_ref, scale_ref = refs
     query_blocks = pair_blocks[:near]
     rows = outs[0].shape[1]
+    half = chips * rows
     load_keys(pair_blocks, key_ref, value_ref)
     forward_pass(query_blocks, outs, key_ref, value_ref, probs_ref, scale_ref)
     for index, part, here in row_parts(query_blocks, rows):
         query, grad = query_pair(query_blocks[index], part)
-        grad, delta = scaled_grad(
-            grad, scale_ref[here], outs[index][0, part]
-        )
+        grad, delta = scaled_grad(grad, scale_ref[here], outs[index][0, part])
         dquery, dkey, dvalue = backward_rows(
             query, grad, delta, probs_ref[here], key_ref[...], value_ref[:, :HD]
         )
         query_outs[index][0, part] = (dquery * SCORE_SCALE).astype(jnp.bfloat16)
-        if here.start == 0:
-            terms_ref[0] = dkey
-            terms_ref[1] = dvalue
-        else:
-            terms_ref[0] += dkey
-            terms_ref[1] += dvalue
-
-
-def far_kernel(chips, far, *refs):
-    pair_blocks, query_blocks, refs = refs[: 2 * chips], refs[2 * chips :][:far], refs[2 * chips + far :]
-    near_ref, outs, refs = refs[0], refs[1 : 1 + far], refs[1 + far :]
-    probs_out, scale_ref, query_terms, other_ref = refs[:4]
-    key_ref, value_ref, probs_ref, terms_ref = refs[4:]
-    rows = outs[0].shape[1]
-    half = chips * rows
-    load_keys(pair_blocks, key_ref, value_ref)
-    forward_pass(query_blocks, outs, key_ref, value_ref, probs_ref, scale_ref)
-    terms_ref[...] = near_ref[:, half:]
-    for index, part, here in row_parts(query_blocks, rows):
-        query, grad = query_pair(query_blocks[index], part)
-        grad, delta = scaled_grad(
-            grad, scale_ref[here], outs[index][0, part]
-        )
-        probs_out[here] = probs_ref[here, :half]
+        add_terms(own_ref, own_ref if here.start else None, dkey[:half], dvalue[:half])
+        add_terms(other_ref, other_ref if here.start else None, dkey[half:], dvalue[half:])
+
+
+def far_kernel(half, key_ref, value_ref, block_ref, given_ref, out, probs_out, scale_ref, query_terms, other_ref, probs_ref, terms_ref):
+    forward_pass([block_ref], [out], key_ref, value_ref, probs_ref, scale_ref)
+    probs_out[...] = probs_ref[:, :half]
+    for index, part, here in row_parts([block_ref], out.shape[1]):
+        query, grad = query_pair(block_ref, part)
+        grad, delta = scaled_grad(grad, scale_ref[here], out[0, part])
         dquery, dkey, dvalue = backward_rows(
             query, grad, delta, probs_ref[here, half:], key_ref[half:], value_ref[half:, :HD]
         )
         query_terms[here] = dquery
-        terms_ref[0] += dkey
-        terms_ref[1] += dvalue
-    other_ref[0] = (terms_ref[0] * SCORE_SCALE).astype(other_ref.dtype)
+        add_terms(terms_ref, terms_ref if here.start else given_ref, dkey, dvalue)
+    last = other_ref.dtype == jnp.bfloat16
+    other_ref[0] = (terms_ref[0] * (SCORE_SCALE if last else 1.0)).astype(other_ref.dtype)
     other_ref[1] = terms_ref[1].astype(other_ref.dtype)
 
 
-def own_kernel(chips, far, *refs):
-    pair_blocks, query_blocks, refs = refs[:chips], refs[chips:][:far], refs[chips + far :]
-    attended, refs = refs[:far], refs[far:]
-    near_ref, probs_ref, scale_ref, query_terms = refs[:4]
-    query_outs, refs = refs[4 : 4 + far], refs[4 + far :]
-    own_ref, key_ref, value_ref = refs
-    rows = attended[0].shape[1]
-    half = chips * rows
-    load_keys(pair_blocks, key_ref, value_ref)
-    own_ref[...] = near_ref[:, :half]
-    for index, part, here in row_parts(query_blocks, rows):
-        query, grad = query_pair(query_blocks[index], part)
-        grad, delta = scaled_grad(
-            grad, scale_ref[here], attended[index][0, part]
-        )
-        dquery, dkey, dvalue = backward_rows(
-            query, grad, delta, probs_ref[here], key_ref[...], value_ref[...]
-        )
-        dquery = (dquery + query_terms[here]) * SCORE_SCALE
-        query_outs[index][0, part] = dquery.astype(jnp.bfloat16)
-        own_ref[0] += dkey
-        own_ref[1] += dvalue
+def own_kernel(half, far, *refs):
+    key_ref, value_ref, given_ref, refs = *refs[:3], refs[3:]
+    query_blocks, attended, probs, scale, query_terms = (
+        refs[at * far : (at + 1) * far] for at in range(5)
+    )
+    query_outs, own_ref = refs[5 * far : -1], refs[-1]
+    for index, block_ref in enumerate(query_blocks):
+        for _, part, here in row_parts([block_ref], attended[index].shape[1]):
+            query, grad = query_pair(block_ref, part)
+            grad, delta = scaled_grad(grad, scale[index][here], attended[index][0, part])
+            dquery, dkey, dvalue = backward_rows(
+                query, grad, delta, probs[index][here], key_ref[:half], value_ref[:half, :HD]
+            )
+            dquery = (dquery + query_terms[index][here]) * SCORE_SCALE
+            query_outs[index][0, part] = dquery.astype(jnp.bfloat16)
+            fresh = index == 0 and here.start == 0
+            add_terms(own_ref, given_ref if fresh else own_ref, dkey, dvalue)
     own_ref[0] *= SCORE_SCALE
 
 
@@ -488,49 +473,52 @@
     chip = (lax.axis_index("seq") // 2).reshape(1)
     pairs = [key_rows, value_rows]
     queries = [query_rows, grad_output]
-    wanted = [(offset, pairs) for offset in range(near, chips)]
-    wanted += [(1, pairs + queries), (0, pairs + queries)]
-    wanted += [(offset, queries) for offset in range(near, chips)]
-    packed = []
-    for offset, arrays in wanted:
-        packed.append(pack(chip, arrays, offset))
-        chip = after(chip, packed[-1])
-    moved = [to_chip(block, offset) if offset else block for block, (offset, _) in zip(packed, wanted)]
-    pair_blocks = [moved[far + 1], moved[far]] + moved[:far]
-    query_blocks = moved[far + 2 :]
-    all_blocks = pair_blocks + [to_core(block) for block in pair_blocks]
+    wanted = [("keys", offset, pairs) for offset in range(2, chips)]
+    wanted += [("keys", offset, pairs + queries) for offset in (1, 0)]
+    wanted += [("queries", offset, queries) for offset in range(2, chips)]
+    moved = {}
+    for name, offset, arrays in wanted:
+        packed = pack(chip, arrays, offset)
+        chip = after(chip, packed)
+        moved[name, offset] = to_chip(packed, offset) if offset else packed
+    pair_blocks = [moved["keys", offset] for offset in range(chips)]
+    query_blocks = [moved["queries", offset] for offset in range(near, chips)]
+    all_blocks = pair_blocks + [to_core(value) for value in pair_blocks]
     block = ((1, rows, HD), bf16)
-    product = near * rows * keys * HD
-    *outs, terms = call_vmem(
+    terms = ((2, half, HD), f32)
+    *outs, own, other, key_all, value_ones = call_vmem(
         functools.partial(near_kernel, chips, near),
         "near",
         all_blocks,
-        [block] * (2 * near) + [((2, keys, HD), f32)],
-        [((keys, HD), bf16), ((keys, 2 * HD), bf16), ((near * rows, keys), bf16), ((near * rows, HD), f32)],
-        6 * product,
-        24 * MIB,
+        [block] * (2 * near) + [terms, terms, ((keys, HD), bf16), ((keys, 2 * HD), bf16)],
+        [((near * rows, keys), bf16), ((near * rows, HD), f32)],
+        6 * near * rows * keys * HD,
+        20 * MIB,
     )
     attended, query_grads = outs[:near], outs[near:]
-    product = far * rows * half * HD
-    *outs, probs, scale, query_terms, other = call_vmem(
-        functools.partial(far_kernel, chips, far),
-        "far",
-        all_blocks + query_blocks + [terms],
-        [block] * far
-        + [((far * rows, half), bf16), ((far * rows, HD), f32), ((far * rows, HD), f32), ((2, half, HD), bf16)],
-        [((keys, HD), bf16), ((keys, 2 * HD), bf16), ((far * rows, keys), bf16), ((2, half, HD), f32)],
-        8 * product,
-        24 * MIB,
-    )
+    parts = []
+    for index in range(far):
+        last = index == far - 1
+        *part, other = call_vmem(
+            functools.partial(far_kernel, half),
+            "far",
+            [key_all, value_ones, query_blocks[index], other],
+            [block, ((rows, half), bf16), ((rows, HD), f32), ((rows, HD), f32), ((2, half, HD), bf16 if last else f32)],
+            [((rows, keys), bf16), ((2, half, HD), f32)],
+            8 * rows * half * HD,
+            16 * MIB,
+        )
+        parts.append(part)
     other = to_core(other)
-    attended = attended + outs
+    columns = [list(column) for column in zip(*parts)]
+    attended = attended + columns[0]
     *outs, own = call_vmem(
-        functools.partial(own_kernel, chips, far),
+        functools.partial(own_kernel, half, far),
         "own",
-        pair_blocks + query_blocks + outs + [terms, probs, scale, query_terms],
-        [block] * far + [((2, half, HD), f32)],
-        [((half, HD), bf16), ((half, HD), bf16)],
-        4 * product,
+        [key_all, value_ones, own] + query_blocks + sum(columns, []),
+        [block] * far + [terms],
+        [],
+        4 * far * rows * half * HD,
         16 * MIB,
     )
     query_grads = query_grads + outs
@@ -543,7 +531,7 @@
         rows,
         8 * MIB,
     )
-    order = list(range(near, chips)) + [1]
+    order = list(range(chips - 1, 0, -1))
     returned = [outs[0]] + [to_chip(outs[offset], offset) for offset in order]
     layout = [(offset, (0, 1, 2, 3)) for offset in [0] + order]
     return tuple(unpack(chip, returned, layout, query_rows.shape[1]))

time: 61.6 us -> 60.4 us (0.981)
  the two profiles are of different devices: /device:TPU:12 before, /device:TPU:2 now
where the time goes in v4:
time: 60.4 us; the launch traced here: 60.3 us
  waiting for transfers between devices  33.3 us (55%)
  starting transfers between devices  14.3 us (24%)
  Pallas kernels  10.4 us (17%)
  local copies, waits for them, and re-layouts  1.18 us (2%)
  between operations  0.92 us (2%)
    ppermute x8, waiting for transfers between devices, to_chip(): lax.ppermute(array, 'seq', [(i, i ^ 2 * offset) for i in range(lax.axis_s...  31.9 us
    ppermute x8, starting transfers between devices, to_chip(): lax.ppermute(array, 'seq', [(i, i ^ 2 * offset) for i in range(lax.axis_s...  13.5 us
    pallas_call x5, Pallas kernels, call_vmem(): pl.pallas_call(kernel, out_shape=[jax.ShapeDtypeStruct(shape, dtype) for...  9.32 us
    ppermute x5, waiting for transfers between devices, to_core(): lax.ppermute(array, 'seq', [(i, i ^ 1) for i in range(lax.axis_size('seq'...  1.41 us
  transfers between devices with their start and end apart: 13, of which 5 were waited for; matrix products, arithmetic and copies ran while one was open for 1% of the time, Pallas kernels for 12%

profile of v4, /device:TPU:2, one launch (start us, length us, event | category | flops | bytes accessed | tf_op | source)
XLA Modules:
  0.0 60.3 jit_solution(4543672523923153343)
XLA Ops:
  0.7 0.9 %dynamic-slice_bitcast_fusion.14 = (bf16[1,256,128]{2,1,0:T(8,128)(2,1)S(1)}, bf16[1,256,128]{2,1,0:T(8,128)(2,1)S(1)}) fusion(bf16[256,512]{1,0:T(8,128)(2,1)} %param.7, s32[]{:T(128)S(6)} %select_n.34, bf16[256,512]{1,0:T(8,128)(2,1)} %param.6), kind=kLoop, calls=%fused_computation.20 | loop fusion | bytes 262148 | tf_op jit(solution)/shard_map/stack | solution.py:266
  1.7 2.7 %collective-permute-start.1 = (bf16[2,256,128]{2,1,0:T(8,128)(2,1)S(1)}, bf16[2,256,128]{2,1,0:T(8,128)(2,1)S(1)}, u32[]{:S(2)}, u32[]{:S(2)}) collective-permute-start(bf16[2,256,128]{2,1,0:T(8,128)(2,1)S(1)} %pad_maximum_fusion.2), channel_id=1, source_target_pairs={{0,8},{2,10},{4,12},{6,14},{8,0},{10,2},{12,4},{14,6},{1,9},{3,11}... | collective-permute-start | bytes 393224 | tf_op jit(solution)/shard_map/ppermute | solution.py:453
  4.4 1.9 %collective-permute-start.2 = (bf16[2,256,128]{2,1,0:T(8,128)(2,1)S(1)}, bf16[2,256,128]{2,1,0:T(8,128)(2,1)S(1)}, u32[]{:S(2)}, u32[]{:S(2)}) collective-permute-start(bf16[2,256,128]{2,1,0:T(8,128)(2,1)S(1)} %pad_maximum_fusion.3), channel_id=1, source_target_pairs={{0,12},{2,14},{4,8},{6,10},{8,4},{10,6},{12,0},{14,2},{1,13},{3,15... | collective-permute-start | bytes 393224 | tf_op jit(solution)/shard_map/ppermute | solution.py:453
  6.5 0.6 collective-permute-start
  7.2 0.1 collective-permute-start.3
  7.3 2.1 %collective-permute-start.7 = (bf16[2,256,128]{2,1,0:T(8,128)(2,1)S(1)}, bf16[2,256,128]{2,1,0:T(8,128)(2,1)S(1)}, u32[]{:S(2)}, u32[]{:S(2)}) collective-permute-start(bf16[2,256,128]{2,1,0:T(8,128)(2,1)S(1)} %pad_maximum_fusion.4), channel_id=1, source_target_pairs={{0,8},{2,10},{4,12},{6,14},{8,0},{10,2},{12,4},{14,6},{1,9},{3,11}... | collective-permute-start | bytes 393224 | tf_op jit(solution)/shard_map/ppermute | solution.py:453
  9.4 10.4 %collective-permute-done.refs_1_ = bf16[4,256,128]{2,1,0:T(8,128)(2,1)S(1)} collective-permute-done((bf16[4,256,128]{2,1,0:T(8,128)(2,1)S(1)}, bf16[4,256,128]{2,1,0:T(8,128)(2,1)S(1)}, u32[]{:S(2)}, u32[]{:S(2)}) %collective-permute-start) | collective-permute-done | bytes 262176 | tf_op jit(solution)/shard_map/ppermute | solution.py:453
  19.9 0.6 collective-permute-start.6
  20.4 0.1 collective-permute-start.5
  20.5 1.0 %collective-permute-done.6.refs_7_ = bf16[2,256,128]{2,1,0:T(8,128)(2,1)S(1)} collective-permute-done((bf16[2,256,128]{2,1,0:T(8,128)(2,1)S(1)}, bf16[2,256,128]{2,1,0:T(8,128)(2,1)S(1)}, u32[]{:S(2)}, u32[]{:S(2)}) %collective-permute-start.6) | collective-permute-done | bytes 131104 | tf_op jit(solution)/shard_map/ppermute | solution.py:459
  21.5 1.8 %collective-permute-start.8 = (bf16[2,256,128]{2,1,0:T(8,128)(2,1)S(1)}, bf16[2,256,128]{2,1,0:T(8,128)(2,1)S(1)}, u32[]{:S(2)}, u32[]{:S(2)}) collective-permute-start(bf16[2,256,128]{2,1,0:T(8,128)(2,1)S(1)} %pad_maximum_fusion.5), channel_id=1, source_target_pairs={{0,12},{2,14},{4,8},{6,10},{8,4},{10,6},{12,0},{14,2},{1,13},{3,15... | collective-permute-start | bytes 393224 | tf_op jit(solution)/shard_map/ppermute | solution.py:453
  23.4 4.0 %near.1 = (bf16[1,256,128]{2,1,0:T(8,128)(2,1)S(1)}, bf16[1,256,128]{2,1,0:T(8,128)(2,1)S(1)}, bf16[1,256,128]{2,1,0:T(8,128)(2,1)S(1)}, bf16[1,256,128]{2,1,0:T...) custom-call(bf16[4,256,128]{2,1,0:T(8,128)(2,1)S(1)} %pad_maximum_fu, ...), custom_call_target="tpu_custom_call" | custom-call | flops 1610612736 | bytes 1048576 | tf_op jit(solution)/shard_map/near/pallas_call | solution.py:429
  27.4 1.9 %far.2 = (bf16[1,256,128]{2,1,0:T(8,128)(2,1)S(1)}, bf16[256,1024]{1,0:T(8,128)(2,1)S(1)}, f32[256,128]{1,0:T(8,128)S(1)}, f32[256,128]{1,0:T(8,128)S(1)}, f32[2,1024,128]{2,1,0:T(8,128)S(1)}) custom-call(bf16[2048,128]{1,0:T(8,128)(2,1)S(1)} %get-tuple-element.41.key_ref.refs_0_, bf16[2048,256]{1,0:T(8,128)(2,1)S(1)} %get-tuple-element.42.value_ref.refs_1_, ...), custom_call_target="tpu_custom_call" | custom-call | flops 536870912 | bytes 1048576 | tf_op jit(solution)/shard_map/far/pallas_call | solution.py:429
  29.3 1.9 %far.3 = (bf16[1,256,128]{2,1,0:T(8,128)(2,1)S(1)}, bf16[256,1024]{1,0:T(8,128)(2,1)S(1)}, f32[256,128]{1,0:T(8,128)S(1)}, f32[256,128]{1,0:T(8,128)S(1)}, bf16[2,1024,128]{2,1,0:T(8,128)(2,1)S(1)}) custom-call(bf16[2048,128]{1,0:T(8,128)(2,1)S(1)} %get-tuple-element.41.key_ref.refs_0_, bf16[2048,256]{1,0:T(8,128)(2,1)S(1)} %get-tuple-element.42.value_ref.refs_1_, ...), custom_call_target="tpu_custom_call" | custom-call | flops 536870912 | bytes 1048576 | tf_op jit(solution)/shard_map/far/pallas_call | solution.py:429
  31.1 0.1 collective-permute-start.9
  31.2 1.5 %own.1 = (bf16[1,256,128]{2,1,0:T(8,128)(2,1)S(1)}, bf16[1,256,128]{2,1,0:T(8,128)(2,1)S(1)}, f32[2,1024,128]{2,1,0:T(8,128)S(1)}) custom-call(bf16[2048,128]{1,0:T(8,128)(2,1)S(1)} %get-tuple-element.41.key_ref.refs_0_, bf16[2048,256]{1,0:T(8,128)(2,1)S(1)} %get-tuple-element.42.value_ref.refs_1_, f32[2,1024,128]{2,1,0:T(8,128)S(1)} %get-tuple-element.43.refs_2_, ...), custom_call_target="tpu_custom_call" | custom-call | flops 536870912 | bytes 1048576 | tf_op jit(solution)/shard_map/own/pallas_call | solution.py:429
  32.7 0.4 collective-permute-done.9.other_ref
  33.1 0.1 add_partials.1
  33.2 2.1 %collective-permute-start.10 = (bf16[4,256,128]{2,1,0:T(8,128)(2,1)S(1)}, bf16[4,256,128]{2,1,0:T(8,128)(2,1)S(1)}, u32[]{:S(2)}, u32[]{:S(2)}) collective-permute-start(bf16[4,256,128]{2,1,0:T(8,128)(2,1)S(1)} %get-tuple-element.63), channel_id=1, source_target_pairs={{0,12},{2,14},{4,8},{6,10},{8,4},{10,6},{12,0},{14,2},{1,13},{3,15... | collective-permute-start | bytes 786440 | tf_op jit(solution)/shard_map/ppermute | solution.py:453
  35.3 0.7 %collective-permute-start.11 = (bf16[4,256,128]{2,1,0:T(8,128)(2,1)S(1)}, bf16[4,256,128]{2,1,0:T(8,128)(2,1)S(1)}, u32[]{:S(2)}, u32[]{:S(2)}) collective-permute-start(bf16[4,256,128]{2,1,0:T(8,128)(2,1)S(1)} %get-tuple-element.64), channel_id=1, source_target_pairs={{0,8},{2,10},{4,12},{6,14},{8,0},{10,2},{12,4},{14,6},{1,9},{3,11}... | collective-permute-start | bytes 786440 | tf_op jit(solution)/shard_map/ppermute | solution.py:453
  36.0 1.7 %collective-permute-start.12 = (bf16[4,256,128]{2,1,0:T(8,128)(2,1)S(1)}, bf16[4,256,128]{2,1,0:T(8,128)(2,1)S(1)}, u32[]{:S(2)}, u32[]{:S(2)}) collective-permute-start(bf16[4,256,128]{2,1,0:T(8,128)(2,1)S(1)} %get-tuple-element.65), channel_id=1, source_target_pairs={{0,4},{2,6},{4,0},{6,2},{8,12},{10,14},{12,8},{14,10},{1,5},{3,7},... | collective-permute-start | bytes 786440 | tf_op jit(solution)/shard_map/ppermute | solution.py:453
  37.7 6.7 %collective-permute-done.10.refs_1_ = bf16[4,256,128]{2,1,0:T(8,128)(2,1)S(1)} collective-permute-done((bf16[4,256,128]{2,1,0:T(8,128)(2,1)S(1)}, bf16[4,256,128]{2,1,0:T(8,128)(2,1)S(1)}, u32[]{:S(2)}, u32[]{:S(2)}) %collective-permute-start.10) | collective-permute-done | bytes 262176 | tf_op jit(solution)/shard_map/ppermute | solution.py:453
  44.4 14.8 %collective-permute-done.11.refs_2_ = bf16[4,256,128]{2,1,0:T(8,128)(2,1)S(1)} collective-permute-done((bf16[4,256,128]{2,1,0:T(8,128)(2,1)S(1)}, bf16[4,256,128]{2,1,0:T(8,128)(2,1)S(1)}, u32[]{:S(2)}, u32[]{:S(2)}) %collective-permute-start.11) | collective-permute-done | bytes 262176 | tf_op jit(solution)/shard_map/ppermute | solution.py:453
  59.2 1.1 %unpack.1 = (bf16[256,512]{1,0:T(8,128)(2,1)}, bf16[256,512]{1,0:T(8,128)(2,1)}, bf16[256,512]{1,0:T(8,128)(2,1)}, bf16[256,512]{1,0:T(8,128)(2,1)}) custom-call(s32[1]{0:T(128)} %bitcast.chip_ref, bf16[4,256,128]{2,1,0:T(8,128)(2,1)S(1)} %get-tuple-element.62.refs_0_, bf16[4,256,128]{2,1,0:T(8,128)(2,1)S(1)} %collective-permute-done.10.refs_1_, ...), custom_call_target="tpu_custom_call" | custom-call | tf_op jit(solution)/shard_map/unpack/pallas_call | solution.py:292
  (37 shorter events, 0.4 us)
Async XLA Ops:
  0.6 5.7 %copy-start = (bf16[256,512]{1,0:T(8,128)(2,1)S(1)}, bf16[256,512]{1,0:T(8,128)(2,1)}, u32[]{:S(2)}) copy-start(bf16[256,512]{1,0:T(8,128)(2,1)} %param.8) | copy-start | bytes 786436
  0.7 3.6 %copy-start.2 = (bf16[256,512]{1,0:T(8,128)(2,1)S(1)}, bf16[256,512]{1,0:T(8,128)(2,1)}, u32[]{:S(2)}) copy-start(bf16[256,512]{1,0:T(8,128)(2,1)} %param.7) | copy-start | bytes 786436
  1.6 2.7 %copy-start.3 = (bf16[256,512]{1,0:T(8,128)(2,1)S(1)}, bf16[256,512]{1,0:T(8,128)(2,1)}, u32[]{:S(2)}) copy-start(bf16[256,512]{1,0:T(8,128)(2,1)} %param.6) | copy-start | bytes 786436
  1.7 18.8 %collective-permute-start.1 = (bf16[2,256,128]{2,1,0:T(8,128)(2,1)S(1)}, bf16[2,256,128]{2,1,0:T(8,128)(2,1)S(1)}, u32[]{:S(2)}, u32[]{:S(2)}) collective-permute-start(bf16[2,256,128]{2,1,0:T(8,128)(2,1)S(1)} %pad_maximum_fusion.2), channel_id=1, source_target_pairs={{0,8},{2,10},{4,12},{6,14},{8,0},{10,2},{12,4},{14,6},{1,9},{3,11}... | collective-permute-start | bytes 393224 | tf_op jit(solution)/shard_map/ppermute | solution.py:453
  4.4 2.0 %copy-start.1 = (bf16[256,512]{1,0:T(8,128)(2,1)S(1)}, bf16[256,512]{1,0:T(8,128)(2,1)}, u32[]{:S(2)}) copy-start(bf16[256,512]{1,0:T(8,128)(2,1)} %param.5) | copy-start | bytes 786436
  4.4 15.4 %collective-permute-start.2 = (bf16[2,256,128]{2,1,0:T(8,128)(2,1)S(1)}, bf16[2,256,128]{2,1,0:T(8,128)(2,1)S(1)}, u32[]{:S(2)}, u32[]{:S(2)}) collective-permute-start(bf16[2,256,128]{2,1,0:T(8,128)(2,1)S(1)} %pad_maximum_fusion.3), channel_id=1, source_target_pairs={{0,12},{2,14},{4,8},{6,10},{8,4},{10,6},{12,0},{14,2},{1,13},{3,15... | collective-permute-start | bytes 393224 | tf_op jit(solution)/shard_map/ppermute | solution.py:453
  6.5 13.4 %collective-permute-start = (bf16[4,256,128]{2,1,0:T(8,128)(2,1)S(1)}, bf16[4,256,128]{2,1,0:T(8,128)(2,1)S(1)}, u32[]{:S(2)}, u32[]{:S(2)}) collective-permute-start(bf16[4,256,128]{2,1,0:T(8,128)(2,1)S(1)} %pad_maximum_fusion), channel_id=1, source_target_pairs={{0,4},{2,6},{4,0},{6,2},{8,12},{10,14},{12,8},{14,10},{1,5},{3,7},... | collective-permute-start | bytes 786440 | tf_op jit(solution)/shard_map/ppermute | solution.py:453
  7.2 16.2 %collective-permute-start.3 = (bf16[4,256,128]{2,1,0:T(8,128)(2,1)S(1)}, bf16[4,256,128]{2,1,0:T(8,128)(2,1)S(1)}, u32[]{:S(2)}, u32[]{:S(2)}) collective-permute-start(bf16[4,256,128]{2,1,0:T(8,128)(2,1)S(1)} %pad_maximum_fusion.1.refs_0_), channel_id=1, source_target_pairs={{0,2},{2,0},{4,6},{6,4},{8,10},{10,8},{12,14},{14,12},{1,3},{3,1},... | collective-permute-start | bytes 786440 | tf_op jit(solution)/shard_map/ppermute | solution.py:459
  7.3 20.1 %collective-permute-start.7 = (bf16[2,256,128]{2,1,0:T(8,128)(2,1)S(1)}, bf16[2,256,128]{2,1,0:T(8,128)(2,1)S(1)}, u32[]{:S(2)}, u32[]{:S(2)}) collective-permute-start(bf16[2,256,128]{2,1,0:T(8,128)(2,1)S(1)} %pad_maximum_fusion.4), channel_id=1, source_target_pairs={{0,8},{2,10},{4,12},{6,14},{8,0},{10,2},{12,4},{14,6},{1,9},{3,11}... | collective-permute-start | bytes 393224 | tf_op jit(solution)/shard_map/ppermute | solution.py:453
  19.8 3.6 %collective-permute-start.4 = (bf16[4,256,128]{2,1,0:T(8,128)(2,1)S(1)}, bf16[4,256,128]{2,1,0:T(8,128)(2,1)S(1)}, u32[]{:S(2)}, u32[]{:S(2)}) collective-permute-start(bf16[4,256,128]{2,1,0:T(8,128)(2,1)S(1)} %collective-permute-done.refs_1_), channel_id=1, source_target_pairs={{0,2},{2,0},{4,6},{6,4},{8,10},{10,8},{12,14},{14,12},{1,3},{3,1},... | collective-permute-start | bytes 786440 | tf_op jit(solution)/shard_map/ppermute | solution.py:459
  19.9 1.7 %collective-permute-start.6 = (bf16[2,256,128]{2,1,0:T(8,128)(2,1)S(1)}, bf16[2,256,128]{2,1,0:T(8,128)(2,1)S(1)}, u32[]{:S(2)}, u32[]{:S(2)}) collective-permute-start(bf16[2,256,128]{2,1,0:T(8,128)(2,1)S(1)} %collective-permute-done.2.refs_3_), channel_id=1, source_target_pairs={{0,2},{2,0},{4,6},{6,4},{8,10},{10,8},{12,14},{14,12},{1,3},{3,1},... | collective-permute-start | bytes 393224 | tf_op jit(solution)/shard_map/ppermute | solution.py:459
  20.4 3.0 %collective-permute-start.5 = (bf16[2,256,128]{2,1,0:T(8,128)(2,1)S(1)}, bf16[2,256,128]{2,1,0:T(8,128)(2,1)S(1)}, u32[]{:S(2)}, u32[]{:S(2)}) collective-permute-start(bf16[2,256,128]{2,1,0:T(8,128)(2,1)S(1)} %collective-permute-done.1.refs_2_), channel_id=1, source_target_pairs={{0,2},{2,0},{4,6},{6,4},{8,10},{10,8},{12,14},{14,12},{1,3},{3,1},... | collective-permute-start | bytes 393224 | tf_op jit(solution)/shard_map/ppermute | solution.py:459
  21.5 7.7 %collective-permute-start.8 = (bf16[2,256,128]{2,1,0:T(8,128)(2,1)S(1)}, bf16[2,256,128]{2,1,0:T(8,128)(2,1)S(1)}, u32[]{:S(2)}, u32[]{:S(2)}) collective-permute-start(bf16[2,256,128]{2,1,0:T(8,128)(2,1)S(1)} %pad_maximum_fusion.5), channel_id=1, source_target_pairs={{0,12},{2,14},{4,8},{6,10},{8,4},{10,6},{12,0},{14,2},{1,13},{3,15... | collective-permute-start | bytes 393224 | tf_op jit(solution)/shard_map/ppermute | solution.py:453
  31.1 2.0 %collective-permute-start.9 = (bf16[2,1024,128]{2,1,0:T(8,128)(2,1)S(1)}, bf16[2,1024,128]{2,1,0:T(8,128)(2,1)S(1)}, u32[]{:S(2)}, u32[]{:S(2)}) collective-permute-start(bf16[2,1024,128]{2,1,0:T(8,128)(2,1)S(1)} %get-tuple-element.55), channel_id=1, source_target_pairs={{0,2},{2,0},{4,6},{6,4},{8,10},{10,8},{12,14},{14,12},{1,3},{3,1},... | collective-permute-start | bytes 1572872 | tf_op jit(solution)/shard_map/ppermute | solution.py:459
  33.2 11.2 %collective-permute-start.10 = (bf16[4,256,128]{2,1,0:T(8,128)(2,1)S(1)}, bf16[4,256,128]{2,1,0:T(8,128)(2,1)S(1)}, u32[]{:S(2)}, u32[]{:S(2)}) collective-permute-start(bf16[4,256,128]{2,1,0:T(8,128)(2,1)S(1)} %get-tuple-element.63), channel_id=1, source_target_pairs={{0,12},{2,14},{4,8},{6,10},{8,4},{10,6},{12,0},{14,2},{1,13},{3,15... | collective-permute-start | bytes 786440 | tf_op jit(solution)/shard_map/ppermute | solution.py:453
  35.3 23.9 %collective-permute-start.11 = (bf16[4,256,128]{2,1,0:T(8,128)(2,1)S(1)}, bf16[4,256,128]{2,1,0:T(8,128)(2,1)S(1)}, u32[]{:S(2)}, u32[]{:S(2)}) collective-permute-start(bf16[4,256,128]{2,1,0:T(8,128)(2,1)S(1)} %get-tuple-element.64), channel_id=1, source_target_pairs={{0,8},{2,10},{4,12},{6,14},{8,0},{10,2},{12,4},{14,6},{1,9},{3,11}... | collective-permute-start | bytes 786440 | tf_op jit(solution)/shard_map/ppermute | solution.py:453
  36.0 23.2 %collective-permute-start.12 = (bf16[4,256,128]{2,1,0:T(8,128)(2,1)S(1)}, bf16[4,256,128]{2,1,0:T(8,128)(2,1)S(1)}, u32[]{:S(2)}, u32[]{:S(2)}) collective-permute-start(bf16[4,256,128]{2,1,0:T(8,128)(2,1)S(1)} %get-tuple-element.65), channel_id=1, source_target_pairs={{0,4},{2,6},{4,0},{6,2},{8,12},{10,14},{12,8},{14,10},{1,5},{3,7},... | collective-permute-start | bytes 786440 | tf_op jit(solution)/shard_map/ppermute | solution.py:453

commit v5 on v4

--- a/solution.py
+++ b/solution.py
@@ -483,7 +483,11 @@
         moved[name, offset] = to_chip(packed, offset) if offset else packed
     pair_blocks = [moved["keys", offset] for offset in range(chips)]
     query_blocks = [moved["queries", offset] for offset in range(near, chips)]
-    all_blocks = pair_blocks + [to_core(value) for value in pair_blocks]
+    swapped = [to_core(pair_blocks[0])]
+    for offset in range(1, chips):
+        value = pair_blocks[offset]
+        swapped.append(to_core(after(value, swapped[0]) if offset in (1,) else value))
+    all_blocks = pair_blocks + swapped
     block = ((1, rows, HD), bf16)
     terms = ((2, half, HD), f32)
     *outs, own, other, key_all, value_ones = call_vmem(
@@ -531,7 +535,7 @@
         rows,
         8 * MIB,
     )
-    order = list(range(chips - 1, 0, -1))
+    order = list(range(2, chips)) + [1]
     returned = [outs[0]] + [to_chip(outs[offset], offset) for offset in order]
     layout = [(offset, (0, 1, 2, 3)) for offset in [0] + order]
     return tuple(unpack(chip, returned, layout, query_rows.shape[1]))

time: 60.4 us -> 58.8 us (0.974)
  the two profiles are of different devices: /device:TPU:2 before, /device:TPU:12 now
where the time goes in v5:
time: 58.8 us; the launch traced here: 58.6 us
  waiting for transfers between devices  34.5 us (59%)
  starting transfers between devices  10.7 us (18%)
  Pallas kernels  10.4 us (18%)
  local copies, waits for them, and re-layouts  1.94 us (3%)
  between operations  0.92 us (2%)
    ppermute x8, waiting for transfers between devices, to_chip(): lax.ppermute(array, 'seq', [(i, i ^ 2 * offset) for i in range(lax.axis_s...  33 us
    ppermute x8, starting transfers between devices, to_chip(): lax.ppermute(array, 'seq', [(i, i ^ 2 * offset) for i in range(lax.axis_s...  10.1 us
    pallas_call x5, Pallas kernels, call_vmem(): pl.pallas_call(kernel, out_shape=[jax.ShapeDtypeStruct(shape, dtype) for...  9.31 us
    ppermute x5, waiting for transfers between devices, to_core(): lax.ppermute(array, 'seq', [(i, i ^ 1) for i in range(lax.axis_size('seq'...  1.49 us
  transfers between devices with their start and end apart: 13, of which 9 were waited for; matrix products, arithmetic and copies ran while one was open for 1% of the time, Pallas kernels for 13%

profile of v5, /device:TPU:12, one launch (start us, length us, event | category | flops | bytes accessed | tf_op | source)
XLA Modules:
  0.0 58.6 jit_solution(1410323658308611369)
XLA Ops:
  0.7 0.9 %dynamic-slice_bitcast_fusion.14 = (bf16[1,256,128]{2,1,0:T(8,128)(2,1)S(1)}, bf16[1,256,128]{2,1,0:T(8,128)(2,1)S(1)}) fusion(bf16[256,512]{1,0:T(8,128)(2,1)} %param.7, s32[]{:T(128)S(6)} %select_n.34, bf16[256,512]{1,0:T(8,128)(2,1)} %param.6), kind=kLoop, calls=%fused_computation.20 | loop fusion | bytes 262148 | tf_op jit(solution)/shard_map/stack | solution.py:266
  1.7 2.7 %collective-permute-start.1 = (bf16[2,256,128]{2,1,0:T(8,128)(2,1)S(1)}, bf16[2,256,128]{2,1,0:T(8,128)(2,1)S(1)}, u32[]{:S(2)}, u32[]{:S(2)}) collective-permute-start(bf16[2,256,128]{2,1,0:T(8,128)(2,1)S(1)} %pad_maximum_fusion.2), channel_id=1, source_target_pairs={{0,8},{2,10},{4,12},{6,14},{8,0},{10,2},{12,4},{14,6},{1,9},{3,11}... | collective-permute-start | bytes 393224 | tf_op jit(solution)/shard_map/ppermute | solution.py:453
  4.6 0.8 %copy-done.1 = bf16[256,512]{1,0:T(8,128)(2,1)S(1)} copy-done((bf16[256,512]{1,0:T(8,128)(2,1)S(1)}, bf16[256,512]{1,0:T(8,128)(2,1)}, u32[]{:S(2)}) %copy-start.1) | copy-done | bytes 262168
  5.4 1.6 %collective-permute-start = (bf16[4,256,128]{2,1,0:T(8,128)(2,1)S(1)}, bf16[4,256,128]{2,1,0:T(8,128)(2,1)S(1)}, u32[]{:S(2)}, u32[]{:S(2)}) collective-permute-start(bf16[4,256,128]{2,1,0:T(8,128)(2,1)S(1)} %pad_maximum_fusion), channel_id=1, source_target_pairs={{0,4},{2,6},{4,0},{6,2},{8,12},{10,14},{12,8},{14,10},{1,5},{3,7},... | collective-permute-start | bytes 786440 | tf_op jit(solution)/shard_map/ppermute | solution.py:453
  7.3 1.3 %collective-permute-start.7 = (bf16[2,256,128]{2,1,0:T(8,128)(2,1)S(1)}, bf16[2,256,128]{2,1,0:T(8,128)(2,1)S(1)}, u32[]{:S(2)}, u32[]{:S(2)}) collective-permute-start(bf16[2,256,128]{2,1,0:T(8,128)(2,1)S(1)} %pad_maximum_fusion.4), channel_id=1, source_target_pairs={{0,8},{2,10},{4,12},{6,14},{8,0},{10,2},{12,4},{14,6},{1,9},{3,11}... | collective-permute-start | bytes 393224 | tf_op jit(solution)/shard_map/ppermute | solution.py:453
  8.5 0.2 collective-permute-done.3.refs_4_
  8.7 9.1 %collective-permute-done.refs_1_ = bf16[4,256,128]{2,1,0:T(8,128)(2,1)S(1)} collective-permute-done((bf16[4,256,128]{2,1,0:T(8,128)(2,1)S(1)}, bf16[4,256,128]{2,1,0:T(8,128)(2,1)S(1)}, u32[]{:S(2)}, u32[]{:S(2)}) %collective-permute-start) | collective-permute-done | bytes 262176 | tf_op jit(solution)/shard_map/ppermute | solution.py:453
  17.8 1.4 %collective-permute-done.2.refs_3_ = bf16[2,256,128]{2,1,0:T(8,128)(2,1)S(1)} collective-permute-done((bf16[2,256,128]{2,1,0:T(8,128)(2,1)S(1)}, bf16[2,256,128]{2,1,0:T(8,128)(2,1)S(1)}, u32[]{:S(2)}, u32[]{:S(2)}) %collective-permute-start.2) | collective-permute-done | bytes 131104 | tf_op jit(solution)/shard_map/ppermute | solution.py:453
  19.3 0.5 collective-permute-start.5
  19.9 0.7 %collective-permute-done.6.refs_7_ = bf16[2,256,128]{2,1,0:T(8,128)(2,1)S(1)} collective-permute-done((bf16[2,256,128]{2,1,0:T(8,128)(2,1)S(1)}, bf16[2,256,128]{2,1,0:T(8,128)(2,1)S(1)}, u32[]{:S(2)}, u32[]{:S(2)}) %collective-permute-start.6) | collective-permute-done | bytes 131104 | tf_op jit(solution)/shard_map/ppermute | solution.py:459
  20.6 0.2 collective-permute-done.5.refs_6_
  20.8 4.0 %near.1 = (bf16[1,256,128]{2,1,0:T(8,128)(2,1)S(1)}, bf16[1,256,128]{2,1,0:T(8,128)(2,1)S(1)}, bf16[1,256,128]{2,1,0:T(8,128)(2,1)S(1)}, bf16[1,256,128]{2,1,0:T...) custom-call(bf16[4,256,128]{2,1,0:T(8,128)(2,1)S(1)} %pad_maximum_fu, ...), custom_call_target="tpu_custom_call" | custom-call | flops 1610612736 | bytes 1048576 | tf_op jit(solution)/shard_map/near/pallas_call | solution.py:429
  24.8 1.9 %far.2 = (bf16[1,256,128]{2,1,0:T(8,128)(2,1)S(1)}, bf16[256,1024]{1,0:T(8,128)(2,1)S(1)}, f32[256,128]{1,0:T(8,128)S(1)}, f32[256,128]{1,0:T(8,128)S(1)}, f32[2,1024,128]{2,1,0:T(8,128)S(1)}) custom-call(bf16[2048,128]{1,0:T(8,128)(2,1)S(1)} %get-tuple-element.43.key_ref.refs_0_, bf16[2048,256]{1,0:T(8,128)(2,1)S(1)} %get-tuple-element.44.value_ref.refs_1_, ...), custom_call_target="tpu_custom_call" | custom-call | flops 536870912 | bytes 1048576 | tf_op jit(solution)/shard_map/far/pallas_call | solution.py:429
  26.7 1.4 %collective-permute-done.8.block_ref.refs_4_ = bf16[2,256,128]{2,1,0:T(8,128)(2,1)S(1)} collective-permute-done((bf16[2,256,128]{2,1,0:T(8,128)(2,1)S(1)}, bf16[2,256,128]{2,1,0:T(8,128)(2,1)S(1)}, u32[]{:S(2)}, u32[]{:S(2)}) %collective-permute-start.8) | collective-permute-done | bytes 131104 | tf_op jit(solution)/shard_map/ppermute | solution.py:453
  28.1 1.9 %far.3 = (bf16[1,256,128]{2,1,0:T(8,128)(2,1)S(1)}, bf16[256,1024]{1,0:T(8,128)(2,1)S(1)}, f32[256,128]{1,0:T(8,128)S(1)}, f32[256,128]{1,0:T(8,128)S(1)}, bf16[2,1024,128]{2,1,0:T(8,128)(2,1)S(1)}) custom-call(bf16[2048,128]{1,0:T(8,128)(2,1)S(1)} %get-tuple-element.43.key_ref.refs_0_, bf16[2048,256]{1,0:T(8,128)(2,1)S(1)} %get-tuple-element.44.value_ref.refs_1_, ...), custom_call_target="tpu_custom_call" | custom-call | flops 536870912 | bytes 1048576 | tf_op jit(solution)/shard_map/far/pallas_call | solution.py:429
  30.0 1.5 %own.1 = (bf16[1,256,128]{2,1,0:T(8,128)(2,1)S(1)}, bf16[1,256,128]{2,1,0:T(8,128)(2,1)S(1)}, f32[2,1024,128]{2,1,0:T(8,128)S(1)}) custom-call(bf16[2048,128]{1,0:T(8,128)(2,1)S(1)} %get-tuple-element.43.key_ref.refs_0_, bf16[2048,256]{1,0:T(8,128)(2,1)S(1)} %get-tuple-element.44.value_ref.refs_1_, f32[2,1024,128]{2,1,0:T(8,128)S(1)} %get-tuple-element.45.refs_2_, ...), custom_call_target="tpu_custom_call" | custom-call | flops 536870912 | bytes 1048576 | tf_op jit(solution)/shard_map/own/pallas_call | solution.py:429
  31.5 0.4 collective-permute-done.9.other_ref
  31.9 0.1 add_partials.1
  32.0 1.3 %collective-permute-start.10 = (bf16[4,256,128]{2,1,0:T(8,128)(2,1)S(1)}, bf16[4,256,128]{2,1,0:T(8,128)(2,1)S(1)}, u32[]{:S(2)}, u32[]{:S(2)}) collective-permute-start(bf16[4,256,128]{2,1,0:T(8,128)(2,1)S(1)} %get-tuple-element.65), channel_id=1, source_target_pairs={{0,8},{2,10},{4,12},{6,14},{8,0},{10,2},{12,4},{14,6},{1,9},{3,11}... | collective-permute-start | bytes 786440 | tf_op jit(solution)/shard_map/ppermute | solution.py:453
  33.3 0.9 %collective-permute-start.11 = (bf16[4,256,128]{2,1,0:T(8,128)(2,1)S(1)}, bf16[4,256,128]{2,1,0:T(8,128)(2,1)S(1)}, u32[]{:S(2)}, u32[]{:S(2)}) collective-permute-start(bf16[4,256,128]{2,1,0:T(8,128)(2,1)S(1)} %get-tuple-element.66), channel_id=1, source_target_pairs={{0,12},{2,14},{4,8},{6,10},{8,4},{10,6},{12,0},{14,2},{1,13},{3,15... | collective-permute-start | bytes 786440 | tf_op jit(solution)/shard_map/ppermute | solution.py:453
  34.3 2.2 %collective-permute-start.12 = (bf16[4,256,128]{2,1,0:T(8,128)(2,1)S(1)}, bf16[4,256,128]{2,1,0:T(8,128)(2,1)S(1)}, u32[]{:S(2)}, u32[]{:S(2)}) collective-permute-start(bf16[4,256,128]{2,1,0:T(8,128)(2,1)S(1)} %get-tuple-element.67), channel_id=1, source_target_pairs={{0,4},{2,6},{4,0},{6,2},{8,12},{10,14},{12,8},{14,10},{1,5},{3,7},... | collective-permute-start | bytes 786440 | tf_op jit(solution)/shard_map/ppermute | solution.py:453
  36.5 14.7 %collective-permute-done.10.refs_1_ = bf16[4,256,128]{2,1,0:T(8,128)(2,1)S(1)} collective-permute-done((bf16[4,256,128]{2,1,0:T(8,128)(2,1)S(1)}, bf16[4,256,128]{2,1,0:T(8,128)(2,1)S(1)}, u32[]{:S(2)}, u32[]{:S(2)}) %collective-permute-start.10) | collective-permute-done | bytes 262176 | tf_op jit(solution)/shard_map/ppermute | solution.py:453
  51.2 6.3 %collective-permute-done.11.refs_2_ = bf16[4,256,128]{2,1,0:T(8,128)(2,1)S(1)} collective-permute-done((bf16[4,256,128]{2,1,0:T(8,128)(2,1)S(1)}, bf16[4,256,128]{2,1,0:T(8,128)(2,1)S(1)}, u32[]{:S(2)}, u32[]{:S(2)}) %collective-permute-start.11) | collective-permute-done | bytes 262176 | tf_op jit(solution)/shard_map/ppermute | solution.py:453
  57.5 1.1 %unpack.1 = (bf16[256,512]{1,0:T(8,128)(2,1)}, bf16[256,512]{1,0:T(8,128)(2,1)}, bf16[256,512]{1,0:T(8,128)(2,1)}, bf16[256,512]{1,0:T(8,128)(2,1)}) custom-call(s32[1]{0:T(128)} %bitcast.chip_ref, bf16[4,256,128]{2,1,0:T(8,128)(2,1)S(1)} %get-tuple-element.64.refs_0_, bf16[4,256,128]{2,1,0:T(8,128)(2,1)S(1)} %collective-permute-done.10.refs_1_, ...), custom_call_target="tpu_custom_call" | custom-call | tf_op jit(solution)/shard_map/unpack/pallas_call | solution.py:292
  (37 shorter events, 0.7 us)
Async XLA Ops:
  0.6 3.9 %copy-start = (bf16[256,512]{1,0:T(8,128)(2,1)S(1)}, bf16[256,512]{1,0:T(8,128)(2,1)}, u32[]{:S(2)}) copy-start(bf16[256,512]{1,0:T(8,128)(2,1)} %param.8) | copy-start | bytes 786436
  0.7 3.6 %copy-start.2 = (bf16[256,512]{1,0:T(8,128)(2,1)S(1)}, bf16[256,512]{1,0:T(8,128)(2,1)}, u32[]{:S(2)}) copy-start(bf16[256,512]{1,0:T(8,128)(2,1)} %param.7) | copy-start | bytes 786436
  1.6 2.7 %copy-start.3 = (bf16[256,512]{1,0:T(8,128)(2,1)S(1)}, bf16[256,512]{1,0:T(8,128)(2,1)}, u32[]{:S(2)}) copy-start(bf16[256,512]{1,0:T(8,128)(2,1)} %param.6) | copy-start | bytes 786436
  1.7 17.6 %collective-permute-start.1 = (bf16[2,256,128]{2,1,0:T(8,128)(2,1)S(1)}, bf16[2,256,128]{2,1,0:T(8,128)(2,1)S(1)}, u32[]{:S(2)}, u32[]{:S(2)}) collective-permute-start(bf16[2,256,128]{2,1,0:T(8,128)(2,1)S(1)} %pad_maximum_fusion.2), channel_id=1, source_target_pairs={{0,8},{2,10},{4,12},{6,14},{8,0},{10,2},{12,4},{14,6},{1,9},{3,11}... | collective-permute-start | bytes 393224 | tf_op jit(solution)/shard_map/ppermute | solution.py:453
  4.4 1.0 %copy-start.1 = (bf16[256,512]{1,0:T(8,128)(2,1)S(1)}, bf16[256,512]{1,0:T(8,128)(2,1)}, u32[]{:S(2)}) copy-start(bf16[256,512]{1,0:T(8,128)(2,1)} %param.5) | copy-start | bytes 786436
  4.4 14.9 %collective-permute-start.2 = (bf16[2,256,128]{2,1,0:T(8,128)(2,1)S(1)}, bf16[2,256,128]{2,1,0:T(8,128)(2,1)S(1)}, u32[]{:S(2)}, u32[]{:S(2)}) collective-permute-start(bf16[2,256,128]{2,1,0:T(8,128)(2,1)S(1)} %pad_maximum_fusion.3), channel_id=1, source_target_pairs={{0,12},{2,14},{4,8},{6,10},{8,4},{10,6},{12,0},{14,2},{1,13},{3,15... | collective-permute-start | bytes 393224 | tf_op jit(solution)/shard_map/ppermute | solution.py:453
  5.4 12.4 %collective-permute-start = (bf16[4,256,128]{2,1,0:T(8,128)(2,1)S(1)}, bf16[4,256,128]{2,1,0:T(8,128)(2,1)S(1)}, u32[]{:S(2)}, u32[]{:S(2)}) collective-permute-start(bf16[4,256,128]{2,1,0:T(8,128)(2,1)S(1)} %pad_maximum_fusion), channel_id=1, source_target_pairs={{0,4},{2,6},{4,0},{6,2},{8,12},{10,14},{12,8},{14,10},{1,5},{3,7},... | collective-permute-start | bytes 786440 | tf_op jit(solution)/shard_map/ppermute | solution.py:453
  7.1 1.6 %collective-permute-start.3 = (bf16[4,256,128]{2,1,0:T(8,128)(2,1)S(1)}, bf16[4,256,128]{2,1,0:T(8,128)(2,1)S(1)}, u32[]{:S(2)}, u32[]{:S(2)}) collective-permute-start(bf16[4,256,128]{2,1,0:T(8,128)(2,1)S(1)} %pad_maximum_fusion.1.refs_0_), channel_id=1, source_target_pairs={{0,2},{2,0},{4,6},{6,4},{8,10},{10,8},{12,14},{14,12},{1,3},{3,1},... | collective-permute-start | bytes 786440 | tf_op jit(solution)/shard_map/ppermute | solution.py:459
  7.3 17.5 %collective-permute-start.7 = (bf16[2,256,128]{2,1,0:T(8,128)(2,1)S(1)}, bf16[2,256,128]{2,1,0:T(8,128)(2,1)S(1)}, u32[]{:S(2)}, u32[]{:S(2)}) collective-permute-start(bf16[2,256,128]{2,1,0:T(8,128)(2,1)S(1)} %pad_maximum_fusion.4), channel_id=1, source_target_pairs={{0,8},{2,10},{4,12},{6,14},{8,0},{10,2},{12,4},{14,6},{1,9},{3,11}... | collective-permute-start | bytes 393224 | tf_op jit(solution)/shard_map/ppermute | solution.py:453
  17.8 3.0 %collective-permute-start.4 = (bf16[4,256,128]{2,1,0:T(8,128)(2,1)S(1)}, bf16[4,256,128]{2,1,0:T(8,128)(2,1)S(1)}, u32[]{:S(2)}, u32[]{:S(2)}) collective-permute-start(bf16[4,256,128]{2,1,0:T(8,128)(2,1)S(1)} %collective-permute-done.refs_1_), channel_id=1, source_target_pairs={{0,2},{2,0},{4,6},{6,4},{8,10},{10,8},{12,14},{14,12},{1,3},{3,1},... | collective-permute-start | bytes 786440 | tf_op jit(solution)/shard_map/ppermute | solution.py:459
  19.2 1.3 %collective-permute-start.6 = (bf16[2,256,128]{2,1,0:T(8,128)(2,1)S(1)}, bf16[2,256,128]{2,1,0:T(8,128)(2,1)S(1)}, u32[]{:S(2)}, u32[]{:S(2)}) collective-permute-start(bf16[2,256,128]{2,1,0:T(8,128)(2,1)S(1)} %collective-permute-done.2.refs_3_), channel_id=1, source_target_pairs={{0,2},{2,0},{4,6},{6,4},{8,10},{10,8},{12,14},{14,12},{1,3},{3,1},... | collective-permute-start | bytes 393224 | tf_op jit(solution)/shard_map/ppermute | solution.py:459
  19.3 1.5 %collective-permute-start.5 = (bf16[2,256,128]{2,1,0:T(8,128)(2,1)S(1)}, bf16[2,256,128]{2,1,0:T(8,128)(2,1)S(1)}, u32[]{:S(2)}, u32[]{:S(2)}) collective-permute-start(bf16[2,256,128]{2,1,0:T(8,128)(2,1)S(1)} %collective-permute-done.1.refs_2_), channel_id=1, source_target_pairs={{0,2},{2,0},{4,6},{6,4},{8,10},{10,8},{12,14},{14,12},{1,3},{3,1},... | collective-permute-start | bytes 393224 | tf_op jit(solution)/shard_map/ppermute | solution.py:459
  19.8 8.3 %collective-permute-start.8 = (bf16[2,256,128]{2,1,0:T(8,128)(2,1)S(1)}, bf16[2,256,128]{2,1,0:T(8,128)(2,1)S(1)}, u32[]{:S(2)}, u32[]{:S(2)}) collective-permute-start(bf16[2,256,128]{2,1,0:T(8,128)(2,1)S(1)} %pad_maximum_fusion.5), channel_id=1, source_target_pairs={{0,12},{2,14},{4,8},{6,10},{8,4},{10,6},{12,0},{14,2},{1,13},{3,15... | collective-permute-start | bytes 393224 | tf_op jit(solution)/shard_map/ppermute | solution.py:453
  29.9 2.0 %collective-permute-start.9 = (bf16[2,1024,128]{2,1,0:T(8,128)(2,1)S(1)}, bf16[2,1024,128]{2,1,0:T(8,128)(2,1)S(1)}, u32[]{:S(2)}, u32[]{:S(2)}) collective-permute-start(bf16[2,1024,128]{2,1,0:T(8,128)(2,1)S(1)} %get-tuple-element.57), channel_id=1, source_target_pairs={{0,2},{2,0},{4,6},{6,4},{8,10},{10,8},{12,14},{14,12},{1,3},{3,1},... | collective-permute-start | bytes 1572872 | tf_op jit(solution)/shard_map/ppermute | solution.py:459
  32.0 19.2 %collective-permute-start.10 = (bf16[4,256,128]{2,1,0:T(8,128)(2,1)S(1)}, bf16[4,256,128]{2,1,0:T(8,128)(2,1)S(1)}, u32[]{:S(2)}, u32[]{:S(2)}) collective-permute-start(bf16[4,256,128]{2,1,0:T(8,128)(2,1)S(1)} %get-tuple-element.65), channel_id=1, source_target_pairs={{0,8},{2,10},{4,12},{6,14},{8,0},{10,2},{12,4},{14,6},{1,9},{3,11}... | collective-permute-start | bytes 786440 | tf_op jit(solution)/shard_map/ppermute | solution.py:453
  33.3 24.2 %collective-permute-start.11 = (bf16[4,256,128]{2,1,0:T(8,128)(2,1)S(1)}, bf16[4,256,128]{2,1,0:T(8,128)(2,1)S(1)}, u32[]{:S(2)}, u32[]{:S(2)}) collective-permute-start(bf16[4,256,128]{2,1,0:T(8,128)(2,1)S(1)} %get-tuple-element.66), channel_id=1, source_target_pairs={{0,12},{2,14},{4,8},{6,10},{8,4},{10,6},{12,0},{14,2},{1,13},{3,15... | collective-permute-start | bytes 786440 | tf_op jit(solution)/shard_map/ppermute | solution.py:453
  34.3 23.2 %collective-permute-start.12 = (bf16[4,256,128]{2,1,0:T(8,128)(2,1)S(1)}, bf16[4,256,128]{2,1,0:T(8,128)(2,1)S(1)}, u32[]{:S(2)}, u32[]{:S(2)}) collective-permute-start(bf16[4,256,128]{2,1,0:T(8,128)(2,1)S(1)} %get-tuple-element.67), channel_id=1, source_target_pairs={{0,4},{2,6},{4,0},{6,2},{8,12},{10,14},{12,8},{14,10},{1,5},{3,7},... | collective-permute-start | bytes 786440 | tf_op jit(solution)/shard_map/ppermute | solution.py:453

commit v6 on v5

--- a/solution.py
+++ b/solution.py
@@ -268,7 +268,7 @@
 
 def unpack_kernel(layout, chip_ref, *refs):
     count = max(max(arrays) for _, arrays in layout) + 1
-    blocks, outs, sems = refs[: len(layout)], refs[len(layout) : -1], refs[-1]
+    blocks, outs, sems = refs[: len(layout)], refs[-1 - count : -1], refs[-1]
     chip = chip_ref[0]
     copies = []
     for at, (offset, arrays) in enumerate(layout):
@@ -286,18 +286,19 @@
         copy.wait()
 
 
-def unpack(chip, blocks, layout, width):
+def unpack(chip, blocks, layout, width, into=()):
     count = max(max(arrays) for _, arrays in layout) + 1
     rows = blocks[0].shape[1]
     return pl.pallas_call(
         functools.partial(unpack_kernel, layout),
         out_shape=[jax.ShapeDtypeStruct((rows, width), blocks[0].dtype)] * count,
-        in_specs=[pl.BlockSpec(memory_space=pltpu.SMEM)] + any_specs(len(blocks)),
+        in_specs=[pl.BlockSpec(memory_space=pltpu.SMEM)] + any_specs(len(blocks) + len(into)),
         out_specs=any_specs(count),
+        input_output_aliases={1 + len(blocks) + at: at for at in range(len(into))},
         scratch_shapes=[pltpu.SemaphoreType.DMA((len(layout), count))],
         compiler_params=pltpu.CompilerParams(vmem_limit_bytes=MIB),
         name="unpack",
-    )(chip, *blocks)
+    )(chip, *blocks, *into)
 
 
 def load_keys(blocks, key_ref, value_ref):
@@ -473,8 +474,9 @@
     chip = (lax.axis_index("seq") // 2).reshape(1)
     pairs = [key_rows, value_rows]
     queries = [query_rows, grad_output]
-    wanted = [("keys", offset, pairs) for offset in range(2, chips)]
-    wanted += [("keys", offset, pairs + queries) for offset in (1, 0)]
+    wanted = [("keys", 2, pairs), ("keys", 1, pairs + queries)]
+    wanted += [("keys", offset, pairs) for offset in range(3, chips)]
+    wanted += [("keys", 0, pairs + queries)]
     wanted += [("queries", offset, queries) for offset in range(2, chips)]
     moved = {}
     for name, offset, arrays in wanted:
@@ -535,10 +537,15 @@
         rows,
         8 * MIB,
     )
-    order = list(range(2, chips)) + [1]
+    order = [2, 1] + list(range(3, chips))
     returned = [outs[0]] + [to_chip(outs[offset], offset) for offset in order]
     layout = [(offset, (0, 1, 2, 3)) for offset in [0] + order]
-    return tuple(unpack(chip, returned, layout, query_rows.shape[1]))
+    width = query_rows.shape[1]
+    last = layout.index((chips - 1, (0, 1, 2, 3)))
+    returned.append(returned.pop(last))
+    layout.append(layout.pop(last))
+    arrays = unpack(chip, returned[:-1], layout[:-1], width)
+    return tuple(unpack(chip, returned[-1:], layout[-1:], width, arrays))
 
 
 def shards(query_rows, key_rows, value_rows, grad_output, dilation_offsets):

time: 58.8 us -> 58.1 us (0.988)
  waiting for transfers between devices: 34.5 us -> 27.6 us
  starting transfers between devices: 10.7 us -> 17.1 us
  local copies, waits for them, and re-layouts: 1.94 us -> 1.18 us
  Pallas kernels: 10.4 us -> 11 us
    ppermute x8, starting transfers between devices: 10.1 us -> 16.3 us  [to_chip(): lax.ppermute(array, 'seq', [(i, i ^ 2 * offset) for i in range(lax.axis_s...]
    ppermute x8, waiting for transfers between devices: 33 us -> 27.2 us  [to_chip(): lax.ppermute(array, 'seq', [(i, i ^ 2 * offset) for i in range(lax.axis_s...]
    ppermute x5, waiting for transfers between devices: 1.49 us -> 0.42 us  [to_core(): lax.ppermute(array, 'seq', [(i, i ^ 1) for i in range(lax.axis_size('seq'...]
    unnamed x8, local copies, waits for them, and re-layouts: 0.79 us -> 0.03 us
    pallas_call x1 -> x2, Pallas kernels: 1.09 us -> 1.69 us  [unpack(): pl.pallas_call(functools.partial(unpack_kernel, layout), out_shape=[jax.S...]
  transfers between devices with their start and end apart: 13 -> 13, of which waited for: 9 -> 6; matrix products, arithmetic and copies ran while one was open for 1% -> 1% of each run, Pallas kernels for 13% -> 14%
where the time goes in v6:
time: 58.1 us; the launch traced here: 57.9 us
  waiting for transfers between devices  27.6 us (48%)
  starting transfers between devices  17.1 us (29%)
  Pallas kernels  11 us (19%)
  local copies, waits for them, and re-layouts  1.18 us (2%)
  between operations  0.92 us (2%)
    ppermute x8, waiting for transfers between devices, to_chip(): lax.ppermute(array, 'seq', [(i, i ^ 2 * offset) for i in range(lax.axis_s...  27.2 us
    ppermute x8, starting transfers between devices, to_chip(): lax.ppermute(array, 'seq', [(i, i ^ 2 * offset) for i in range(lax.axis_s...  16.3 us
    pallas_call x5, Pallas kernels, call_vmem(): pl.pallas_call(kernel, out_shape=[jax.ShapeDtypeStruct(shape, dtype) for...  9.31 us
    pallas_call x2, Pallas kernels, unpack(): pl.pallas_call(functools.partial(unpack_kernel, layout), out_shape=[jax.S...  1.69 us
  transfers between devices with their start and end apart: 13, of which 6 were waited for; matrix products, arithmetic and copies ran while one was open for 1% of the time, Pallas kernels for 14%

profile of v6, /device:TPU:12, one launch (start us, length us, event | category | flops | bytes accessed | tf_op | source)
XLA Modules:
  0.0 57.9 jit_solution(14887091164648610576)
XLA Ops:
  0.7 0.9 %dynamic-slice_bitcast_fusion.14 = (bf16[1,256,128]{2,1,0:T(8,128)(2,1)S(1)}, bf16[1,256,128]{2,1,0:T(8,128)(2,1)S(1)}) fusion(bf16[256,512]{1,0:T(8,128)(2,1)} %param.7, s32[]{:T(128)S(6)} %select_n.34, bf16[256,512]{1,0:T(8,128)(2,1)} %param.6), kind=kLoop, calls=%fused_computation.20 | loop fusion | bytes 262148 | tf_op jit(solution)/shard_map/stack | solution.py:266
  1.7 2.7 %collective-permute-start.1 = (bf16[2,256,128]{2,1,0:T(8,128)(2,1)S(1)}, bf16[2,256,128]{2,1,0:T(8,128)(2,1)S(1)}, u32[]{:S(2)}, u32[]{:S(2)}) collective-permute-start(bf16[2,256,128]{2,1,0:T(8,128)(2,1)S(1)} %pad_maximum_fusion.2), channel_id=1, source_target_pairs={{0,8},{2,10},{4,12},{6,14},{8,0},{10,2},{12,4},{14,6},{1,9},{3,11}... | collective-permute-start | bytes 393224 | tf_op jit(solution)/shard_map/ppermute | solution.py:454
  4.5 0.5 collective-permute-start
  5.1 1.0 %collective-permute-start.2 = (bf16[2,256,128]{2,1,0:T(8,128)(2,1)S(1)}, bf16[2,256,128]{2,1,0:T(8,128)(2,1)S(1)}, u32[]{:S(2)}, u32[]{:S(2)}) collective-permute-start(bf16[2,256,128]{2,1,0:T(8,128)(2,1)S(1)} %pad_maximum_fusion.3), channel_id=1, source_target_pairs={{0,12},{2,14},{4,8},{6,10},{8,4},{10,6},{12,0},{14,2},{1,13},{3,15... | collective-permute-start | bytes 393224 | tf_op jit(solution)/shard_map/ppermute | solution.py:454
  6.4 3.1 %collective-permute-start.7 = (bf16[2,256,128]{2,1,0:T(8,128)(2,1)S(1)}, bf16[2,256,128]{2,1,0:T(8,128)(2,1)S(1)}, u32[]{:S(2)}, u32[]{:S(2)}) collective-permute-start(bf16[2,256,128]{2,1,0:T(8,128)(2,1)S(1)} %pad_maximum_fusion.4), channel_id=1, source_target_pairs={{0,8},{2,10},{4,12},{6,14},{8,0},{10,2},{12,4},{14,6},{1,9},{3,11}... | collective-permute-start | bytes 393224 | tf_op jit(solution)/shard_map/ppermute | solution.py:454
  9.4 5.8 %collective-permute-done.refs_1_ = bf16[4,256,128]{2,1,0:T(8,128)(2,1)S(1)} collective-permute-done((bf16[4,256,128]{2,1,0:T(8,128)(2,1)S(1)}, bf16[4,256,128]{2,1,0:T(8,128)(2,1)S(1)}, u32[]{:S(2)}, u32[]{:S(2)}) %collective-permute-start) | collective-permute-done | bytes 262176 | tf_op jit(solution)/shard_map/ppermute | solution.py:454
  15.3 0.6 collective-permute-start.6
  15.8 0.1 collective-permute-start.5
  16.0 5.5 %collective-permute-start.8 = (bf16[2,256,128]{2,1,0:T(8,128)(2,1)S(1)}, bf16[2,256,128]{2,1,0:T(8,128)(2,1)S(1)}, u32[]{:S(2)}, u32[]{:S(2)}) collective-permute-start(bf16[2,256,128]{2,1,0:T(8,128)(2,1)S(1)} %pad_maximum_fusion.5), channel_id=1, source_target_pairs={{0,12},{2,14},{4,8},{6,10},{8,4},{10,6},{12,0},{14,2},{1,13},{3,15... | collective-permute-start | bytes 393224 | tf_op jit(solution)/shard_map/ppermute | solution.py:454
  21.4 4.0 %near.1 = (bf16[1,256,128]{2,1,0:T(8,128)(2,1)S(1)}, bf16[1,256,128]{2,1,0:T(8,128)(2,1)S(1)}, bf16[1,256,128]{2,1,0:T(8,128)(2,1)S(1)}, bf16[1,256,128]{2,1,0:T...) custom-call(bf16[4,256,128]{2,1,0:T(8,128)(2,1)S(1)} %pad_maximum_fu, ...), custom_call_target="tpu_custom_call" | custom-call | flops 1610612736 | bytes 1048576 | tf_op jit(solution)/shard_map/near/pallas_call | solution.py:430
  25.4 1.9 %far.2 = (bf16[1,256,128]{2,1,0:T(8,128)(2,1)S(1)}, bf16[256,1024]{1,0:T(8,128)(2,1)S(1)}, f32[256,128]{1,0:T(8,128)S(1)}, f32[256,128]{1,0:T(8,128)S(1)}, f32[2,1024,128]{2,1,0:T(8,128)S(1)}) custom-call(bf16[2048,128]{1,0:T(8,128)(2,1)S(1)} %get-tuple-element.47.key_ref.refs_0_, bf16[2048,256]{1,0:T(8,128)(2,1)S(1)} %get-tuple-element.48.value_ref.refs_1_, ...), custom_call_target="tpu_custom_call" | custom-call | flops 536870912 | bytes 1048576 | tf_op jit(solution)/shard_map/far/pallas_call | solution.py:430
  27.3 0.6 %collective-permute-done.8.block_ref.refs_4_ = bf16[2,256,128]{2,1,0:T(8,128)(2,1)S(1)} collective-permute-done((bf16[2,256,128]{2,1,0:T(8,128)(2,1)S(1)}, bf16[2,256,128]{2,1,0:T(8,128)(2,1)S(1)}, u32[]{:S(2)}, u32[]{:S(2)}) %collective-permute-start.8) | collective-permute-done | bytes 131104 | tf_op jit(solution)/shard_map/ppermute | solution.py:454
  27.9 1.9 %far.3 = (bf16[1,256,128]{2,1,0:T(8,128)(2,1)S(1)}, bf16[256,1024]{1,0:T(8,128)(2,1)S(1)}, f32[256,128]{1,0:T(8,128)S(1)}, f32[256,128]{1,0:T(8,128)S(1)}, bf16[2,1024,128]{2,1,0:T(8,128)(2,1)S(1)}) custom-call(bf16[2048,128]{1,0:T(8,128)(2,1)S(1)} %get-tuple-element.47.key_ref.refs_0_, bf16[2048,256]{1,0:T(8,128)(2,1)S(1)} %get-tuple-element.48.value_ref.refs_1_, ...), custom_call_target="tpu_custom_call" | custom-call | flops 536870912 | bytes 1048576 | tf_op jit(solution)/shard_map/far/pallas_call | solution.py:430
  29.9 1.5 %own.1 = (bf16[1,256,128]{2,1,0:T(8,128)(2,1)S(1)}, bf16[1,256,128]{2,1,0:T(8,128)(2,1)S(1)}, f32[2,1024,128]{2,1,0:T(8,128)S(1)}) custom-call(bf16[2048,128]{1,0:T(8,128)(2,1)S(1)} %get-tuple-element.47.key_ref.refs_0_, bf16[2048,256]{1,0:T(8,128)(2,1)S(1)} %get-tuple-element.48.value_ref.refs_1_, f32[2,1024,128]{2,1,0:T(8,128)S(1)} %get-tuple-element.49.refs_2_, ...), custom_call_target="tpu_custom_call" | custom-call | flops 536870912 | bytes 1048576 | tf_op jit(solution)/shard_map/own/pallas_call | solution.py:430
  31.3 0.4 collective-permute-done.9.other_ref
  31.7 0.1 add_partials.1
  31.9 0.1 collective-permute-start.11
  32.0 3.2 %collective-permute-start.12 = (bf16[4,256,128]{2,1,0:T(8,128)(2,1)S(1)}, bf16[4,256,128]{2,1,0:T(8,128)(2,1)S(1)}, u32[]{:S(2)}, u32[]{:S(2)}) collective-permute-start(bf16[4,256,128]{2,1,0:T(8,128)(2,1)S(1)} %get-tuple-element.71), channel_id=1, source_target_pairs={{0,4},{2,6},{4,0},{6,2},{8,12},{10,14},{12,8},{14,10},{1,5},{3,7},... | collective-permute-start | bytes 786440 | tf_op jit(solution)/shard_map/ppermute | solution.py:454
  35.1 0.3 collective-permute-start.10
  35.4 8.8 %collective-permute-done.11.refs_1_ = bf16[4,256,128]{2,1,0:T(8,128)(2,1)S(1)} collective-permute-done((bf16[4,256,128]{2,1,0:T(8,128)(2,1)S(1)}, bf16[4,256,128]{2,1,0:T(8,128)(2,1)S(1)}, u32[]{:S(2)}, u32[]{:S(2)}) %collective-permute-start.11) | collective-permute-done | bytes 262176 | tf_op jit(solution)/shard_map/ppermute | solution.py:454
  44.2 3.7 %collective-permute-done.12.refs_2_ = bf16[4,256,128]{2,1,0:T(8,128)(2,1)S(1)} collective-permute-done((bf16[4,256,128]{2,1,0:T(8,128)(2,1)S(1)}, bf16[4,256,128]{2,1,0:T(8,128)(2,1)S(1)}, u32[]{:S(2)}, u32[]{:S(2)}) %collective-permute-start.12) | collective-permute-done | bytes 262176 | tf_op jit(solution)/shard_map/ppermute | solution.py:454
  47.9 1.0 %unpack.2 = (bf16[256,512]{1,0:T(8,128)(2,1)}, bf16[256,512]{1,0:T(8,128)(2,1)}, bf16[256,512]{1,0:T(8,128)(2,1)}, bf16[256,512]{1,0:T(8,128)(2,1)}) custom-call(s32[1]{0:T(128)} %bitcast.chip_ref, bf16[4,256,128]{2,1,0:T(8,128)(2,1)S(1)} %get-tuple-element.69.refs_0_, bf16[4,256,128]{2,1,0:T(8,128)(2,1)S(1)} %collective-permute-done.11.refs_1_, ...), custom_call_target="tpu_custom_call" | custom-call | tf_op jit(solution)/shard_map/unpack/pallas_call | solution.py:292
  48.9 8.3 %collective-permute-done.10.refs_0_ = bf16[4,256,128]{2,1,0:T(8,128)(2,1)S(1)} collective-permute-done((bf16[4,256,128]{2,1,0:T(8,128)(2,1)S(1)}, bf16[4,256,128]{2,1,0:T(8,128)(2,1)S(1)}, u32[]{:S(2)}, u32[]{:S(2)}) %collective-permute-start.10) | collective-permute-done | bytes 262176 | tf_op jit(solution)/shard_map/ppermute | solution.py:454
  57.2 0.7 %unpack.3 = (bf16[256,512]{1,0:T(8,128)(2,1)}, bf16[256,512]{1,0:T(8,128)(2,1)}, bf16[256,512]{1,0:T(8,128)(2,1)}, bf16[256,512]{1,0:T(8,128)(2,1)}) custom-call(s32[1]{0:T(128)} %bitcast.chip_ref, bf16[4,256,128]{2,1,0:T(8,128)(2,1)S(1)} %collective-permute-done.10.refs_0_, ...), custom_call_target="tpu_custom_call", output_to_operand_aliasing={{0}: (2, {}), {1}: (3, {}), {2}: (4, {}), {3}: (5, {})} | custom-call | tf_op jit(solution)/shard_map/unpack/pallas_call | solution.py:292
  (38 shorter events, 0.5 us)
Async XLA Ops:
  0.6 3.7 %copy-start = (bf16[256,512]{1,0:T(8,128)(2,1)S(1)}, bf16[256,512]{1,0:T(8,128)(2,1)}, u32[]{:S(2)}) copy-start(bf16[256,512]{1,0:T(8,128)(2,1)} %param.8) | copy-start | bytes 786436
  0.7 3.7 %copy-start.2 = (bf16[256,512]{1,0:T(8,128)(2,1)S(1)}, bf16[256,512]{1,0:T(8,128)(2,1)}, u32[]{:S(2)}) copy-start(bf16[256,512]{1,0:T(8,128)(2,1)} %param.7) | copy-start | bytes 786436
  1.6 2.7 %copy-start.3 = (bf16[256,512]{1,0:T(8,128)(2,1)S(1)}, bf16[256,512]{1,0:T(8,128)(2,1)}, u32[]{:S(2)}) copy-start(bf16[256,512]{1,0:T(8,128)(2,1)} %param.6) | copy-start | bytes 786436
  1.7 2.8 %copy-start.1 = (bf16[256,512]{1,0:T(8,128)(2,1)S(1)}, bf16[256,512]{1,0:T(8,128)(2,1)}, u32[]{:S(2)}) copy-start(bf16[256,512]{1,0:T(8,128)(2,1)} %param.5) | copy-start | bytes 786436
  1.7 14.2 %collective-permute-start.1 = (bf16[2,256,128]{2,1,0:T(8,128)(2,1)S(1)}, bf16[2,256,128]{2,1,0:T(8,128)(2,1)S(1)}, u32[]{:S(2)}, u32[]{:S(2)}) collective-permute-start(bf16[2,256,128]{2,1,0:T(8,128)(2,1)S(1)} %pad_maximum_fusion.2), channel_id=1, source_target_pairs={{0,8},{2,10},{4,12},{6,14},{8,0},{10,2},{12,4},{14,6},{1,9},{3,11}... | collective-permute-start | bytes 393224 | tf_op jit(solution)/shard_map/ppermute | solution.py:454
  4.5 10.7 %collective-permute-start = (bf16[4,256,128]{2,1,0:T(8,128)(2,1)S(1)}, bf16[4,256,128]{2,1,0:T(8,128)(2,1)S(1)}, u32[]{:S(2)}, u32[]{:S(2)}) collective-permute-start(bf16[4,256,128]{2,1,0:T(8,128)(2,1)S(1)} %pad_maximum_fusion), channel_id=1, source_target_pairs={{0,4},{2,6},{4,0},{6,2},{8,12},{10,14},{12,8},{14,10},{1,5},{3,7},... | collective-permute-start | bytes 786440 | tf_op jit(solution)/shard_map/ppermute | solution.py:454
  5.1 10.2 %collective-permute-start.2 = (bf16[2,256,128]{2,1,0:T(8,128)(2,1)S(1)}, bf16[2,256,128]{2,1,0:T(8,128)(2,1)S(1)}, u32[]{:S(2)}, u32[]{:S(2)}) collective-permute-start(bf16[2,256,128]{2,1,0:T(8,128)(2,1)S(1)} %pad_maximum_fusion.3), channel_id=1, source_target_pairs={{0,12},{2,14},{4,8},{6,10},{8,4},{10,6},{12,0},{14,2},{1,13},{3,15... | collective-permute-start | bytes 393224 | tf_op jit(solution)/shard_map/ppermute | solution.py:454
  6.2 3.2 %collective-permute-start.3 = (bf16[4,256,128]{2,1,0:T(8,128)(2,1)S(1)}, bf16[4,256,128]{2,1,0:T(8,128)(2,1)S(1)}, u32[]{:S(2)}, u32[]{:S(2)}) collective-permute-start(bf16[4,256,128]{2,1,0:T(8,128)(2,1)S(1)} %pad_maximum_fusion.1.refs_0_), channel_id=1, source_target_pairs={{0,2},{2,0},{4,6},{6,4},{8,10},{10,8},{12,14},{14,12},{1,3},{3,1},... | collective-permute-start | bytes 786440 | tf_op jit(solution)/shard_map/ppermute | solution.py:460
  6.4 19.1 %collective-permute-start.7 = (bf16[2,256,128]{2,1,0:T(8,128)(2,1)S(1)}, bf16[2,256,128]{2,1,0:T(8,128)(2,1)S(1)}, u32[]{:S(2)}, u32[]{:S(2)}) collective-permute-start(bf16[2,256,128]{2,1,0:T(8,128)(2,1)S(1)} %pad_maximum_fusion.4), channel_id=1, source_target_pairs={{0,8},{2,10},{4,12},{6,14},{8,0},{10,2},{12,4},{14,6},{1,9},{3,11}... | collective-permute-start | bytes 393224 | tf_op jit(solution)/shard_map/ppermute | solution.py:454
  15.2 6.2 %collective-permute-start.4 = (bf16[4,256,128]{2,1,0:T(8,128)(2,1)S(1)}, bf16[4,256,128]{2,1,0:T(8,128)(2,1)S(1)}, u32[]{:S(2)}, u32[]{:S(2)}) collective-permute-start(bf16[4,256,128]{2,1,0:T(8,128)(2,1)S(1)} %collective-permute-done.refs_1_), channel_id=1, source_target_pairs={{0,2},{2,0},{4,6},{6,4},{8,10},{10,8},{12,14},{14,12},{1,3},{3,1},... | collective-permute-start | bytes 786440 | tf_op jit(solution)/shard_map/ppermute | solution.py:460
  15.3 6.2 %collective-permute-start.6 = (bf16[2,256,128]{2,1,0:T(8,128)(2,1)S(1)}, bf16[2,256,128]{2,1,0:T(8,128)(2,1)S(1)}, u32[]{:S(2)}, u32[]{:S(2)}) collective-permute-start(bf16[2,256,128]{2,1,0:T(8,128)(2,1)S(1)} %collective-permute-done.2.refs_3_), channel_id=1, source_target_pairs={{0,2},{2,0},{4,6},{6,4},{8,10},{10,8},{12,14},{14,12},{1,3},{3,1},... | collective-permute-start | bytes 393224 | tf_op jit(solution)/shard_map/ppermute | solution.py:460
  15.8 5.6 %collective-permute-start.5 = (bf16[2,256,128]{2,1,0:T(8,128)(2,1)S(1)}, bf16[2,256,128]{2,1,0:T(8,128)(2,1)S(1)}, u32[]{:S(2)}, u32[]{:S(2)}) collective-permute-start(bf16[2,256,128]{2,1,0:T(8,128)(2,1)S(1)} %collective-permute-done.1.refs_2_), channel_id=1, source_target_pairs={{0,2},{2,0},{4,6},{6,4},{8,10},{10,8},{12,14},{14,12},{1,3},{3,1},... | collective-permute-start | bytes 393224 | tf_op jit(solution)/shard_map/ppermute | solution.py:460
  16.0 12.0 %collective-permute-start.8 = (bf16[2,256,128]{2,1,0:T(8,128)(2,1)S(1)}, bf16[2,256,128]{2,1,0:T(8,128)(2,1)S(1)}, u32[]{:S(2)}, u32[]{:S(2)}) collective-permute-start(bf16[2,256,128]{2,1,0:T(8,128)(2,1)S(1)} %pad_maximum_fusion.5), channel_id=1, source_target_pairs={{0,12},{2,14},{4,8},{6,10},{8,4},{10,6},{12,0},{14,2},{1,13},{3,15... | collective-permute-start | bytes 393224 | tf_op jit(solution)/shard_map/ppermute | solution.py:454
  29.8 2.0 %collective-permute-start.9 = (bf16[2,1024,128]{2,1,0:T(8,128)(2,1)S(1)}, bf16[2,1024,128]{2,1,0:T(8,128)(2,1)S(1)}, u32[]{:S(2)}, u32[]{:S(2)}) collective-permute-start(bf16[2,1024,128]{2,1,0:T(8,128)(2,1)S(1)} %get-tuple-element.61), channel_id=1, source_target_pairs={{0,2},{2,0},{4,6},{6,4},{8,10},{10,8},{12,14},{14,12},{1,3},{3,1},... | collective-permute-start | bytes 1572872 | tf_op jit(solution)/shard_map/ppermute | solution.py:460
  31.9 12.4 %collective-permute-start.11 = (bf16[4,256,128]{2,1,0:T(8,128)(2,1)S(1)}, bf16[4,256,128]{2,1,0:T(8,128)(2,1)S(1)}, u32[]{:S(2)}, u32[]{:S(2)}) collective-permute-start(bf16[4,256,128]{2,1,0:T(8,128)(2,1)S(1)} %get-tuple-element.70), channel_id=1, source_target_pairs={{0,8},{2,10},{4,12},{6,14},{8,0},{10,2},{12,4},{14,6},{1,9},{3,11}... | collective-permute-start | bytes 786440 | tf_op jit(solution)/shard_map/ppermute | solution.py:454
  32.0 16.0 %collective-permute-start.12 = (bf16[4,256,128]{2,1,0:T(8,128)(2,1)S(1)}, bf16[4,256,128]{2,1,0:T(8,128)(2,1)S(1)}, u32[]{:S(2)}, u32[]{:S(2)}) collective-permute-start(bf16[4,256,128]{2,1,0:T(8,128)(2,1)S(1)} %get-tuple-element.71), channel_id=1, source_target_pairs={{0,4},{2,6},{4,0},{6,2},{8,12},{10,14},{12,8},{14,10},{1,5},{3,7},... | collective-permute-start | bytes 786440 | tf_op jit(solution)/shard_map/ppermute | solution.py:454
  35.1 22.0 %collective-permute-start.10 = (bf16[4,256,128]{2,1,0:T(8,128)(2,1)S(1)}, bf16[4,256,128]{2,1,0:T(8,128)(2,1)S(1)}, u32[]{:S(2)}, u32[]{:S(2)}) collective-permute-start(bf16[4,256,128]{2,1,0:T(8,128)(2,1)S(1)} %get-tuple-element.68), channel_id=1, source_target_pairs={{0,12},{2,14},{4,8},{6,10},{8,4},{10,6},{12,0},{14,2},{1,13},{3,15... | collective-permute-start | bytes 786440 | tf_op jit(solution)/shard_map/ppermute | solution.py:454
